TPU v7x, 32 devices: a whole 2x2x4 slice. The times are simulated.
32 devices in a mesh: dp: 16 (over z, y, x), mp: 2 (over core).
Axes of the slice: x: 2, y: 2, z: 4, core: 2. Of those that a mesh axis runs over, the one named last changes fastest.
Arguments:
- tokens: bfloat16 [2, 4096, 1024], P(None, 'dp', 'mp'), may hold values from -6 to 6
- class_ids: int32 [2, 16], replicated, may hold values from 0 to 999
- final_scale: int32 [2, 16, 16], P(None, 'dp'), may hold values from -1 to 6, as said below
- row_slots: int32 [2, 16, 256], P(None, 'dp'), may hold values from 0 to 255, as said below
- class_table: bfloat16 [1000, 1024], P(None, 'dp'), may hold values from -6 to 6
- ada_weight: bfloat16 [1024, 6, 1024], P('dp'), may hold values from -0.1875 to 0.1875
- ada_bias: float32 [6, 1024], P(None, 'mp'), may hold values from -1.75 to 1.75
- qkv_weight: bfloat16 [1024, 3, 1024], P(None, None, 'mp'), may hold values from -0.1875 to 0.1875
- qv_bias: float32 [2, 1024], P(None, 'mp'), may hold values from -0.875 to 0.875
- log_scale: float32 [16], P('mp'), may hold values from 2 to 3
- proj_weight: bfloat16 [1024, 1024], P('mp'), may hold values from -0.75 to 0.75
- proj_bias: float32 [1024], P('mp'), may hold values from -1.25 to 1.25
- fc1_weight: bfloat16 [1024, 4096], P(None, 'mp'), may hold values from -0.1875 to 0.1875
- fc1_bias: float32 [4096], P('mp'), may hold values from -1.75 to 1.75
- fc2_weight: bfloat16 [4096, 1024], P('mp'), may hold values from -0.09375 to 0.09375
- fc2_bias: float32 [1024], P('mp'), may hold values from -1.25 to 1.25
- out_grad: bfloat16 [2, 4096, 1024], P(None, 'dp', 'mp'), may hold values from -6 to 6
Outputs:
- output: bfloat16 [2, 4096, 1024], P(None, 'dp', 'mp')
- tokens_grad: bfloat16 [2, 4096, 1024], P(None, 'dp', 'mp')
- class_table_grad: float32 [1000, 1024], P(None, 'dp')
- ada_weight_grad: float32 [1024, 6, 1024], P('dp')
- ada_bias_grad: float32 [6, 1024], replicated
- qkv_weight_grad: float32 [1024, 3, 1024], P('dp', None, 'mp')
- qv_bias_grad: float32 [2, 1024], P(None, 'mp')
- log_scale_grad: float32 [16], P('mp')
- proj_weight_grad: float32 [1024, 1024], P('mp', 'dp')
- proj_bias_grad: float32 [1024], P('mp')
- fc1_weight_grad: float32 [1024, 4096], P('dp', 'mp')
- fc1_bias_grad: float32 [4096], P('mp')
- fc2_weight_grad: float32 [4096, 1024], P('mp', 'dp')
- fc2_bias_grad: float32 [1024], P('mp')
Inputs may be any that keep to these rules, and one draw needn't show every extreme that they name: `final_scale`: items fill positions from 0 in order, lengths sum to at most 256; the first item of each row has index 4 or more; -1 marks an empty place and only empty places follow it; in each micro-batch some row's first item has index 6. `row_slots`: each row's entries are a permutation of its positions; slots 0, 128 and 255 hold positions 0, 1 and 2.
All inputs are finite; a program needn't handle non-finite values.
Results may differ from a plain program's by a relative error of at most 0.025.
Values may be sent and summed in bfloat16 or wider, within the bound.
No kernel may reach another device: no remote copies, remote signals or barrier semaphores. Data moves between devices by JAX's collectives and lax.ppermute only.
A program may use at most 192 MiB of HBM per device.

v0:
```python
import functools

import jax
import jax.numpy as jnp
from jax import lax
from jax.experimental import pallas as pl
from jax.experimental.pallas import tpu as pltpu
from jax.sharding import PartitionSpec as P

HEAD_DIM = 64
LANES = 128
scale_ends = (1, 5, 14, 30, 55, 91, 155, 255, 424, 680)
norm_eps = 1e-06
unit_eps = 1e-06
bf16 = jnp.bfloat16
f32 = jnp.float32
gelu_c = 0.7978845608028654
gelu_a = 0.044715


def slot_layout(final_row, slots_row):
    ends_table = jnp.asarray(scale_ends, dtype=jnp.int32)
    chosen = final_row[:, None] == jnp.arange(len(scale_ends), dtype=jnp.int32)[None, :]
    lengths = jnp.sum(jnp.where(chosen, ends_table[None, :], 0), axis=1)
    items = final_row.shape[0]
    before = jnp.arange(items)[:, None] <= jnp.arange(items)[None, :]
    item_ends = jnp.sum(jnp.where(before, lengths[:, None], 0), axis=0)
    passed = slots_row[:, None] >= item_ends[None, :]
    segment = jnp.sum(passed.astype(jnp.int32), axis=1)
    item_start = jnp.sum(jnp.where(passed, lengths[None, :], 0), axis=1)
    offset = slots_row - item_start
    level = jnp.sum((offset[:, None] >= ends_table[None, :]).astype(jnp.int32), axis=1)
    return segment, jnp.where(segment == items, 0, level)


def dot(a, b):
    return jnp.dot(a, b, preferred_element_type=f32)


def dot_nt(a, b):
    return lax.dot_general(a, b, (((1,), (1,)), ((), ())), preferred_element_type=f32)


def dot_tn(a, b):
    return lax.dot_general(a, b, (((0,), (0,)), ((), ())), preferred_element_type=f32)


def half_sums(values, first):
    low = jnp.sum(jnp.where(first, values, 0.0), axis=1, keepdims=True)
    high = jnp.sum(jnp.where(first, 0.0, values), axis=1, keepdims=True)
    return jnp.where(first, low, high)


def head_parts(queries, keys, mult, first):
    query_scale = lax.rsqrt(half_sums(queries * queries, first) + unit_eps)
    key_scale = lax.rsqrt(half_sums(keys * keys, first) + unit_eps)
    return queries * query_scale * mult, keys * key_scale, query_scale, key_scale


def start_copies(pairs, sems):
    copies = [pltpu.make_async_copy(src, dst, sems.at[i]) for i, (src, dst) in enumerate(pairs)]
    for copy in copies:
        copy.start()
    return copies


def wait_all(copies):
    for copy in copies:
        copy.wait()


def tiles(size, most):
    tile = min(most, size)
    return [slice(start, start + tile) for start in range(0, size, tile)]


def forward_kernel(
    x_ref, mods, qkv_bias, mult, mask_ref, proj_bias, fc1_bias, *refs
):
    weights, outs, held, rest = split_refs(refs, [10, 17, 17])
    qkv_w, proj_w, fc1_w, qkv_s, in_sems, out_sems = rest
    copies = start_copies(
        [(weights[i], qkv_w.at[i // 3, i % 3]) for i in range(6)]
        + [(weights[6 + i], proj_w.at[i]) for i in range(2)]
        + [(weights[8 + i], fc1_w.at[i]) for i in range(2)],
        in_sems,
    )
    leaving = []

    def leave(index, *at):
        src, dst = held[index], outs[index]
        if at:
            src, dst = src.at[at], dst.at[at]
        copy = pltpu.make_async_copy(src, dst, out_sems.at[len(leaving)])
        copy.start()
        leaving.append(copy)

    h1, qn_out, kn_out, v_out, rq_out, rk_out, p_out, mixed0, mixed1, attn_out = held[:10]
    middle_out, h2_out, act0, act1a, act1b, slope0, slope1 = held[10:]
    rows, width = x_ref.shape
    half = width // 2
    x = x_ref[...].astype(f32)
    h1[...] = (normalize(x)[0] * (1.0 + mods[2:3, :]) + mods[4:5, :]).astype(bf16)
    leave(0)
    first = lax.broadcasted_iota(jnp.int32, (rows, LANES), 1) < HEAD_DIM
    mask = mask_ref[...]
    heads = half // HEAD_DIM
    for side, mixed_out in enumerate((mixed0, mixed1)):
        for part in range(3):
            copies[3 * side + part].wait()
            at = slice(part * half, (part + 1) * half)
            qkv_s[:, at] = dot(h1[...], qkv_w[side, part]) + qkv_bias[side : side + 1, at]
        for pair in range(half // LANES):
            at = slice(pair * LANES, (pair + 1) * LANES)
            qn, kn, query_scale, key_scale = head_parts(
                qkv_s[:, at],
                qkv_s[:, half + pair * LANES : half + (pair + 1) * LANES],
                mult[side : side + 1, at],
                first,
            )
            q_low, k_low = qn.astype(bf16), kn.astype(bf16)
            v_low = qkv_s[:, 2 * half + pair * LANES : 2 * half + (pair + 1) * LANES].astype(bf16)
            qn_out[side, :, at] = q_low
            kn_out[side, :, at] = k_low
            v_out[side, :, at] = v_low
            rq_out[side, :, at] = query_scale
            rk_out[side, :, at] = key_scale
            mixed = []
            for head in range(2):
                own = first if head == 0 else jnp.logical_not(first)
                scores = dot_nt(jnp.where(own, k_low, jnp.zeros_like(k_low)), q_low)
                raised = jnp.exp(scores) * mask
                weight = raised * (1.0 / jnp.sum(raised, axis=0, keepdims=True))
                p_out[side * heads + 2 * pair + head] = weight
                mixed.append(dot_tn(weight.astype(bf16), v_low))
            mixed_out[:, at] = jnp.where(first, mixed[0], mixed[1]).astype(bf16)
        leave(7 + side)
        for index in range(1, 6):
            leave(index, side)
        leave(6, pl.ds(side * heads, heads))
    copies[6].wait()
    copies[7].wait()
    attn_out[...] = dot(mixed0[...], proj_w[0]) + dot(mixed1[...], proj_w[1]) + proj_bias[...]
    leave(9)
    middle = x + mods[0:1, :] * attn_out[...]
    middle_out[...] = middle
    leave(10)
    h2_out[...] = (normalize(middle)[0] * (1.0 + mods[3:4, :]) + mods[5:6, :]).astype(bf16)
    leave(11)

    def expand(side, act, slope, first_col):
        for to in tiles(act.shape[1], 512):
            at = slice(first_col + to.start, first_col + to.stop)
            pre = dot(h2_out[...], fc1_w[side, :, at]) + fc1_bias[side : side + 1, at]
            value, rise = gelu_parts(pre)
            act[:, to] = value.astype(bf16)
            slope[:, at] = rise.astype(bf16)

    copies[9].wait()
    expand(1, act1a, slope1, 0)
    leave(13)
    expand(1, act1b, slope1, act1a.shape[1])
    leave(14)
    leave(16)
    copies[8].wait()
    expand(0, act0, slope0, 0)
    leave(12)
    leave(15)
    wait_all(leaving)


def hidden_back_kernel(grad_ref, *refs):
    ins, outs, held, rest = split_refs(refs, [4, 3, 3])
    slope_s, fc2_w, in_sems, out_sems = rest
    slope0, slope1, fc2_0, fc2_1 = ins
    pre0, pre1a, pre1b = held
    cut = pre1a.shape[1]
    pairs = []
    for side in (1, 0):
        fc2, slope = (fc2_0, slope0) if side == 0 else (fc2_1, slope1)
        for at in (slice(0, cut), slice(cut, 2 * cut)):
            pairs.append((fc2.at[at, :], fc2_w.at[side, at, :]))
            pairs.append((slope.at[:, at], slope_s.at[side, :, at]))
    copies = start_copies(pairs, in_sems)
    leaving = []
    for side, pre, at, first_col in (
        (1, pre1a, slice(0, cut), 0),
        (1, pre1b, slice(cut, 2 * cut), 0),
        (0, pre0, slice(0, cut), 0),
        (0, pre0, slice(cut, 2 * cut), cut),
    ):
        step = 2 * (1 - side) + at.start // cut
        copies[2 * step].wait()
        copies[2 * step + 1].wait()
        for to in tiles(cut, 512):
            cols = slice(at.start + to.start, at.start + to.stop)
            grad = dot_nt(grad_ref[...], fc2_w[side, cols, :])
            pre[:, first_col + to.start : first_col + to.stop] = (
                grad * slope_s[side, :, cols].astype(f32)
            ).astype(bf16)
        if step < 2 or step == 3:
            index = {0: 1, 1: 2, 3: 0}[step]
            leaving += start_copies([(held[index], outs[index])], out_sems.at[pl.ds(index, 1)])
    wait_all(leaving)


def row_back_kernel(mods, mult, *refs):
    ins, outs, held, got, rest = split_refs(refs, [16, 6, 6, 16])
    h2_s, mixed_s, in_sems, out_sems = rest
    copies = start_copies(list(zip(ins, got)), in_sems)
    leaving = []

    def leave(index):
        copy = pltpu.make_async_copy(held[index], outs[index], out_sems.at[index])
        copy.start()
        leaving.append(copy)

    pre0, fc1_0, pre1a, pre1b, fc1_1, middle_ref, grad_out_ref, attn_ref = got[:8]
    proj_0, proj_1, qn_ref, kn_ref, v_ref, p_ref, rq_ref, rk_ref = got[8:]
    middle_grad, attn_grad, qkv_grad0, qkv1a, qkv1b, small = held
    rows, width = middle_ref.shape
    half = width // 2
    heads = half // HEAD_DIM
    copies[0].wait()
    copies[1].wait()
    for at in tiles(width, 512):
        h2_s[:, at] = dot_nt(pre0[...], fc1_0[at, :])
    wait_all(copies[2:5])
    for at in tiles(width, 512):
        total = h2_s[:, at]
        for index, pre in enumerate((pre1a, pre1b)):
            cut = pre.shape[1]
            total = total + dot_nt(pre[...], fc1_1[at, index * cut : (index + 1) * cut])
        h2_s[:, at] = total
    wait_all(copies[5:8])
    normed, spread = normalize(middle_ref[...])
    grad = h2_s[...]
    small[0:1, :] = jnp.sum(grad * normed, axis=0, keepdims=True)
    small[1:2, :] = jnp.sum(grad, axis=0, keepdims=True)
    total = grad_out_ref[...].astype(f32) + norm_back(
        grad * (1.0 + mods[3:4, :]), normed, spread
    )
    middle_grad[...] = total
    leave(0)
    small[2:3, :] = jnp.sum(total * attn_ref[...], axis=0, keepdims=True)
    attn_grad[...] = (mods[0:1, :] * total).astype(bf16)
    leave(1)
    first = lax.broadcasted_iota(jnp.int32, (rows, LANES), 1) < HEAD_DIM
    cut = qkv1a.shape[1]

    def put(side, start, values):
        if side == 0:
            qkv_grad0[:, start : start + LANES] = values
        else:
            index, to = start // cut, start % cut
            (qkv1a, qkv1b)[index][:, to : to + LANES] = values

    wait_all(copies[8:])
    for side in (1, 0):
        mixed_s[...] = dot_nt(attn_grad[...], (proj_0, proj_1)[side][...]).astype(bf16)
        for pair in range(half // LANES):
            at = slice(pair * LANES, (pair + 1) * LANES)
            mixed = mixed_s[:, at]
            q_low, k_low, v_low = qn_ref[side, :, at], kn_ref[side, :, at], v_ref[side, :, at]
            parts = []
            for head in range(2):
                own = first if head == 0 else jnp.logical_not(first)
                probs = p_ref[side * heads + 2 * pair + head]
                prob_grad = dot_nt(jnp.where(own, v_low, jnp.zeros_like(v_low)), mixed)
                centred = jnp.sum(prob_grad * probs, axis=0, keepdims=True)
                score_grad = (probs * (prob_grad - centred)).astype(bf16)
                parts.append(
                    (dot_tn(score_grad, k_low), dot(score_grad, q_low), dot(probs.astype(bf16), mixed))
                )
            query_grad, key_grad, value_grad = [
                jnp.where(first, low, high).astype(bf16) for low, high in zip(*parts)
            ]
            scaled = mult[side : side + 1, at]
            query_unit = q_low.astype(f32) * (1.0 / scaled)
            key_unit = k_low.astype(f32)
            unit_grad = query_grad.astype(f32) * scaled
            key_grad = key_grad.astype(f32)
            cross = unit_grad * query_unit
            small[3:4, side * half + pair * LANES : side * half + (pair + 1) * LANES] = jnp.sum(
                cross, axis=0, keepdims=True
            )
            query_pre = rq_ref[side, :, at] * (unit_grad - query_unit * half_sums(cross, first))
            key_pre = rk_ref[side, :, at] * (
                key_grad - key_unit * half_sums(key_grad * key_unit, first)
            )
            put(side, pair * LANES, query_pre.astype(bf16))
            put(side, half + pair * LANES, key_pre.astype(bf16))
            put(side, 2 * half + pair * LANES, value_grad)
        for index in (3, 4) if side == 1 else (2, 5):
            leave(index)
    wait_all(leaving)


def branch_kernel(mods, fc2_bias, *refs):
    ins, outs, got, rest = split_refs(refs, [7, 2, 7])
    output, mod_out = outs
    (in_sems,) = rest
    copies = start_copies(list(zip(ins, got)), in_sems)
    act0, fc2_0, act1a, act1b, fc2_1, grad_out_ref, middle_ref = got
    wait_all(copies)
    cut = act1a.shape[1]
    for at in tiles(middle_ref.shape[1], 512):
        value = (
            dot(act0[...], fc2_0[:, at])
            + dot(act1a[...], fc2_1[:cut, at])
            + dot(act1b[...], fc2_1[cut:, at])
            + fc2_bias[:, at]
        )
        output[:, at] = (middle_ref[:, at] + mods[1:2, at] * value).astype(bf16)
        mod_out[0:1, at] = jnp.sum(grad_out_ref[:, at].astype(f32) * value, axis=0, keepdims=True)


def input_back_kernel(mods, *refs):
    ins, outs, got, rest = split_refs(refs, [11, 2, 11])
    tokens_grad, mod_out = outs
    sum_s, in_sems = rest
    copies = start_copies(list(zip(ins, got)), in_sems)
    qkv_grad0, qkv1a, qkv1b, x_ref, middle_grad = got[:5]
    weights = got[5:]
    wait_all(copies)
    width = x_ref.shape[1]
    half, cut = width // 2, qkv1a.shape[1]
    normed, spread = normalize(x_ref[...].astype(f32))
    for at in tiles(width, 512):
        total = jnp.zeros((x_ref.shape[0], at.stop - at.start), f32)
        for part in range(3):
            total = total + dot_nt(
                qkv_grad0[:, part * half : (part + 1) * half], weights[part][at, :]
            )
        for start in range(0, 3 * half, half // 2):
            piece = (qkv1a, qkv1b)[start // cut][:, start % cut : start % cut + half // 2]
            inner = start % half
            total = total + dot_nt(piece, weights[3 + start // half][at, inner : inner + half // 2])
        sum_s[:, at] = total
    grad = sum_s[...]
    mod_out[0:1, :] = jnp.sum(grad * normed, axis=0, keepdims=True)
    mod_out[1:2, :] = jnp.sum(grad, axis=0, keepdims=True)
    tokens_grad[...] = (
        middle_grad[...] + norm_back(grad * (1.0 + mods[2:3, :]), normed, spread)
    ).astype(bf16)


def column_tiles(rights, flow):
    start = 0
    for source, (near, *pieces) in enumerate(rights):
        quarter, cut = near.shape[1] // 4, pieces[0].shape[1]
        for step in range(2):
            at = (2 * flow + step) * quarter
            to = start + step * quarter
            far = pieces[at // cut][:, at % cut : at % cut + quarter]
            both = jnp.concatenate([near[:, at : at + quarter], far], axis=0)
            yield source, both, slice(at, at + quarter), slice(to, to + quarter)
        start += 2 * quarter


def split_refs(refs, counts):
    out = []
    for count in counts:
        out.append(refs[:count])
        refs = refs[count:]
    return out + [refs]


def grad_kernel(pieces, bit_ref, *refs):
    sources = len(pieces)
    *ins, outs = split_refs(refs, [3 + count for count in pieces])
    left_sums, right_sums = outs[:sources], outs[sources : 2 * sources]
    left_t = outs[2 * sources : 3 * sources]
    sent_a, sent_b, picked = outs[3 * sources :]
    moved, part, columns = sent_a.shape
    tokens, half = ins[0][0].shape[0], ins[0][0].shape[1] // 2
    depth = 2 * tokens
    ones = jnp.ones((8, depth), bf16)
    for source in range(sources):
        for side in range(2):
            cols = slice(side * half, (side + 1) * half)
            near, far = ins[source][0][:, cols], ins[source][1][:, cols]
            rows = slice(side * moved, (side + 1) * moved)
            left_sums[source][:, cols] = dot(ones, jnp.concatenate([near, far], axis=0))[0:1]
            left_t[source][rows, :, :tokens] = near.T.reshape(moved, part, tokens)
            left_t[source][rows, :, tokens:] = far.T.reshape(moved, part, tokens)
    rights = [refs[2:] for refs in ins]
    for flow, sent in enumerate((sent_a, sent_b)):
        away = 1 - bit_ref[flow]
        for source in range(sources):
            for row in range(moved):
                at = 2 * row + away if flow == 0 else (row // 2) * 4 + row % 2 + 2 * away
                picked[source, row] = left_t[source][at]
        for source, right, at, to in column_tiles(rights, flow):
            left = picked[source].reshape(moved * part, depth)
            sent[:, :, to] = dot(left, right).astype(bf16).reshape(moved, part, -1)
            right_sums[source][:, at] = dot(ones, right)[0:1]


def second_kernel(pieces, bit_ref, *refs):
    sources = len(pieces)
    left_t, *rights, ends = split_refs(refs, [sources] + [1 + count for count in pieces])
    came_a, came_b, sent_a, sent_b, own, picked = ends
    moved, part, columns = sent_a.shape
    depth = left_t[0].shape[2]
    for flow, (came, sent) in enumerate(((came_a, sent_a), (came_b, sent_b))):
        mine, away = bit_ref[flow], 1 - bit_ref[1 - flow]
        for source in range(sources):
            for row in range(moved):
                if flow == 0:
                    base, other = 4 * row + mine, 2
                else:
                    base, other = 4 * row + 2 * mine, 1
                picked[source, row] = left_t[source][base + other * away]
                picked[source, moved + row] = left_t[source][base + other * (1 - away)]
        for source, right, at, to in column_tiles(rights, flow):
            left = picked[source].reshape(2 * moved * part, depth)
            block = dot(left, right).reshape(2 * moved, part, -1)
            kept = slice(flow * columns + to.start, flow * columns + to.stop)
            for row in range(moved):
                sent[row, :, to] = (block[row] + came[2 * row + away, :, to].astype(f32)).astype(
                    bf16
                )
                own[row, :, kept] = (
                    block[moved + row] + came[2 * row + 1 - away, :, to].astype(f32)
                ).astype(bf16)


def third_kernel(bit, bit_ref, own, *refs):
    came, (sent, kept) = refs[:-2], refs[-2:]
    mine = bit_ref[bit]
    start = 0
    for part in came:
        to = slice(start, start + part.shape[2])
        start += part.shape[2]
        for row in range(sent.shape[0]):
            away, near = 2 * row + 1 - mine, 2 * row + mine
            sent[row, :, to] = (own[away, :, to].astype(f32) + part[away].astype(f32)).astype(bf16)
            kept[row, :, to] = (own[near, :, to].astype(f32) + part[near].astype(f32)).astype(kept.dtype)


def local_call(kernel, limit, outs, scratch, kinds, *values, out_kind="v"):
    places = {
        "s": pl.BlockSpec(memory_space=pltpu.SMEM),
        "v": pl.BlockSpec(memory_space=pltpu.VMEM),
        "h": pl.BlockSpec(memory_space=pl.ANY),
    }
    return pl.pallas_call(
        kernel,
        out_shape=outs,
        in_specs=[places[kind] for kind in kinds],
        out_specs=[places[out_kind]] * len(outs),
        scratch_shapes=scratch,
        compiler_params=pltpu.CompilerParams(vmem_limit_bytes=limit * 2**20),
        cost_estimate=pl.CostEstimate(flops=1, bytes_accessed=1, transcendentals=0),
    )(*values)


def normalize(values):
    mean = jnp.mean(values, axis=1, keepdims=True)
    spread = jnp.mean(values * values, axis=1, keepdims=True) - mean * mean
    scale = lax.rsqrt(spread + norm_eps)
    return (values - mean) * scale, scale


def norm_back(grad, normed, scale):
    return scale * (
        grad
        - jnp.mean(grad, axis=1, keepdims=True)
        - normed * jnp.mean(grad * normed, axis=1, keepdims=True)
    )


def gelu_parts(pre):
    square = pre * pre
    tanh = jnp.tanh(pre * (gelu_c + gelu_c * gelu_a * square))
    gate = 0.5 + 0.5 * tanh
    slope = gate + pre * (0.5 - 0.5 * tanh * tanh) * (gelu_c + 3.0 * gelu_c * gelu_a * square)
    return pre * gate, slope


def shards(
    tokens,
    class_ids,
    final_scale,
    row_slots,
    class_table,
    ada_weight,
    ada_bias,
    qkv_weight,
    qv_bias,
    log_scale,
    proj_weight,
    proj_bias,
    fc1_weight,
    fc1_bias,
    fc2_weight,
    fc2_bias,
    out_grad,
):
    groups = lax.axis_size("dp")
    bits = groups.bit_length() - 1
    here = lax.axis_index("dp")
    core = lax.axis_index("mp")
    micro, row_len, half = tokens.shape
    width = 2 * half
    share = row_len // groups
    heads = log_scale.shape[0]
    hidden = fc1_weight.shape[1]

    def swap(values):
        return lax.ppermute(values, "mp", [(0, 1), (1, 0)])

    def flip(values, bit):
        return lax.ppermute(values, "dp", [(i, i ^ (1 << bit)) for i in range(groups)])

    def in_order(own, other, axis):
        return jnp.where(
            core == 0,
            jnp.concatenate([own, other], axis),
            jnp.concatenate([other, own], axis),
        )

    class_picks = (
        class_ids.reshape(-1)[:, None] == jnp.arange(class_table.shape[0], dtype=jnp.int32)[None, :]
    )
    condition = dot(class_picks.astype(bf16), class_table)
    lifted = jax.nn.silu(condition).astype(bf16)
    ada_half = lax.dynamic_slice_in_dim(ada_weight, core * half, half, 2)
    ada_terms = dot(lifted, ada_half.reshape(ada_half.shape[0], 6 * half)).astype(bf16)

    def by_target(values):
        return values.reshape(micro, groups, -1, half).swapaxes(0, 1).reshape(2 * groups, -1, half)

    def exchange(values):
        return lax.all_to_all(values, ("dp", "mp"), split_axis=0, concat_axis=0, tiled=True)

    def to_row(values):
        return (
            values.reshape(groups, 2, share, half).transpose(0, 2, 1, 3).reshape(row_len, width)
        )

    first_message = jnp.concatenate([by_target(tokens), by_target(ada_terms)], axis=1)
    arrived = exchange(first_message)

    def after(values, *earlier):
        return lax.optimization_barrier((values, earlier))[0]

    small = jnp.concatenate(
        [ada_bias.reshape(-1), qv_bias.reshape(-1), log_scale, proj_bias, fc1_bias, fc2_bias]
    )
    small_sizes = [6 * half, 2 * half, heads, half, hidden, half]

    def unpack(flat):
        starts = [sum(small_sizes[:i]) for i in range(7)]
        return [flat[starts[i] : starts[i + 1]] for i in range(6)]

    own_small, oth_small = unpack(small), unpack(swap(small))
    qkv_w = [qkv_weight[:, part] for part in range(3)]
    qkv_w += [swap(weight) for weight in qkv_w]
    proj_w = (proj_weight, swap(proj_weight))
    fc1_w = (fc1_weight, swap(fc1_weight))
    fc2_w = (fc2_weight, swap(fc2_weight))
    ada_shift = in_order(own_small[0].reshape(6, half), oth_small[0].reshape(6, half), 1)
    proj_shift = in_order(own_small[3], oth_small[3], 0)
    fc2_shift = in_order(own_small[5], oth_small[5], 0)
    fc1_shift = jnp.stack([own_small[4], oth_small[4]])
    qkv_shift = jnp.stack(
        [
            jnp.concatenate([part[1][:half], jnp.zeros((half,), f32), part[1][half:]])
            for part in (own_small, oth_small)
        ]
    )
    head_mult = jnp.stack([jnp.repeat(jnp.exp(part[2]), HEAD_DIM) for part in (own_small, oth_small)])

    segments, levels = slot_layout(
        lax.dynamic_index_in_dim(final_scale[:, 0], core, 0, keepdims=False),
        lax.dynamic_index_in_dim(row_slots[:, 0], core, 0, keepdims=False),
    )
    mask = (
        (segments[:, None] == segments[None, :]) & (levels[:, None] <= levels[None, :])
    ).astype(f32)

    resident = to_row(arrived[:, :share])
    grads_arrived = exchange(
        after(by_target(out_grad), arrived, qkv_shift, head_mult, mask, proj_shift, fc1_shift, fc2_shift)
    )
    mods = (
        jnp.sum(arrived[:, share:].reshape(groups, 2, 6, half).astype(f32), axis=0)
        .transpose(1, 0, 2)
        .reshape(6, width)
        + ada_shift
    )

    def array(*dims, kind=bf16):
        return jax.ShapeDtypeStruct(dims, kind)

    vmem, dma = pltpu.VMEM, pltpu.SemaphoreType.DMA

    def scratch(arrays):
        return [vmem(value.shape, value.dtype) for value in arrays]

    wide = array(2, row_len, half)
    wide32 = array(2, row_len, half, kind=f32)
    kept = [
        array(row_len, width),
        wide,
        wide,
        wide,
        wide32,
        wide32,
        array(2 * heads, row_len, row_len, kind=f32),
        array(row_len, half),
        array(row_len, half),
        array(row_len, width, kind=f32),
        array(row_len, width, kind=f32),
        array(row_len, width),
        array(row_len, hidden),
        array(row_len, hidden // 2),
        array(row_len, hidden // 2),
        array(row_len, hidden),
        array(row_len, hidden),
    ]
    h1, qn, kn, vn, rq, rk, probs, mixed0, mixed1, attn, middle, h2, act0, *more = local_call(
        forward_kernel,
        56,
        kept,
        scratch(kept)
        + [
            vmem((2, 3, width, half), bf16),
            vmem((2, half, width), bf16),
            vmem((2, width, hidden), bf16),
            vmem((row_len, 3 * half), f32),
            dma((10,)),
            dma((23,)),
        ],
        "vvvvvvv" + "h" * 10,
        resident,
        mods,
        qkv_shift,
        head_mult,
        mask,
        proj_shift[None],
        fc1_shift,
        *qkv_w,
        *proj_w,
        *fc1_w,
        out_kind="h",
    )
    act1, (slope0, slope1) = more[:2], more[2:]

    own_bits = jnp.stack([(here >> bit) & 1 for bit in range(bits)])
    part = width // groups

    def source(near_left, far_left, near_right, sent_right):
        return (near_left, far_left, near_right, *[swap(values) for values in sent_right])

    def scatter_start(*sources):
        count = len(sources)
        pieces = [len(source) - 3 for source in sources]
        columns = sum(source[2].shape[1] for source in sources) // 2
        outs = local_call(
            functools.partial(grad_kernel, pieces),
            56,
            [array(1, width, kind=f32)] * count
            + [array(1, source[2].shape[1], kind=f32) for source in sources]
            + [array(groups, part, 2 * row_len)] * count
            + [array(groups // 2, part, columns)] * 2,
            [vmem((count, groups // 2, part, 2 * row_len), bf16)],
            "s" + "v" * sum(3 + piece for piece in pieces),
            own_bits,
            *[value for source in sources for value in source],
        )
        left_sums, right_sums = outs[:count], outs[count : 2 * count]
        rest = list(outs[2 * count : 3 * count])
        rest += [value for source in sources for value in source[2:]]
        return left_sums, right_sums, (pieces, rest), tuple(outs[3 * count :])

    def travel(sent):
        return flip(sent[0], 0), flip(sent[1], 1)

    def scatter_second(started, came):
        pieces, rest = started
        count = len(pieces)
        columns = came[0].shape[2]
        sent_a, sent_b, own = local_call(
            functools.partial(second_kernel, pieces),
            56,
            [array(groups // 4, part, columns)] * 2
            + [array(groups // 4, part, 2 * columns)],
            [vmem((count, groups // 2, part, 2 * row_len), bf16)],
            "s" + "v" * (len(rest) + 2),
            own_bits,
            *rest,
            *came,
        )
        return own, (sent_a, sent_b)

    def scatter_more(bit, own, came):
        rows, _, columns = own.shape
        sent, own = local_call(
            functools.partial(third_kernel, bit),
            56,
            [
                array(rows // 2, part, columns),
                array(rows // 2, part, columns, kind=f32 if bit == bits - 1 else bf16),
            ],
            [],
            "sv" + "v" * len(came),
            own_bits,
            own,
            *came,
        )
        return own, sent

    def scatter_end(begin, own, came):
        for bit in range(begin, bits):
            own, sent = scatter_more(bit, own, came)
            came = (flip(sent, bit),)
        return own[0] + came[0][0].astype(f32)

    grad_out = to_row(after(grads_arrived, act0))
    grad_branch = (mods[1:2] * grad_out.astype(f32)).astype(bf16)
    fc2_left, _, fc2_rest, fc2_sent = scatter_start(
        source(grad_branch, swap(grad_branch), act0, act1)
    )
    h1_far, h2_far, mixed_far = swap(h1), swap(h2), swap(mixed1)
    fc2_came = travel(fc2_sent)

    pre_kept = [array(row_len, hidden)] + [array(row_len, hidden // 2)] * 2
    pre0, *pre1 = local_call(
        hidden_back_kernel,
        56,
        pre_kept,
        scratch(pre_kept)
        + [vmem((2, row_len, hidden), bf16), vmem((2, hidden, width), bf16), dma((8,)), dma((3,))],
        "vhhhh",
        after(grad_branch, fc2_sent, h1_far, h2_far, mixed_far),
        slope0,
        slope1,
        *fc2_w,
        out_kind="h",
    )
    _, fc1_right, fc1_rest, fc1_sent = scatter_start(
        source(h2, h2_far, pre0, pre1)
    )
    fc1_came = travel(fc1_sent)
    def to_target(values):
        return (
            values.reshape(groups, share, 2, half).transpose(0, 2, 1, 3).reshape(-1, share, half)
        )

    branch_ins = [after(act0, fc1_sent), fc2_w[0], *act1, fc2_w[1], grad_out, middle]
    output, branch_mods = local_call(
        branch_kernel,
        56,
        [array(row_len, width), array(1, width, kind=f32)],
        scratch(branch_ins) + [dma((7,))],
        "vv" + "h" * 7,
        mods,
        fc2_shift[None],
        *branch_ins,
    )
    output_back = exchange(to_target(output))
    fc2_own, fc2_sent = scatter_second(fc2_rest, after(fc2_came, fc1_sent, output))
    fc2_came = travel(fc2_sent[::-1])[::-1]
    row_ins = [
        after(pre0, fc2_sent),
        fc1_w[0],
        *pre1,
        fc1_w[1],
        middle,
        grad_out,
        attn,
        *proj_w,
        qn,
        kn,
        vn,
        probs,
        rq,
        rk,
    ]
    row_kept = [
        array(row_len, width, kind=f32),
        array(row_len, width),
        array(row_len, 3 * half),
        array(row_len, 3 * half // 2),
        array(row_len, 3 * half // 2),
        array(4, width, kind=f32),
    ]
    middle_grad, attn_grad, qkv_grad0, qkv1a, qkv1b, row_mods = local_call(
        row_back_kernel,
        56,
        row_kept,
        scratch(row_kept)
        + scratch(row_ins)
        + [vmem((row_len, width), f32), vmem((row_len, half), bf16), dma((16,)), dma((6,))],
        "vv" + "h" * 16,
        mods,
        head_mult,
        *row_ins,
        out_kind="h",
    )
    ready = after((qkv1a, qkv1b, attn_grad), fc2_came, fc1_came)
    attn_far = swap(ready[2])
    qkv_source = source(h1, h1_far, qkv_grad0, ready[:2])
    fc1_own, fc1_sent = scatter_second(fc1_rest, fc1_came)
    fc1_came = travel(fc1_sent[::-1])[::-1]
    fc2_own, fc2_sent = scatter_more(2, fc2_own, fc2_came)
    fc2_came = (flip(fc2_sent, 2),)
    qkv_left, qkv_right, qkv_rest, qkv_sent = scatter_start(
        after(qkv_source, fc1_sent, fc2_sent),
        (attn_grad, attn_far, mixed0, mixed_far),
    )
    qkv_came = travel(qkv_sent)
    fc2_own, fc2_sent = scatter_more(3, fc2_own, after(fc2_came, qkv_sent))
    fc2_came = (flip(fc2_sent, 3),)
    end_ins = [
        after(qkv_grad0, fc2_sent, output_back),
        qkv1a,
        qkv1b,
        resident,
        middle_grad,
        *qkv_w,
    ]
    tokens_grad, end_mods = local_call(
        input_back_kernel,
        56,
        [array(row_len, width), array(2, width, kind=f32)],
        scratch(end_ins) + [vmem((row_len, width), f32), dma((11,))],
        "v" + "h" * 11,
        mods,
        *end_ins,
    )

    row_grads = jnp.stack(
        [row_mods[2], branch_mods[0], end_mods[0], row_mods[0], end_mods[1], row_mods[1]]
    ).astype(bf16)
    scale_terms = jnp.sum(row_mods[3].reshape(2, heads, HEAD_DIM), axis=2)
    scale_sum = scale_terms[0] + swap(scale_terms[1])

    def own_half(values):
        return lax.dynamic_slice_in_dim(values, core * half, half, 0)

    bias_sum = jnp.concatenate(
        [
            qkv_right[0][0, :half],
            qkv_right[0][0, 2 * half :],
            own_half(qkv_left[1][0]),
            fc1_right[0][0],
            own_half(fc2_left[0][0]),
            scale_sum,
        ]
    )

    def double(gathered, bias_sum, bit):
        rounded = bias_sum.astype(bf16)
        count = gathered.size
        came = flip(jnp.concatenate([gathered.reshape(-1), rounded]), bit)
        theirs = came[:count].reshape(gathered.shape)
        mine = (here >> bit) & 1
        both = jnp.where(mine == 0, jnp.stack([gathered, theirs]), jnp.stack([theirs, gathered]))
        return both, rounded.astype(f32) + came[count:].astype(f32)

    gathered, bias_sum = double(row_grads.reshape(6 * width), bias_sum, 2)
    tokens_back = exchange(to_target(after(tokens_grad, row_grads)))
    qkv_own, qkv_sent = scatter_second(
        qkv_rest, after(qkv_came, fc1_came, fc2_came, gathered)
    )
    qkv_came = travel(qkv_sent[::-1])[::-1]
    fc1_own, fc1_sent = scatter_more(2, fc1_own, after(fc1_came, qkv_sent))
    fc1_came = (flip(fc1_sent, 2),)
    gathered = after(gathered, qkv_sent)
    for bit in range(2):
        gathered, bias_sum = double(gathered, bias_sum, bit)
    qkv_own, qkv_sent = scatter_more(2, qkv_own, after(qkv_came, fc1_came, gathered))
    qkv_came = (flip(qkv_sent, 2),)
    fc1_own, fc1_sent = scatter_more(3, fc1_own, after(fc1_came, qkv_sent))
    fc1_came = (flip(fc1_sent, 3),)
    gathered = after(gathered, fc1_sent)
    for bit in range(3, bits):
        gathered, bias_sum = double(gathered, bias_sum, bit)
    order = list(range(bits - 1, 2, -1)) + [1, 0, 2]
    gathered = gathered.transpose(
        *[order.index(bit) for bit in range(bits - 1, -1, -1)], bits
    ).reshape(groups, 6 * width)
    qkv_own, qkv_sent = scatter_more(3, qkv_own, after(qkv_came, fc1_came, gathered))
    qkv_came = (flip(qkv_sent, 3),)
    gathered = after(gathered, qkv_sent)
    gathered = in_order(gathered, swap(gathered), 0)
    fc2_sum = scatter_end(4, fc2_own, fc2_came)
    fc1_sum = scatter_end(4, fc1_own, fc1_came)
    qkv_sum = scatter_end(4, qkv_own, qkv_came)

    ada_weight_grad = dot_tn(lifted, gathered).reshape(ada_weight.shape)
    ada_bias_grad = jnp.sum(gathered.astype(f32), axis=0).reshape(6, width)
    grad_lifted = dot_nt(gathered, ada_weight.reshape(ada_weight.shape[0], 6 * width))
    _, silu_pull = jax.vjp(jax.nn.silu, condition)
    table_grad = lax.dot_general(
        class_picks.astype(f32),
        silu_pull(grad_lifted)[0],
        (((0,), (0,)), ((), ())),
        precision=lax.Precision.HIGHEST,
    )

    def from_rows(values):
        return values.reshape(groups, 2, share, half).swapaxes(0, 1).reshape(2, row_len, half)

    qkv_cols, proj_cols = 3 * half // 2, half // 2
    turn = qkv_cols + proj_cols
    qkv_own_sum = jnp.concatenate([qkv_sum[:, :qkv_cols], qkv_sum[:, turn : turn + qkv_cols]], 1)
    proj_sum = jnp.concatenate([qkv_sum[:, qkv_cols:turn], qkv_sum[:, turn + qkv_cols :]], 1)
    ends = [half, 2 * half, 3 * half, 3 * half + hidden, 4 * half + hidden]
    return (
        from_rows(output_back),
        from_rows(tokens_back),
        table_grad,
        ada_weight_grad,
        ada_bias_grad,
        qkv_own_sum.reshape(-1, 3, half),
        bias_sum[: ends[1]].reshape(2, half),
        bias_sum[ends[4] :],
        proj_sum.T,
        bias_sum[ends[1] : ends[2]],
        fc1_sum,
        bias_sum[ends[2] : ends[3]],
        fc2_sum.T,
        bias_sum[ends[3] : ends[4]],
    )


def solution(mesh):
    placed = (
        P(None, "dp", "mp"),
        P(),
        P(None, "dp", None),
        P(None, "dp", None),
        P(None, "dp"),
        P("dp", None, None),
        P(None, "mp"),
        P(None, None, "mp"),
        P(None, "mp"),
        P("mp"),
        P("mp", None),
        P("mp"),
        P(None, "mp"),
        P("mp"),
        P("mp", None),
        P("mp"),
        P(None, "dp", "mp"),
    )
    return jax.shard_map(
        shards,
        mesh=mesh,
        in_specs=placed,
        out_specs=(
            P(None, "dp", "mp"),
            P(None, "dp", "mp"),
            P(None, "dp"),
            P("dp", None, None),
            P(),
            P("dp", None, "mp"),
            P(None, "mp"),
            P("mp"),
            P("mp", "dp"),
            P("mp"),
            P("dp", "mp"),
            P("mp"),
            P("mp", "dp"),
            P("mp"),
        ),
        check_vma=False,
    )
```

profile of v0, /device:TPU:0, one launch (start us, length us, event | category | flops | bytes accessed | tf_op | source)
XLA Modules:
  0.0 284.6 jit_solution(18044076871166131372)
XLA Ops:
  4.9 7.1 %all-to-all-start = ((bf16[32,22,512]{2,1,0:T(8,128)(2,1)}), bf16[32,22,512]{2,1,0:T(8,128)(2,1)}, u32[]{:S(2)}, u32[]{:S(2)}) async-start(bf16[32,22,512]{2,1,0:T(8,128)(2,1)} %pad_maximum_fusion), calls=%async_computation | async-start | bytes 1572864 | tf_op jit(solution)/shard_map/all_to_all | solution.py:536
  12.4 2.1 slice_bitcast_fusion
  16.9 1.9 copy.79
  21.5 11.1 %all-to-all-done = bf16[32,22,512]{2,1,0:T(8,128)(2,1)} async-done(((bf16[32,22,512]{2,1,0:T(8,128)(2,1)}), bf16[32,22,512]{2,1,0:T(8,128)(2,1)}, u32[]{:S(2)}, u32[]{:S(2)}) %all-to-all-start) | async-done | bytes 720928 | tf_op jit(solution)/shard_map/all_to_all | solution.py:536
  32.6 3.9 %all-to-all-start.1 = ((bf16[32,16,512]{2,1,0:T(8,128)(2,1)}), bf16[32,16,512]{2,1,0:T(8,128)(2,1)}, u32[]{:S(2)}, u32[]{:S(2)}) async-start(bf16[32,16,512]{2,1,0:T(8,128)(2,1)} %bitcast.124), calls=%async_computation.1 | async-start | bytes 1048576 | tf_op jit(solution)/shard_map/all_to_all | solution.py:536
  41.3 16.2 %shard_map.281 = (bf16[256,1024]{1,0:T(8,128)(2,1)}, bf16[2,256,512]{2,1,0:T(8,128)(2,1)}, bf16[2,256,512]{2,1,0:T(8,128)(2,1)}, bf16[2,256,512]{2,1,0:T(8,128)(...) custom-call(bf16[256,1024]{1,0:T(8,128)(2,1)} %bitcast.120, ...), custom_call_target="tpu_custom_call" | custom-call | flops 1 | bytes 1 | tf_op jit(solution)/shard_map/pallas_call | solution.py:448
  57.6 1.6 copy.80
  64.7 5.3 %shard_map.282 = (f32[1,1024]{1,0:T(1,128)}, f32[1,2048]{1,0:T(1,128)}, bf16[16,64,512]{2,1,0:T(8,128)(2,1)}, bf16[8,64,1024]{2,1,0:T(8,128)(2,1)}, bf16[8,64,1024]{2,1,0:T(8,128)(2,1)}) custom-call(s32[4]{0:T(128)} %pad_add_fusion.bit_ref, bf16[256,1024]{1,0:T(8,128)(2,1)} %copy-done.6, bf16[256,1024]{1,0:T(8,128)(2,1)} %copy-done.36, ...), custom_call_target="tpu_custom_call" | custom-call | flops 1 | bytes 1 | tf_op jit(solution)/shard_map/pallas_call | solution.py:448
  70.0 1.7 collective-permute-start.15
  71.7 1.5 collective-permute-start.16
  73.1 7.4 %shard_map.283 = (bf16[256,2048]{1,0:T(8,128)(2,1)}, bf16[256,1024]{1,0:T(8,128)(2,1)}, bf16[256,1024]{1,0:T(8,128)(2,1)}) custom-call(bf16[256,1024]{1,0:T(8,128)(2,1)} %copy-done.6, bf16[256,2048]{1,0:T(8,128)(2,1)} %get-tuple-element.118.refs_0_, bf16[256,2048]{1,0:T(8,128)(2,1)} %get-tuple-element.119.refs_1_, bf16[2048,1024]{1,0:T(8,128)(2,1)} %refs_1_.2, ...), custom_call_target="tpu_custom_call" | custom-call | flops 1 | bytes 1 | tf_op jit(solution)/shard_map/pallas_call | solution.py:448
  81.2 1.6 collective-permute-done.13.refs_3_.refs_2_
  84.3 5.1 %shard_map.284 = (f32[1,1024]{1,0:T(1,128)}, f32[1,2048]{1,0:T(1,128)}, bf16[16,64,512]{2,1,0:T(8,128)(2,1)}, bf16[8,64,1024]{2,1,0:T(8,128)(2,1)}, bf16[8,64,1024]{2,1,0:T(8,128)(2,1)}) custom-call(s32[4]{0:T(128)} %pad_add_fusion.bit_ref, bf16[256,1024]{1,0:T(8,128)(2,1)} %get-tuple-element.108.refs_0_, bf16[256,1024]{1,0:T(8,128)(2,1)} %collective-permute-done.6.refs_1_, ...), custom_call_target="tpu_custom_call" | custom-call | flops 1 | bytes 1 | tf_op jit(solution)/shard_map/pallas_call | solution.py:448
  90.9 8.5 %shard_map.285 = (bf16[256,1024]{1,0:T(8,128)(2,1)}, f32[1,1024]{1,0:T(1,128)}) custom-call(f32[6,1024]{1,0:T(8,128)} %copy-done.21, f32[1,1024]{1,0:T(1,128)} %broadcast_select_fusion.6.fc2_bias, bf16[256,2048]{1,0:T(8,128)(2,1)} %get-tuple-element.125.refs_2_.refs_0_.refs_1_, bf16[2048,1024]{1,0:T(8,128)(2,1)} %refs_1_.2, ...), custom_call_target="tpu_custom_call" | custom-call | flops 1 | bytes 1 | tf_op jit(solution)/shard_map/pallas_call | solution.py:448
  100.8 4.9 %shard_map.286 = (bf16[4,64,1024]{2,1,0:T(8,128)(2,1)}, bf16[4,64,1024]{2,1,0:T(8,128)(2,1)}, bf16[4,64,2048]{2,1,0:T(8,128)(2,1)}) custom-call(s32[4]{0:T(128)} %pad_add_fusion.bit_ref, bf16[16,64,512]{2,1,0:T(8,128)(2,1)} %get-tuple-element.128.refs_0_, bf16[256,2048]{1,0:T(8,128)(2,1)} %get-tuple-element.125.refs_2_.refs_0_.refs_1_, ...), custom_call_target="tpu_custom_call" | custom-call | flops 1 | bytes 1 | tf_op jit(solution)/shard_map/pallas_call | solution.py:448
  105.7 1.7 collective-permute-start.17
  107.4 1.5 collective-permute-start.18
  111.2 4.1 %all-to-all-start.2 = ((bf16[32,16,512]{2,1,0:T(8,128)(2,1)}), bf16[32,16,512]{2,1,0:T(8,128)(2,1)S(1)}, u32[]{:S(2)}, u32[]{:S(2)}) async-start(bf16[32,16,512]{2,1,0:T(8,128)(2,1)} %bitcast.34), calls=%async_computation.2 | async-start | bytes 1048576 | tf_op jit(solution)/shard_map/all_to_all | solution.py:536
  115.4 15.6 %shard_map.287 = (f32[256,1024]{1,0:T(8,128)}, bf16[256,1024]{1,0:T(8,128)(2,1)}, bf16[256,1536]{1,0:T(8,128)(2,1)}, bf16[256,768]{1,0:T(8,128)(2,1)}, bf16[256,768]{1,0:T(8,128)(2,1)}, /*index=5*/f32[4,1024]{1,0:T(4,128)}) custom-call(f32[6,1024]{1,0:T(8,128)} %copy-done.21, f32[2,512]{1,0:T(2,128)} %pad_maximum_fusion.9.mult, ...), custom_call_target="tpu_custom_call" | custom-call | flops 1 | bytes 1 | tf_op jit(solution)/shard_map/pallas_call | solution.py:448
  131.0 4.7 %collective-permute-done.17.refs_0_ = bf16[4,64,1024]{2,1,0:T(8,128)(2,1)S(1)} collective-permute-done((bf16[4,64,1024]{2,1,0:T(8,128)(2,1)}, bf16[4,64,1024]{2,1,0:T(8,128)(2,1)S(1)}, u32[]{:S(2)}, u32[]{:S(2)}) %collective-permute-start.17) | collective-permute-done | bytes 524320 | tf_op jit(solution)/shard_map/ppermute | solution.py:515
  136.5 2.7 shard_map.288
  139.3 1.5 collective-permute-start.19
  143.6 4.8 %shard_map.289 = (bf16[4,64,1024]{2,1,0:T(8,128)(2,1)}, bf16[4,64,1024]{2,1,0:T(8,128)(2,1)}, bf16[4,64,2048]{2,1,0:T(8,128)(2,1)}) custom-call(s32[4]{0:T(128)} %pad_add_fusion.bit_ref, bf16[16,64,512]{2,1,0:T(8,128)(2,1)} %get-tuple-element.150.refs_0_, bf16[256,2048]{1,0:T(8,128)(2,1)} %get-tuple-element.133.refs_2_.refs_0_.refs_1_, ...), custom_call_target="tpu_custom_call" | custom-call | flops 1 | bytes 1 | tf_op jit(solution)/shard_map/pallas_call | solution.py:448
  149.4 6.0 %shard_map.290 = (f32[1,1024]{1,0:T(1,128)}, f32[1,1024]{1,0:T(1,128)}, f32[1,1536]{1,0:T(1,128)}, f32[1,512]{1,0:T(1,128)}, bf16[16,64,512]{2,1,0:T(8,128)(2,1)...) custom-call(s32[4]{0:T(128)} %pad_add_fusion.bit_ref, ...), custom_call_target="tpu_custom_call" | custom-call | flops 1 | bytes 1 | tf_op jit(solution)/shard_map/pallas_call | solution.py:448
  155.5 2.2 collective-permute-start.28
  158.5 2.2 shard_map.291
  160.7 7.6 %shard_map.292 = (bf16[256,1024]{1,0:T(8,128)(2,1)}, f32[2,1024]{1,0:T(2,128)}) custom-call(f32[6,1024]{1,0:T(8,128)} %copy-done.21, bf16[256,1536]{1,0:T(8,128)(2,1)} %get-tuple-element.164.refs_2_.refs_0_, bf16[256,768]{1,0:T(8,128)(2,1)} %get-tuple-element.148.refs_1_, bf16[256,768]{1,0:T(8,128)(2,1)} %get-tuple-element.149.refs_2_, ...), custom_call_target="tpu_custom_call" | custom-call | flops 1 | bytes 1 | tf_op jit(solution)/shard_map/pallas_call | solution.py:448
  172.2 1.8 collective-permute-start.30
  175.4 2.5 collective-permute-start.31
  178.0 14.3 %collective-permute-done.29.refs_0_ = bf16[4,64,1024]{2,1,0:T(8,128)(2,1)S(1)} collective-permute-done((bf16[4,64,1024]{2,1,0:T(8,128)(2,1)}, bf16[4,64,1024]{2,1,0:T(8,128)(2,1)S(1)}, u32[]{:S(2)}, u32[]{:S(2)}) %collective-permute-start.29) | collective-permute-done | bytes 524320 | tf_op jit(solution)/shard_map/ppermute | solution.py:515
  194.1 5.8 %shard_map.293 = (bf16[4,64,1024]{2,1,0:T(8,128)(2,1)}, bf16[4,64,1024]{2,1,0:T(8,128)(2,1)}, bf16[4,64,2048]{2,1,0:T(8,128)(2,1)}) custom-call(s32[4]{0:T(128)} %pad_add_fusion.bit_ref, bf16[16,64,512]{2,1,0:T(8,128)(2,1)} %get-tuple-element.174.refs_0_, bf16[16,64,512]{2,1,0:T(8,128)(2,1)} %get-tuple-element.175.refs_1_, ...), custom_call_target="tpu_custom_call" | custom-call | flops 1 | bytes 1 | tf_op jit(solution)/shard_map/pallas_call | solution.py:448
  200.5 1.6 collective-permute-start.32
  205.3 3.9 %all-to-all-start.3 = ((bf16[32,16,512]{2,1,0:T(8,128)(2,1)}), bf16[32,16,512]{2,1,0:T(8,128)(2,1)S(1)}, u32[]{:S(2)}, u32[]{:S(2)}) async-start(bf16[32,16,512]{2,1,0:T(8,128)(2,1)} %bitcast.39), calls=%async_computation.3 | async-start | bytes 1048576 | tf_op jit(solution)/shard_map/all_to_all | solution.py:536
  209.2 1.8 collective-permute-start.35
  211.0 1.5 collective-permute-start.36
  212.5 2.8 shard_map.294
  215.3 1.5 collective-permute-start.34
  219.5 1.5 broadcast_select_fusion.3
  221.0 9.2 %collective-permute-done.33 = bf16[28680]{0:T(1024)(128)(2,1)S(1)} collective-permute-done((bf16[28680]{0:T(1024)(128)(2,1)S(1)}, bf16[28680]{0:T(1024)(128)(2,1)S(1)}, u32[]{:S(2)}, u32[]{:S(2)}) %collective-permute-start.33) | collective-permute-done | bytes 57392 | tf_op jit(solution)/shard_map/ppermute | solution.py:515
  234.4 2.7 shard_map.295
  237.1 2.2 shard_map.296
  239.3 2.4 collective-permute-start.37
  243.4 1.6 collective-permute-start.38
  245.5 1.7 collective-permute-done.37
  250.1 11.6 %collective-permute-done.39 = bf16[1,64,2048]{2,1,0:T(8,128)(2,1)S(1)} collective-permute-done((bf16[1,64,2048]{2,1,0:T(8,128)(2,1)}, bf16[1,64,2048]{2,1,0:T(8,128)(2,1)S(1)}, u32[]{:S(2)}, u32[]{:S(2)}) %collective-permute-start.39) | collective-permute-done | bytes 262176 | tf_op jit(solution)/shard_map/ppermute | solution.py:515
  261.7 1.9 collective-permute-done.38.refs_0_
  264.3 2.1 shard_map.297
  272.6 10.2 %collective-permute-done.41 = bf16[1,64,2048]{2,1,0:T(8,128)(2,1)S(1)} collective-permute-done((bf16[1,64,2048]{2,1,0:T(8,128)(2,1)}, bf16[1,64,2048]{2,1,0:T(8,128)(2,1)S(1)}, u32[]{:S(2)}, u32[]{:S(2)}) %collective-permute-start.41) | collective-permute-done | bytes 262176 | tf_op jit(solution)/shard_map/ppermute | solution.py:515
  (316 shorter events, 63.9 us)
Async XLA Ops:
  0.7 40.1 %collective-permute-start.5 = (bf16[1024,2048]{1,0:T(8,128)(2,1)}, bf16[1024,2048]{1,0:T(8,128)(2,1)}, u32[]{:S(2)}, u32[]{:S(2)}) collective-permute-start(bf16[1024,2048]{1,0:T(8,128)(2,1)} %refs_1_.3), channel_id=1, source_target_pairs={{0,1},{1,0},{2,3},{3,2},{4,5},{5,4},{6,7},{7,6},{8,9},{9,8},{10,11... | collective-permute-start | bytes 12582920 | tf_op jit(solution)/shard_map/ppermute | solution.py:512
  4.9 27.7 %all-to-all-start = ((bf16[32,22,512]{2,1,0:T(8,128)(2,1)}), bf16[32,22,512]{2,1,0:T(8,128)(2,1)}, u32[]{:S(2)}, u32[]{:S(2)}) async-start(bf16[32,22,512]{2,1,0:T(8,128)(2,1)} %pad_maximum_fusion), calls=%async_computation | async-start | bytes 1572864 | tf_op jit(solution)/shard_map/all_to_all | solution.py:536
  12.1 6.7 %collective-permute-start = (f32[7176]{0:T(1024)S(1)}, f32[7176]{0:T(1024)S(1)}, u32[]{:S(2)}, u32[]{:S(2)}) collective-permute-start(f32[7176]{0:T(1024)S(1)} %concatenate.110), channel_id=1, source_target_pairs={{0,1},{1,0},{2,3},{3,2},{4,5},{5,4},{6,7},{7,6},{8,9},{9,8},{10,11... | collective-permute-start | bytes 86120 | tf_op jit(solution)/shard_map/ppermute | solution.py:512
  14.5 6.1 %collective-permute-start.1 = (bf16[1024,512]{1,0:T(8,128)(2,1)S(1)}, bf16[1024,512]{1,0:T(8,128)(2,1)}, u32[]{:S(2)}, u32[]{:S(2)}) collective-permute-start(bf16[1024,512]{1,0:T(8,128)(2,1)S(1)} %get-tuple-element.275.refs_0_.refs_5_), channel_id=1, source_target_pairs={{0,1},{1,0},{2,3},{3,2},{4,5},{5,4},{6,7},{7,6},{8,9},{9,8},{10,11... | collective-permute-start | bytes 3145736 | tf_op jit(solution)/shard_map/ppermute | solution.py:512
  14.9 25.9 %collective-permute-start.2 = (bf16[1024,512]{1,0:T(8,128)(2,1)S(1)}, bf16[1024,512]{1,0:T(8,128)(2,1)}, u32[]{:S(2)}, u32[]{:S(2)}) collective-permute-start(bf16[1024,512]{1,0:T(8,128)(2,1)S(1)} %get-tuple-element.276.refs_1_.refs_6_), channel_id=1, source_target_pairs={{0,1},{1,0},{2,3},{3,2},{4,5},{5,4},{6,7},{7,6},{8,9},{9,8},{10,11... | collective-permute-start | bytes 3145736 | tf_op jit(solution)/shard_map/ppermute | solution.py:512
  15.1 58.1 %collective-permute-start.12 = (bf16[2048,1024]{1,0:T(8,128)(2,1)}, bf16[2048,1024]{1,0:T(8,128)(2,1)}, u32[]{:S(2)}, u32[]{:S(2)}) collective-permute-start(bf16[2048,1024]{1,0:T(8,128)(2,1)} %refs_1_.2), channel_id=1, source_target_pairs={{0,1},{1,0},{2,3},{3,2},{4,5},{5,4},{6,7},{7,6},{8,9},{9,8},{10,11... | collective-permute-start | bytes 12582920 | tf_op jit(solution)/shard_map/ppermute | solution.py:512
  18.8 21.9 %collective-permute-start.3 = (bf16[1024,512]{1,0:T(8,128)(2,1)S(1)}, bf16[1024,512]{1,0:T(8,128)(2,1)}, u32[]{:S(2)}, u32[]{:S(2)}) collective-permute-start(bf16[1024,512]{1,0:T(8,128)(2,1)S(1)} %get-tuple-element.274.refs_2_.refs_7_), channel_id=1, source_target_pairs={{0,1},{1,0},{2,3},{3,2},{4,5},{5,4},{6,7},{7,6},{8,9},{9,8},{10,11... | collective-permute-start | bytes 3145736 | tf_op jit(solution)/shard_map/ppermute | solution.py:512
  20.6 20.2 %collective-permute-start.4 = (bf16[512,1024]{1,0:T(8,128)(2,1)}, bf16[512,1024]{1,0:T(8,128)(2,1)}, u32[]{:S(2)}, u32[]{:S(2)}) collective-permute-start(bf16[512,1024]{1,0:T(8,128)(2,1)} %refs_8_.3), channel_id=1, source_target_pairs={{0,1},{1,0},{2,3},{3,2},{4,5},{5,4},{6,7},{7,6},{8,9},{9,8},{10,11... | collective-permute-start | bytes 3145736 | tf_op jit(solution)/shard_map/ppermute | solution.py:512
  32.6 25.0 %all-to-all-start.1 = ((bf16[32,16,512]{2,1,0:T(8,128)(2,1)}), bf16[32,16,512]{2,1,0:T(8,128)(2,1)}, u32[]{:S(2)}, u32[]{:S(2)}) async-start(bf16[32,16,512]{2,1,0:T(8,128)(2,1)} %bitcast.124), calls=%async_computation.1 | async-start | bytes 1048576 | tf_op jit(solution)/shard_map/all_to_all | solution.py:536
  59.4 2.0 collective-permute-start.7
  59.7 3.4 %collective-permute-start.8 = (bf16[256,1024]{1,0:T(8,128)(2,1)}, bf16[256,1024]{1,0:T(8,128)(2,1)S(1)}, u32[]{:S(2)}, u32[]{:S(2)}) collective-permute-start(bf16[256,1024]{1,0:T(8,128)(2,1)} %get-tuple-element.111.refs_2_), channel_id=1, source_target_pairs={{0,1},{1,0},{2,3},{3,2},{4,5},{5,4},{6,7},{7,6},{8,9},{9,8},{10,11... | collective-permute-start | bytes 1572872 | tf_op jit(solution)/shard_map/ppermute | solution.py:512
  60.0 3.9 %collective-permute-start.9 = (bf16[256,1024]{1,0:T(8,128)(2,1)}, bf16[256,1024]{1,0:T(8,128)(2,1)S(1)}, u32[]{:S(2)}, u32[]{:S(2)}) collective-permute-start(bf16[256,1024]{1,0:T(8,128)(2,1)} %get-tuple-element.112.refs_3_), channel_id=1, source_target_pairs={{0,1},{1,0},{2,3},{3,2},{4,5},{5,4},{6,7},{7,6},{8,9},{9,8},{10,11... | collective-permute-start | bytes 1572872 | tf_op jit(solution)/shard_map/ppermute | solution.py:512
  60.2 13.0 %collective-permute-start.6 = (bf16[256,1024]{1,0:T(8,128)(2,1)}, bf16[256,1024]{1,0:T(8,128)(2,1)}, u32[]{:S(2)}, u32[]{:S(2)}) collective-permute-start(bf16[256,1024]{1,0:T(8,128)(2,1)} %get-tuple-element.108.refs_0_), channel_id=1, source_target_pairs={{0,1},{1,0},{2,3},{3,2},{4,5},{5,4},{6,7},{7,6},{8,9},{9,8},{10,11... | collective-permute-start | bytes 1572872 | tf_op jit(solution)/shard_map/ppermute | solution.py:512
  62.2 10.9 %collective-permute-start.10 = (bf16[256,1024]{1,0:T(8,128)(2,1)S(1)}, bf16[256,1024]{1,0:T(8,128)(2,1)S(1)}, u32[]{:S(2)}, u32[]{:S(2)}) collective-permute-start(bf16[256,1024]{1,0:T(8,128)(2,1)S(1)} %copy-done.22), channel_id=1, source_target_pairs={{0,1},{1,0},{2,3},{3,2},{4,5},{5,4},{6,7},{7,6},{8,9},{9,8},{10,11... | collective-permute-start | bytes 1572872 | tf_op jit(solution)/shard_map/ppermute | solution.py:512
  63.1 8.5 %collective-permute-start.11 = (bf16[256,512]{1,0:T(8,128)(2,1)}, bf16[256,512]{1,0:T(8,128)(2,1)S(1)}, u32[]{:S(2)}, u32[]{:S(2)}) collective-permute-start(bf16[256,512]{1,0:T(8,128)(2,1)} %get-tuple-element.116), channel_id=1, source_target_pairs={{0,1},{1,0},{2,3},{3,2},{4,5},{5,4},{6,7},{7,6},{8,9},{9,8},{10,11... | collective-permute-start | bytes 786440 | tf_op jit(solution)/shard_map/ppermute | solution.py:512
  70.0 29.5 %collective-permute-start.15 = (bf16[8,64,1024]{2,1,0:T(8,128)(2,1)}, bf16[8,64,1024]{2,1,0:T(8,128)(2,1)S(1)}, u32[]{:S(2)}, u32[]{:S(2)}) collective-permute-start(bf16[8,64,1024]{2,1,0:T(8,128)(2,1)} %get-tuple-element.113), channel_id=1, source_target_pairs={{0,2},{2,0},{4,6},{6,4},{8,10},{10,8},{12,14},{14,12},{16,18},{18,... | collective-permute-start | bytes 3145736 | tf_op jit(solution)/shard_map/ppermute | solution.py:515
  71.7 27.8 %collective-permute-start.16 = (bf16[8,64,1024]{2,1,0:T(8,128)(2,1)}, bf16[8,64,1024]{2,1,0:T(8,128)(2,1)S(1)}, u32[]{:S(2)}, u32[]{:S(2)}) collective-permute-start(bf16[8,64,1024]{2,1,0:T(8,128)(2,1)} %get-tuple-element.114), channel_id=1, source_target_pairs={{0,4},{2,6},{4,0},{6,2},{8,12},{10,14},{12,8},{14,10},{16,20},{18,... | collective-permute-start | bytes 3145736 | tf_op jit(solution)/shard_map/ppermute | solution.py:515
  80.6 2.2 collective-permute-start.13
  80.7 2.9 %collective-permute-start.14 = (bf16[256,1024]{1,0:T(8,128)(2,1)}, bf16[256,1024]{1,0:T(8,128)(2,1)S(1)}, u32[]{:S(2)}, u32[]{:S(2)}) collective-permute-start(bf16[256,1024]{1,0:T(8,128)(2,1)} %get-tuple-element.122.refs_3_), channel_id=1, source_target_pairs={{0,1},{1,0},{2,3},{3,2},{4,5},{5,4},{6,7},{7,6},{8,9},{9,8},{10,11... | collective-permute-start | bytes 1572872 | tf_op jit(solution)/shard_map/ppermute | solution.py:512
  89.4 51.3 %collective-permute-start.20 = (bf16[8,64,1024]{2,1,0:T(8,128)(2,1)}, bf16[8,64,1024]{2,1,0:T(8,128)(2,1)S(1)}, u32[]{:S(2)}, u32[]{:S(2)}) collective-permute-start(bf16[8,64,1024]{2,1,0:T(8,128)(2,1)} %get-tuple-element.123), channel_id=1, source_target_pairs={{0,2},{2,0},{4,6},{6,4},{8,10},{10,8},{12,14},{14,12},{16,18},{18,... | collective-permute-start | bytes 3145736 | tf_op jit(solution)/shard_map/ppermute | solution.py:515
  90.0 50.8 %collective-permute-start.21 = (bf16[8,64,1024]{2,1,0:T(8,128)(2,1)}, bf16[8,64,1024]{2,1,0:T(8,128)(2,1)S(1)}, u32[]{:S(2)}, u32[]{:S(2)}) collective-permute-start(bf16[8,64,1024]{2,1,0:T(8,128)(2,1)} %get-tuple-element.124), channel_id=1, source_target_pairs={{0,4},{2,6},{4,0},{6,2},{8,12},{10,14},{12,8},{14,10},{16,20},{18,... | collective-permute-start | bytes 3145736 | tf_op jit(solution)/shard_map/ppermute | solution.py:515
  105.7 30.1 %collective-permute-start.17 = (bf16[4,64,1024]{2,1,0:T(8,128)(2,1)}, bf16[4,64,1024]{2,1,0:T(8,128)(2,1)S(1)}, u32[]{:S(2)}, u32[]{:S(2)}) collective-permute-start(bf16[4,64,1024]{2,1,0:T(8,128)(2,1)} %get-tuple-element.131), channel_id=1, source_target_pairs={{0,4},{2,6},{4,0},{6,2},{8,12},{10,14},{12,8},{14,10},{16,20},{18,... | collective-permute-start | bytes 1572872 | tf_op jit(solution)/shard_map/ppermute | solution.py:515
  107.4 28.4 %collective-permute-start.18 = (bf16[4,64,1024]{2,1,0:T(8,128)(2,1)}, bf16[4,64,1024]{2,1,0:T(8,128)(2,1)}, u32[]{:S(2)}, u32[]{:S(2)}) collective-permute-start(bf16[4,64,1024]{2,1,0:T(8,128)(2,1)} %get-tuple-element.132), channel_id=1, source_target_pairs={{0,2},{2,0},{4,6},{6,4},{8,10},{10,8},{12,14},{14,12},{16,18},{18,... | collective-permute-start | bytes 1572872 | tf_op jit(solution)/shard_map/ppermute | solution.py:515
  111.2 49.5 %all-to-all-start.2 = ((bf16[32,16,512]{2,1,0:T(8,128)(2,1)}), bf16[32,16,512]{2,1,0:T(8,128)(2,1)S(1)}, u32[]{:S(2)}, u32[]{:S(2)}) async-start(bf16[32,16,512]{2,1,0:T(8,128)(2,1)} %bitcast.34), calls=%async_computation.2 | async-start | bytes 1048576 | tf_op jit(solution)/shard_map/all_to_all | solution.py:536
  139.3 18.4 %collective-permute-start.19 = (bf16[2,64,2048]{2,1,0:T(8,128)(2,1)}, bf16[2,64,2048]{2,1,0:T(8,128)(2,1)S(1)}, u32[]{:S(2)}, u32[]{:S(2)}) collective-permute-start(bf16[2,64,2048]{2,1,0:T(8,128)(2,1)} %get-tuple-element.144), channel_id=1, source_target_pairs={{0,8},{2,10},{4,12},{6,14},{8,0},{10,2},{12,4},{14,6},{16,24},{18,... | collective-permute-start | bytes 1572872 | tf_op jit(solution)/shard_map/ppermute | solution.py:515
  140.8 7.7 %collective-permute-start.24 = (bf16[256,1024]{1,0:T(8,128)(2,1)}, bf16[256,1024]{1,0:T(8,128)(2,1)}, u32[]{:S(2)}, u32[]{:S(2)}) collective-permute-start(bf16[256,1024]{1,0:T(8,128)(2,1)} %get-tuple-element.158.refs_5_), channel_id=1, source_target_pairs={{0,1},{1,0},{2,3},{3,2},{4,5},{5,4},{6,7},{7,6},{8,9},{9,8},{10,11... | collective-permute-start | bytes 1572872 | tf_op jit(solution)/shard_map/ppermute | solution.py:512
  141.9 6.6 %collective-permute-start.22 = (bf16[256,768]{1,0:T(8,128)(2,1)}, bf16[256,768]{1,0:T(8,128)(2,1)S(1)}, u32[]{:S(2)}, u32[]{:S(2)}) collective-permute-start(bf16[256,768]{1,0:T(8,128)(2,1)} %get-tuple-element.148.refs_1_), channel_id=1, source_target_pairs={{0,1},{1,0},{2,3},{3,2},{4,5},{5,4},{6,7},{7,6},{8,9},{9,8},{10,11... | collective-permute-start | bytes 1179656 | tf_op jit(solution)/shard_map/ppermute | solution.py:512
  142.2 6.2 %collective-permute-start.23 = (bf16[256,768]{1,0:T(8,128)(2,1)}, bf16[256,768]{1,0:T(8,128)(2,1)S(1)}, u32[]{:S(2)}, u32[]{:S(2)}) collective-permute-start(bf16[256,768]{1,0:T(8,128)(2,1)} %get-tuple-element.149.refs_2_), channel_id=1, source_target_pairs={{0,1},{1,0},{2,3},{3,2},{4,5},{5,4},{6,7},{7,6},{8,9},{9,8},{10,11... | collective-permute-start | bytes 1179656 | tf_op jit(solution)/shard_map/ppermute | solution.py:512
  142.4 29.2 %collective-permute-start.25 = (f32[8]{0:T(128)S(1)}, f32[8]{0:T(128)S(1)}, u32[]{:S(2)}, u32[]{:S(2)}) collective-permute-start(f32[8]{0:T(128)S(1)} %slice_bitcast_fusion.3), channel_id=1, source_target_pairs={{0,1},{1,0},{2,3},{3,2},{4,5},{5,4},{6,7},{7,6},{8,9},{9,8},{10,11... | collective-permute-start | bytes 104 | tf_op jit(solution)/shard_map/ppermute | solution.py:512
  155.3 37.1 %collective-permute-start.27 = (bf16[8,64,1024]{2,1,0:T(8,128)(2,1)}, bf16[8,64,1024]{2,1,0:T(8,128)(2,1)S(1)}, u32[]{:S(2)}, u32[]{:S(2)}) collective-permute-start(bf16[8,64,1024]{2,1,0:T(8,128)(2,1)} %get-tuple-element.160), channel_id=1, source_target_pairs={{0,2},{2,0},{4,6},{6,4},{8,10},{10,8},{12,14},{14,12},{16,18},{18,... | collective-permute-start | bytes 3145736 | tf_op jit(solution)/shard_map/ppermute | solution.py:515
  155.5 36.9 %collective-permute-start.28 = (bf16[8,64,1024]{2,1,0:T(8,128)(2,1)}, bf16[8,64,1024]{2,1,0:T(8,128)(2,1)S(1)}, u32[]{:S(2)}, u32[]{:S(2)}) collective-permute-start(bf16[8,64,1024]{2,1,0:T(8,128)(2,1)} %get-tuple-element.161), channel_id=1, source_target_pairs={{0,4},{2,6},{4,0},{6,2},{8,12},{10,14},{12,8},{14,10},{16,20},{18,... | collective-permute-start | bytes 3145736 | tf_op jit(solution)/shard_map/ppermute | solution.py:515
  171.6 3.9 %collective-permute-start.26 = (bf16[10248]{0:T(1024)(128)(2,1)S(1)}, bf16[10248]{0:T(1024)(128)(2,1)S(1)}, u32[]{:S(2)}, u32[]{:S(2)}) collective-permute-start(bf16[10248]{0:T(1024)(128)(2,1)S(1)} %get-tuple-element.296), channel_id=1, source_target_pairs={{0,8},{2,10},{4,12},{6,14},{8,0},{10,2},{12,4},{14,6},{16,24},{18,... | collective-permute-start | bytes 61496 | tf_op jit(solution)/shard_map/ppermute | solution.py:515
  172.2 20.2 %collective-permute-start.29 = (bf16[4,64,1024]{2,1,0:T(8,128)(2,1)}, bf16[4,64,1024]{2,1,0:T(8,128)(2,1)S(1)}, u32[]{:S(2)}, u32[]{:S(2)}) collective-permute-start(bf16[4,64,1024]{2,1,0:T(8,128)(2,1)} %get-tuple-element.151), channel_id=1, source_target_pairs={{0,4},{2,6},{4,0},{6,2},{8,12},{10,14},{12,8},{14,10},{16,20},{18,... | collective-permute-start | bytes 1572872 | tf_op jit(solution)/shard_map/ppermute | solution.py:515
  172.2 20.1 %collective-permute-start.30 = (bf16[4,64,1024]{2,1,0:T(8,128)(2,1)S(1)}, bf16[4,64,1024]{2,1,0:T(8,128)(2,1)S(1)}, u32[]{:S(2)}, u32[]{:S(2)}) collective-permute-start(bf16[4,64,1024]{2,1,0:T(8,128)(2,1)S(1)} %copy-done.58), channel_id=1, source_target_pairs={{0,2},{2,0},{4,6},{6,4},{8,10},{10,8},{12,14},{14,12},{16,18},{18,... | collective-permute-start | bytes 1572872 | tf_op jit(solution)/shard_map/ppermute | solution.py:515
  175.4 16.9 %collective-permute-start.31 = (bf16[1,64,2048]{2,1,0:T(8,128)(2,1)S(1)}, bf16[1,64,2048]{2,1,0:T(8,128)(2,1)S(1)}, u32[]{:S(2)}, u32[]{:S(2)}) collective-permute-start(bf16[1,64,2048]{2,1,0:T(8,128)(2,1)S(1)} %copy-done.59), channel_id=1, source_target_pairs={{0,16},{2,18},{4,20},{6,22},{8,24},{10,26},{12,28},{14,30},{16,0},... | collective-permute-start | bytes 786440 | tf_op jit(solution)/shard_map/ppermute | solution.py:515
  178.0 40.0 %copy-start.39 = (bf16[4104]{0:T(1024)(128)(2,1)}, bf16[4104]{0:T(1024)(128)(2,1)S(1)}, u32[]{:S(2)}) copy-start(bf16[4104]{0:T(1024)(128)(2,1)S(1)} %add_convert_fusion.2) | copy-start | bytes 24628
  200.5 16.2 %collective-permute-start.32 = (bf16[16392]{0:T(1024)(128)(2,1)}, bf16[16392]{0:T(1024)(128)(2,1)S(1)}, u32[]{:S(2)}, u32[]{:S(2)}) collective-permute-start(bf16[16392]{0:T(1024)(128)(2,1)} %pad_maximum_fusion.4), channel_id=1, source_target_pairs={{0,2},{2,0},{4,6},{6,4},{8,10},{10,8},{12,14},{14,12},{16,18},{18,... | collective-permute-start | bytes 98360 | tf_op jit(solution)/shard_map/ppermute | solution.py:515
  205.3 37.2 %all-to-all-start.3 = ((bf16[32,16,512]{2,1,0:T(8,128)(2,1)}), bf16[32,16,512]{2,1,0:T(8,128)(2,1)S(1)}, u32[]{:S(2)}, u32[]{:S(2)}) async-start(bf16[32,16,512]{2,1,0:T(8,128)(2,1)} %bitcast.39), calls=%async_computation.3 | async-start | bytes 1048576 | tf_op jit(solution)/shard_map/all_to_all | solution.py:536
  209.2 24.2 %collective-permute-start.35 = (bf16[4,64,1024]{2,1,0:T(8,128)(2,1)}, bf16[4,64,1024]{2,1,0:T(8,128)(2,1)S(1)}, u32[]{:S(2)}, u32[]{:S(2)}) collective-permute-start(bf16[4,64,1024]{2,1,0:T(8,128)(2,1)} %get-tuple-element.178), channel_id=1, source_target_pairs={{0,4},{2,6},{4,0},{6,2},{8,12},{10,14},{12,8},{14,10},{16,20},{18,... | collective-permute-start | bytes 1572872 | tf_op jit(solution)/shard_map/ppermute | solution.py:515
  211.0 22.3 %collective-permute-start.36 = (bf16[4,64,1024]{2,1,0:T(8,128)(2,1)}, bf16[4,64,1024]{2,1,0:T(8,128)(2,1)S(1)}, u32[]{:S(2)}, u32[]{:S(2)}) collective-permute-start(bf16[4,64,1024]{2,1,0:T(8,128)(2,1)} %get-tuple-element.179), channel_id=1, source_target_pairs={{0,2},{2,0},{4,6},{6,4},{8,10},{10,8},{12,14},{14,12},{16,18},{18,... | collective-permute-start | bytes 1572872 | tf_op jit(solution)/shard_map/ppermute | solution.py:515
  212.5 29.2 %copy-start.30 = (f32[1,64,2048]{2,1,0:T(8,128)S(1)}, f32[1,64,2048]{2,1,0:T(8,128)}, u32[]{:S(2)}) copy-start(f32[1,64,2048]{2,1,0:T(8,128)} %get-tuple-element.199) | copy-start | bytes 1572868
  215.3 18.1 %collective-permute-start.34 = (bf16[2,64,2048]{2,1,0:T(8,128)(2,1)}, bf16[2,64,2048]{2,1,0:T(8,128)(2,1)S(1)}, u32[]{:S(2)}, u32[]{:S(2)}) collective-permute-start(bf16[2,64,2048]{2,1,0:T(8,128)(2,1)} %get-tuple-element.185), channel_id=1, source_target_pairs={{0,8},{2,10},{4,12},{6,14},{8,0},{10,2},{12,4},{14,6},{16,24},{18,... | collective-permute-start | bytes 1572872 | tf_op jit(solution)/shard_map/ppermute | solution.py:515
  218.8 11.4 %collective-permute-start.33 = (bf16[28680]{0:T(1024)(128)(2,1)S(1)}, bf16[28680]{0:T(1024)(128)(2,1)S(1)}, u32[]{:S(2)}, u32[]{:S(2)}) collective-permute-start(bf16[28680]{0:T(1024)(128)(2,1)S(1)} %pad_maximum_fusion.3), channel_id=1, source_target_pairs={{0,4},{2,6},{4,0},{6,2},{8,12},{10,14},{12,8},{14,10},{16,20},{18,... | collective-permute-start | bytes 172088 | tf_op jit(solution)/shard_map/ppermute | solution.py:515
  239.3 7.9 %collective-permute-start.37 = (bf16[53256]{0:T(1024)(128)(2,1)S(1)}, bf16[53256]{0:T(1024)(128)(2,1)S(1)}, u32[]{:S(2)}, u32[]{:S(2)}) collective-permute-start(bf16[53256]{0:T(1024)(128)(2,1)S(1)} %pad_maximum_fusion.2), channel_id=1, source_target_pairs={{0,16},{2,18},{4,20},{6,22},{8,24},{10,26},{12,28},{14,30},{16,0},... | collective-permute-start | bytes 319544 | tf_op jit(solution)/shard_map/ppermute | solution.py:515
  243.4 20.2 %collective-permute-start.38 = (bf16[2,64,2048]{2,1,0:T(8,128)(2,1)}, bf16[2,64,2048]{2,1,0:T(8,128)(2,1)S(1)}, u32[]{:S(2)}, u32[]{:S(2)}) collective-permute-start(bf16[2,64,2048]{2,1,0:T(8,128)(2,1)} %get-tuple-element.189), channel_id=1, source_target_pairs={{0,8},{2,10},{4,12},{6,14},{8,0},{10,2},{12,4},{14,6},{16,24},{18,... | collective-permute-start | bytes 1572872 | tf_op jit(solution)/shard_map/ppermute | solution.py:515
  244.9 16.8 %collective-permute-start.39 = (bf16[1,64,2048]{2,1,0:T(8,128)(2,1)}, bf16[1,64,2048]{2,1,0:T(8,128)(2,1)S(1)}, u32[]{:S(2)}, u32[]{:S(2)}) collective-permute-start(bf16[1,64,2048]{2,1,0:T(8,128)(2,1)} %get-tuple-element.191), channel_id=1, source_target_pairs={{0,16},{2,18},{4,20},{6,22},{8,24},{10,26},{12,28},{14,30},{16,0},... | collective-permute-start | bytes 786440 | tf_op jit(solution)/shard_map/ppermute | solution.py:515
  266.5 2.3 collective-permute-start.40
  267.3 15.4 %collective-permute-start.41 = (bf16[1,64,2048]{2,1,0:T(8,128)(2,1)}, bf16[1,64,2048]{2,1,0:T(8,128)(2,1)S(1)}, u32[]{:S(2)}, u32[]{:S(2)}) collective-permute-start(bf16[1,64,2048]{2,1,0:T(8,128)(2,1)} %get-tuple-element.195), channel_id=1, source_target_pairs={{0,16},{2,18},{4,20},{6,22},{8,24},{10,26},{12,28},{14,30},{16,0},... | collective-permute-start | bytes 786440 | tf_op jit(solution)/shard_map/ppermute | solution.py:515
  (59 other events, 403.8 us)
where the time goes:
time: 289 us; the launch traced here: 285 us
  Pallas kernels  102 us (35%)
  waiting for transfers between devices  70.1 us (24%)
  starting transfers between devices  53.1 us (18%)
  local copies, waits for them, and re-layouts  41.5 us (14%)
  other arithmetic  14 us (5%)
    pallas_call x17, Pallas kernels, local_call(): pl.pallas_call(kernel, out_shape=outs, in_specs=[places[kind] for kind in...  102 us
    ppermute x22, waiting for transfers between devices, flip(): lax.ppermute(values, 'dp', [(i, i ^ 1 << bit) for i in range(groups)])  55 us
    ppermute x22, starting transfers between devices, flip(): lax.ppermute(values, 'dp', [(i, i ^ 1 << bit) for i in range(groups)])  28.9 us
    all_to_all x4, starting transfers between devices, exchange(): lax.all_to_all(values, ('dp', 'mp'), split_axis=0, concat_axis=0, tiled=T...  19.1 us
    unnamed x141, local copies, waits for them, and re-layouts  16.1 us
    all_to_all x4, waiting for transfers between devices, exchange(): lax.all_to_all(values, ('dp', 'mp'), split_axis=0, concat_axis=0, tiled=T...  11.1 us
  transfers between devices with their start and end apart: 46, of which 13 were waited for; matrix products, arithmetic and copies ran while one was open for 15% of the time, Pallas kernels for 33%

commit v1 on v0

--- a/solution.py
+++ b/solution.py
@@ -75,9 +75,9 @@
 
 
 def forward_kernel(
-    x_ref, mods, qkv_bias, mult, mask_ref, proj_bias, fc1_bias, *refs
+    share, arrived, ada_ref, qkv_bias, mult, mask_ref, proj_bias, fc1_bias, *refs
 ):
-    weights, outs, held, rest = split_refs(refs, [10, 17, 17])
+    weights, outs, (x_ref, mods), held, rest = split_refs(refs, [10, 17, 2, 17])
     qkv_w, proj_w, fc1_w, qkv_s, in_sems, out_sems = rest
     copies = start_copies(
         [(weights[i], qkv_w.at[i // 3, i % 3]) for i in range(6)]
@@ -99,6 +99,20 @@
     middle_out, h2_out, act0, act1a, act1b, slope0, slope1 = held[10:]
     rows, width = x_ref.shape
     half = width // 2
+    if share:
+        for side in range(2):
+            cols = slice(side * half, (side + 1) * half)
+            terms = jnp.zeros((8, half), f32)
+            for group in range(rows // share):
+                block = arrived.at[2 * group + side]
+                x_ref[group * share : (group + 1) * share, cols] = block[:share, :]
+                terms = terms + block[share : share + 8, :].astype(f32)
+            mods[:, cols] = ada_ref[:, cols] + terms[:6]
+            mods[2:3, cols] = mods[2:3, cols] + terms[6:7]
+            mods[4:5, cols] = mods[4:5, cols] + terms[7:8]
+    else:
+        x_ref[...] = arrived[...]
+        mods[...] = ada_ref[...]
     x = x_ref[...].astype(f32)
     h1[...] = (normalize(x)[0] * (1.0 + mods[2:3, :]) + mods[4:5, :]).astype(bf16)
     leave(0)
@@ -368,15 +382,30 @@
 
 def grad_kernel(pieces, bit_ref, *refs):
     sources = len(pieces)
-    *ins, outs = split_refs(refs, [3 + count for count in pieces])
+    count = sum(pieces) + 3 * sources
+    far, outs, got, held, rest = split_refs(refs, [count, 3 * sources + 2, count, sources + 2])
+    *ins, _ = split_refs(got, [3 + count for count in pieces])
+    picked, in_sems, out_sems = rest
+    copies = start_copies(list(zip(far, got)), in_sems)
+    waits = []
+    for piece in pieces:
+        waits.append(copies[: 3 + piece])
+        copies = copies[3 + piece :]
     left_sums, right_sums = outs[:sources], outs[sources : 2 * sources]
-    left_t = outs[2 * sources : 3 * sources]
-    sent_a, sent_b, picked = outs[3 * sources :]
+    left_t, (sent_a, sent_b) = held[:sources], held[sources:]
+    leaving = []
+
+    def leave(index):
+        copy = pltpu.make_async_copy(held[index], outs[2 * sources + index], out_sems.at[index])
+        copy.start()
+        leaving.append(copy)
+
     moved, part, columns = sent_a.shape
     tokens, half = ins[0][0].shape[0], ins[0][0].shape[1] // 2
     depth = 2 * tokens
     ones = jnp.ones((8, depth), bf16)
     for source in range(sources):
+        wait_all(waits[source][:2])
         for side in range(2):
             cols = slice(side * half, (side + 1) * half)
             near, far = ins[source][0][:, cols], ins[source][1][:, cols]
@@ -384,7 +413,10 @@
             left_sums[source][:, cols] = dot(ones, jnp.concatenate([near, far], axis=0))[0:1]
             left_t[source][rows, :, :tokens] = near.T.reshape(moved, part, tokens)
             left_t[source][rows, :, tokens:] = far.T.reshape(moved, part, tokens)
+        leave(source)
     rights = [refs[2:] for refs in ins]
+    for source in range(sources):
+        wait_all(waits[source][2:])
     for flow, sent in enumerate((sent_a, sent_b)):
         away = 1 - bit_ref[flow]
         for source in range(sources):
@@ -395,15 +427,24 @@
             left = picked[source].reshape(moved * part, depth)
             sent[:, :, to] = dot(left, right).astype(bf16).reshape(moved, part, -1)
             right_sums[source][:, at] = dot(ones, right)[0:1]
+        leave(sources + flow)
+    wait_all(leaving)
 
 
 def second_kernel(pieces, bit_ref, *refs):
     sources = len(pieces)
-    left_t, *rights, ends = split_refs(refs, [sources] + [1 + count for count in pieces])
-    came_a, came_b, sent_a, sent_b, own, picked = ends
+    count = 2 * sources + sum(pieces) + 2
+    far, outs, got, held, rest = split_refs(refs, [count, 3, count, 3])
+    left_t, *rights, (came_a, came_b) = split_refs(got, [sources] + [1 + count for count in pieces])
+    sent_a, sent_b, own = held
+    picked, in_sems, out_sems = rest
+    copies = start_copies(list(zip(far, got)), in_sems)
+    wait_all(copies[:-2])
+    leaving = []
     moved, part, columns = sent_a.shape
     depth = left_t[0].shape[2]
     for flow, (came, sent) in enumerate(((came_a, sent_a), (came_b, sent_b))):
+        copies[flow - 2].wait()
         mine, away = bit_ref[flow], 1 - bit_ref[1 - flow]
         for source in range(sources):
             for row in range(moved):
@@ -424,6 +465,9 @@
                 own[row, :, kept] = (
                     block[moved + row] + came[2 * row + 1 - away, :, to].astype(f32)
                 ).astype(bf16)
+        leaving += start_copies([(held[flow], outs[flow])], out_sems.at[pl.ds(flow, 1)])
+    leaving += start_copies([(own, outs[2])], out_sems.at[pl.ds(2, 1)])
+    wait_all(leaving)
 
 
 def third_kernel(bit, bit_ref, own, *refs):
@@ -439,7 +483,7 @@
             kept[row, :, to] = (own[near, :, to].astype(f32) + part[near].astype(f32)).astype(kept.dtype)
 
 
-def local_call(kernel, limit, outs, scratch, kinds, *values, out_kind="v"):
+def local_call(kernel, limit, outs, scratch, kinds, *values, out_kind="v", flops=1):
     places = {
         "s": pl.BlockSpec(memory_space=pltpu.SMEM),
         "v": pl.BlockSpec(memory_space=pltpu.VMEM),
@@ -449,10 +493,10 @@
         kernel,
         out_shape=outs,
         in_specs=[places[kind] for kind in kinds],
-        out_specs=[places[out_kind]] * len(outs),
+        out_specs=[places[kind] for kind in (out_kind if len(out_kind) > 1 else out_kind * len(outs))],
         scratch_shapes=scratch,
         compiler_params=pltpu.CompilerParams(vmem_limit_bytes=limit * 2**20),
-        cost_estimate=pl.CostEstimate(flops=1, bytes_accessed=1, transcendentals=0),
+        cost_estimate=pl.CostEstimate(flops=flops, bytes_accessed=1, transcendentals=0),
     )(*values)
 
 
@@ -527,7 +571,11 @@
     condition = dot(class_picks.astype(bf16), class_table)
     lifted = jax.nn.silu(condition).astype(bf16)
     ada_half = lax.dynamic_slice_in_dim(ada_weight, core * half, half, 2)
-    ada_terms = dot(lifted, ada_half.reshape(ada_half.shape[0], 6 * half)).astype(bf16)
+    ada_terms = dot(lifted, ada_half.reshape(ada_half.shape[0], 6 * half))
+    ada_terms = ada_terms.reshape(micro, groups, 6, half)
+    ada_round = lax.reduce_precision(ada_terms, 8, 7)
+    ada_rest = jnp.stack([ada_terms[:, :, c] - ada_round[:, :, c] for c in (2, 4)], axis=2)
+    ada_sent = jnp.concatenate([ada_round, ada_rest], axis=2).astype(bf16)
 
     def by_target(values):
         return values.reshape(micro, groups, -1, half).swapaxes(0, 1).reshape(2 * groups, -1, half)
@@ -540,7 +588,7 @@
             values.reshape(groups, 2, share, half).transpose(0, 2, 1, 3).reshape(row_len, width)
         )
 
-    first_message = jnp.concatenate([by_target(tokens), by_target(ada_terms)], axis=1)
+    first_message = jnp.concatenate([by_target(tokens), by_target(ada_sent)], axis=1)
     arrived = exchange(first_message)
 
     def after(values, *earlier):
@@ -581,16 +629,9 @@
         (segments[:, None] == segments[None, :]) & (levels[:, None] <= levels[None, :])
     ).astype(f32)
 
-    resident = to_row(arrived[:, :share])
     grads_arrived = exchange(
         after(by_target(out_grad), arrived, qkv_shift, head_mult, mask, proj_shift, fc1_shift, fc2_shift)
     )
-    mods = (
-        jnp.sum(arrived[:, share:].reshape(groups, 2, 6, half).astype(f32), axis=0)
-        .transpose(1, 0, 2)
-        .reshape(6, width)
-        + ada_shift
-    )
 
     def array(*dims, kind=bf16):
         return jax.ShapeDtypeStruct(dims, kind)
@@ -602,6 +643,14 @@
 
     wide = array(2, row_len, half)
     wide32 = array(2, row_len, half, kind=f32)
+    whole_tiles = share % 16 == 0
+    if whole_tiles:
+        row_in, ada_in = arrived, ada_shift
+    else:
+        row_in = to_row(arrived[:, :share])
+        terms = jnp.sum(arrived[:, share:].reshape(groups, 2, 8, half).astype(f32), axis=0)
+        terms = terms.transpose(1, 0, 2).reshape(8, width)
+        ada_in = (ada_shift + terms[:6]).at[2].add(terms[6]).at[4].add(terms[7])
     kept = [
         array(row_len, width),
         wide,
@@ -622,9 +671,9 @@
         array(row_len, hidden),
     ]
     h1, qn, kn, vn, rq, rk, probs, mixed0, mixed1, attn, middle, h2, act0, *more = local_call(
-        forward_kernel,
+        functools.partial(forward_kernel, share if whole_tiles else 0),
         56,
-        kept,
+        kept + [array(row_len, width), array(6, width, kind=f32)],
         scratch(kept)
         + [
             vmem((2, 3, width, half), bf16),
@@ -635,8 +684,8 @@
             dma((23,)),
         ],
         "vvvvvvv" + "h" * 10,
-        resident,
-        mods,
+        row_in,
+        ada_in,
         qkv_shift,
         head_mult,
         mask,
@@ -645,9 +694,9 @@
         *qkv_w,
         *proj_w,
         *fc1_w,
-        out_kind="h",
-    )
-    act1, (slope0, slope1) = more[:2], more[2:]
+        out_kind="h" * len(kept) + "vv",
+    )
+    act1, (slope0, slope1, resident, mods) = more[:2], more[2:]
 
     own_bits = jnp.stack([(here >> bit) & 1 for bit in range(bits)])
     part = width // groups
@@ -659,17 +708,27 @@
         count = len(sources)
         pieces = [len(source) - 3 for source in sources]
         columns = sum(source[2].shape[1] for source in sources) // 2
+        ins = [value for source in sources for value in source]
+        kept = [array(groups, part, 2 * row_len)] * count + [
+            array(groups // 2, part, columns)
+        ] * 2
         outs = local_call(
             functools.partial(grad_kernel, pieces),
             56,
             [array(1, width, kind=f32)] * count
             + [array(1, source[2].shape[1], kind=f32) for source in sources]
-            + [array(groups, part, 2 * row_len)] * count
-            + [array(groups // 2, part, columns)] * 2,
-            [vmem((count, groups // 2, part, 2 * row_len), bf16)],
-            "s" + "v" * sum(3 + piece for piece in pieces),
+            + kept,
+            scratch(ins)
+            + scratch(kept)
+            + [
+                vmem((count, groups // 2, part, 2 * row_len), bf16),
+                dma((len(ins),)),
+                dma((len(kept),)),
+            ],
+            "s" + "h" * len(ins),
             own_bits,
-            *[value for source in sources for value in source],
+            *ins,
+            out_kind="v" * (2 * count) + "h" * len(kept),
         )
         left_sums, right_sums = outs[:count], outs[count : 2 * count]
         rest = list(outs[2 * count : 3 * count])
@@ -679,20 +738,28 @@
     def travel(sent):
         return flip(sent[0], 0), flip(sent[1], 1)
 
-    def scatter_second(started, came):
+    def scatter_second(started, came, flops=1):
         pieces, rest = started
         count = len(pieces)
         columns = came[0].shape[2]
+        ins = [*rest, *came]
+        kept = [array(groups // 4, part, columns)] * 2 + [array(groups // 4, part, 2 * columns)]
         sent_a, sent_b, own = local_call(
             functools.partial(second_kernel, pieces),
             56,
-            [array(groups // 4, part, columns)] * 2
-            + [array(groups // 4, part, 2 * columns)],
-            [vmem((count, groups // 2, part, 2 * row_len), bf16)],
-            "s" + "v" * (len(rest) + 2),
+            kept,
+            scratch(ins)
+            + scratch(kept)
+            + [
+                vmem((count, groups // 2, part, 2 * row_len), bf16),
+                dma((len(ins),)),
+                dma((3,)),
+            ],
+            "s" + "h" * len(ins),
             own_bits,
-            *rest,
-            *came,
+            *ins,
+            out_kind="h",
+            flops=flops,
         )
         return own, (sent_a, sent_b)
 
@@ -750,19 +817,7 @@
             values.reshape(groups, share, 2, half).transpose(0, 2, 1, 3).reshape(-1, share, half)
         )
 
-    branch_ins = [after(act0, fc1_sent), fc2_w[0], *act1, fc2_w[1], grad_out, middle]
-    output, branch_mods = local_call(
-        branch_kernel,
-        56,
-        [array(row_len, width), array(1, width, kind=f32)],
-        scratch(branch_ins) + [dma((7,))],
-        "vv" + "h" * 7,
-        mods,
-        fc2_shift[None],
-        *branch_ins,
-    )
-    output_back = exchange(to_target(output))
-    fc2_own, fc2_sent = scatter_second(fc2_rest, after(fc2_came, fc1_sent, output))
+    fc2_own, fc2_sent = scatter_second(fc2_rest, after(fc2_came, fc1_sent), int(3e9))
     fc2_came = travel(fc2_sent[::-1])[::-1]
     row_ins = [
         after(pre0, fc2_sent),
@@ -801,22 +856,31 @@
         *row_ins,
         out_kind="h",
     )
-    ready = after((qkv1a, qkv1b, attn_grad), fc2_came, fc1_came)
-    attn_far = swap(ready[2])
-    qkv_source = source(h1, h1_far, qkv_grad0, ready[:2])
-    fc1_own, fc1_sent = scatter_second(fc1_rest, fc1_came)
+    fc1_own, fc1_sent = scatter_second(fc1_rest, after(fc1_came, attn_grad))
+    ready = after((qkv1a, qkv1b, attn_grad), fc2_came, fc1_sent)
     fc1_came = travel(fc1_sent[::-1])[::-1]
-    fc2_own, fc2_sent = scatter_more(2, fc2_own, fc2_came)
+    qkv_left, qkv_right, qkv_rest, qkv_sent = scatter_start(
+        source(h1, h1_far, qkv_grad0, ready[:2]),
+        (attn_grad, swap(ready[2]), mixed0, mixed_far),
+    )
+    qkv_came = travel(qkv_sent)
+    fc2_own, fc2_sent = scatter_more(2, fc2_own, after(fc2_came, qkv_sent))
     fc2_came = (flip(fc2_sent, 2),)
-    qkv_left, qkv_right, qkv_rest, qkv_sent = scatter_start(
-        after(qkv_source, fc1_sent, fc2_sent),
-        (attn_grad, attn_far, mixed0, mixed_far),
-    )
-    qkv_came = travel(qkv_sent)
-    fc2_own, fc2_sent = scatter_more(3, fc2_own, after(fc2_came, qkv_sent))
+    branch_ins = [after(act0, fc1_came, fc2_sent), fc2_w[0], *act1, fc2_w[1], grad_out, middle]
+    output, branch_mods = local_call(
+        branch_kernel,
+        56,
+        [array(row_len, width), array(1, width, kind=f32)],
+        scratch(branch_ins) + [dma((7,))],
+        "vv" + "h" * 7,
+        mods,
+        fc2_shift[None],
+        *branch_ins,
+    )
+    fc2_own, fc2_sent = scatter_more(3, fc2_own, after(fc2_came, output))
     fc2_came = (flip(fc2_sent, 3),)
     end_ins = [
-        after(qkv_grad0, fc2_sent, output_back),
+        after(qkv_grad0, fc2_sent),
         qkv1a,
         qkv1b,
         resident,
@@ -863,7 +927,11 @@
         return both, rounded.astype(f32) + came[count:].astype(f32)
 
     gathered, bias_sum = double(row_grads.reshape(6 * width), bias_sum, 2)
-    tokens_back = exchange(to_target(after(tokens_grad, row_grads)))
+    returned = exchange(
+        jnp.concatenate(
+            [to_target(values) for values in after((output, tokens_grad), row_grads)], axis=1
+        )
+    )
     qkv_own, qkv_sent = scatter_second(
         qkv_rest, after(qkv_came, fc1_came, fc2_came, gathered)
     )
@@ -871,19 +939,16 @@
     fc1_own, fc1_sent = scatter_more(2, fc1_own, after(fc1_came, qkv_sent))
     fc1_came = (flip(fc1_sent, 2),)
     gathered = after(gathered, qkv_sent)
-    for bit in range(2):
+    for bit in range(3, bits):
         gathered, bias_sum = double(gathered, bias_sum, bit)
-    qkv_own, qkv_sent = scatter_more(2, qkv_own, after(qkv_came, fc1_came, gathered))
+    qkv_own, qkv_sent = scatter_more(2, qkv_own, after(qkv_came, fc1_came, gathered, returned))
     qkv_came = (flip(qkv_sent, 2),)
     fc1_own, fc1_sent = scatter_more(3, fc1_own, after(fc1_came, qkv_sent))
     fc1_came = (flip(fc1_sent, 3),)
     gathered = after(gathered, fc1_sent)
-    for bit in range(3, bits):
+    for bit in range(2):
         gathered, bias_sum = double(gathered, bias_sum, bit)
-    order = list(range(bits - 1, 2, -1)) + [1, 0, 2]
-    gathered = gathered.transpose(
-        *[order.index(bit) for bit in range(bits - 1, -1, -1)], bits
-    ).reshape(groups, 6 * width)
+    gathered = gathered.transpose(*range(2, bits), 0, 1, bits).reshape(groups, 6 * width)
     qkv_own, qkv_sent = scatter_more(3, qkv_own, after(qkv_came, fc1_came, gathered))
     qkv_came = (flip(qkv_sent, 3),)
     gathered = after(gathered, qkv_sent)
@@ -912,8 +977,8 @@
     proj_sum = jnp.concatenate([qkv_sum[:, qkv_cols:turn], qkv_sum[:, turn + qkv_cols :]], 1)
     ends = [half, 2 * half, 3 * half, 3 * half + hidden, 4 * half + hidden]
     return (
-        from_rows(output_back),
-        from_rows(tokens_back),
+        from_rows(returned[:, :share]),
+        from_rows(returned[:, share:]),
         table_grad,
         ada_weight_grad,
         ada_bias_grad,

time: 289 us -> 265 us (0.917)
  local copies, waits for them, and re-layouts: 41.5 us -> 30.6 us
  waiting for transfers between devices: 70.1 us -> 59.5 us
  starting transfers between devices: 53.1 us -> 46.1 us
  Pallas kernels: 102 us -> 107 us
    ppermute x22, waiting for transfers between devices: 55 us -> 43.9 us  [flip(): lax.ppermute(values, 'dp', [(i, i ^ 1 << bit) for i in range(groups)])]
    all_to_all x4 -> x3, starting transfers between devices: 19.1 us -> 13.7 us  [exchange(): lax.all_to_all(values, ('dp', 'mp'), split_axis=0, concat_axis=0, tiled=T...]
    pallas_call x17, Pallas kernels: 102 us -> 107 us  [local_call(): pl.pallas_call(kernel, out_shape=outs, in_specs=[places[kind] for kind in...]
    unnamed x141 -> x133, local copies, waits for them, and re-layouts: 16.1 us -> 11.6 us
    all_to_all x4 -> x3, waiting for transfers between devices: 11.1 us -> 11.1 us  [exchange(): lax.all_to_all(values, ('dp', 'mp'), split_axis=0, concat_axis=0, tiled=T...]
  transfers between devices with their start and end apart: 46 -> 45, of which waited for: 13 -> 16; matrix products, arithmetic and copies ran while one was open for 15% -> 14% of each run, Pallas kernels for 33% -> 38%
where the time goes in v1:
time: 265 us; the launch traced here: 261 us
  Pallas kernels  107 us (40%)
  waiting for transfers between devices  59.5 us (22%)
  starting transfers between devices  46.1 us (17%)
  local copies, waits for them, and re-layouts  30.6 us (12%)
  other arithmetic  11.9 us (4%)
  matrix products  3.76 us (1%)
    pallas_call x17, Pallas kernels, local_call(): pl.pallas_call(kernel, out_shape=outs, in_specs=[places[kind] for kind in...  107 us
    ppermute x22, waiting for transfers between devices, flip(): lax.ppermute(values, 'dp', [(i, i ^ 1 << bit) for i in range(groups)])  43.9 us
    ppermute x22, starting transfers between devices, flip(): lax.ppermute(values, 'dp', [(i, i ^ 1 << bit) for i in range(groups)])  27.6 us
    all_to_all x3, starting transfers between devices, exchange(): lax.all_to_all(values, ('dp', 'mp'), split_axis=0, concat_axis=0, tiled=T...  13.7 us
    unnamed x133, local copies, waits for them, and re-layouts  11.6 us
    all_to_all x3, waiting for transfers between devices, exchange(): lax.all_to_all(values, ('dp', 'mp'), split_axis=0, concat_axis=0, tiled=T...  11.1 us
  transfers between devices with their start and end apart: 45, of which 16 were waited for; matrix products, arithmetic and copies ran while one was open for 14% of the time, Pallas kernels for 38%

profile of v1, /device:TPU:0, one launch (start us, length us, event | category | flops | bytes accessed | tf_op | source)
XLA Modules:
  0.0 260.9 jit_solution(13804336778269156545)
XLA Ops:
  5.3 7.1 %all-to-all-start = ((bf16[32,24,512]{2,1,0:T(8,128)(2,1)}), bf16[32,24,512]{2,1,0:T(8,128)(2,1)}, u32[]{:S(2)}, u32[]{:S(2)}) async-start(bf16[32,24,512]{2,1,0:T(8,128)(2,1)} %pad_maximum_fusion.1), calls=%async_computation | async-start | bytes 1572864 | tf_op jit(solution)/shard_map/all_to_all | solution.py:584
  12.8 2.1 slice_bitcast_fusion
  17.3 1.9 copy.64
  21.9 11.1 %all-to-all-done.arrived = bf16[32,24,512]{2,1,0:T(8,128)(2,1)} async-done(((bf16[32,24,512]{2,1,0:T(8,128)(2,1)}), bf16[32,24,512]{2,1,0:T(8,128)(2,1)}, u32[]{:S(2)}, u32[]{:S(2)}) %all-to-all-start) | async-done | bytes 786464 | tf_op jit(solution)/shard_map/all_to_all | solution.py:584
  33.0 3.9 %all-to-all-start.1 = ((bf16[32,16,512]{2,1,0:T(8,128)(2,1)}), bf16[32,16,512]{2,1,0:T(8,128)(2,1)}, u32[]{:S(2)}, u32[]{:S(2)}) async-start(bf16[32,16,512]{2,1,0:T(8,128)(2,1)} %bitcast.135), calls=%async_computation.1 | async-start | bytes 1048576 | tf_op jit(solution)/shard_map/all_to_all | solution.py:584
  38.2 17.1 %shard_map.281 = (bf16[256,1024]{1,0:T(8,128)(2,1)}, bf16[2,256,512]{2,1,0:T(8,128)(2,1)}, bf16[2,256,512]{2,1,0:T(8,128)(2,1)}, bf16[2,256,512]{2,1,0:T(8,128)(...) custom-call(bf16[32,24,512]{2,1,0:T(8,128)(2,1)} %all-to-all-done.ar, ...), custom_call_target="tpu_custom_call" | custom-call | flops 1 | bytes 1 | tf_op jit(solution)/shard_map/pallas_call | solution.py:492
  55.4 1.7 copy.65
  63.5 5.7 %shard_map.282 = (f32[1,1024]{1,0:T(1,128)}, f32[1,2048]{1,0:T(1,128)}, bf16[16,64,512]{2,1,0:T(8,128)(2,1)}, bf16[8,64,1024]{2,1,0:T(8,128)(2,1)}, bf16[8,64,1024]{2,1,0:T(8,128)(2,1)}) custom-call(s32[4]{0:T(128)} %pad_add_fusion.bit_ref, bf16[256,1024]{1,0:T(8,128)(2,1)} %copy-done.6, bf16[256,1024]{1,0:T(8,128)(2,1)} %copy-done.38, ...), custom_call_target="tpu_custom_call" | custom-call | flops 1 | bytes 1 | tf_op jit(solution)/shard_map/pallas_call | solution.py:492
  69.3 1.8 collective-permute-start.17
  71.1 1.5 collective-permute-start.18
  72.6 7.4 %shard_map.283 = (bf16[256,2048]{1,0:T(8,128)(2,1)}, bf16[256,1024]{1,0:T(8,128)(2,1)}, bf16[256,1024]{1,0:T(8,128)(2,1)}) custom-call(bf16[256,1024]{1,0:T(8,128)(2,1)} %copy-done.6, bf16[256,2048]{1,0:T(8,128)(2,1)} %get-tuple-element.122.refs_0_, bf16[256,2048]{1,0:T(8,128)(2,1)} %get-tuple-element.123.refs_1_, bf16[2048,1024]{1,0:T(8,128)(2,1)} %refs_1_.3, ...), custom_call_target="tpu_custom_call" | custom-call | flops 1 | bytes 1 | tf_op jit(solution)/shard_map/pallas_call | solution.py:492
  80.6 1.6 collective-permute-done.13.refs_3_.refs_2_
  83.7 5.7 %shard_map.284 = (f32[1,1024]{1,0:T(1,128)}, f32[1,2048]{1,0:T(1,128)}, bf16[16,64,512]{2,1,0:T(8,128)(2,1)}, bf16[8,64,1024]{2,1,0:T(8,128)(2,1)}, bf16[8,64,1024]{2,1,0:T(8,128)(2,1)}) custom-call(s32[4]{0:T(128)} %pad_add_fusion.bit_ref, bf16[256,1024]{1,0:T(8,128)(2,1)} %get-tuple-element.112.refs_0_, bf16[256,1024]{1,0:T(8,128)(2,1)} %copy-done.37, ...), custom_call_target="tpu_custom_call" | custom-call | flops 1 | bytes 1 | tf_op jit(solution)/shard_map/pallas_call | solution.py:492
  90.4 5.2 %collective-permute-done.17.refs_4_ = bf16[8,64,1024]{2,1,0:T(8,128)(2,1)S(1)} collective-permute-done((bf16[8,64,1024]{2,1,0:T(8,128)(2,1)}, bf16[8,64,1024]{2,1,0:T(8,128)(2,1)S(1)}, u32[]{:S(2)}, u32[]{:S(2)}) %collective-permute-start.17) | collective-permute-done | bytes 1048608 | tf_op jit(solution)/shard_map/ppermute | solution.py:559
  95.5 1.7 collective-permute-done.18.refs_5_
  98.3 5.5 %shard_map.285 = (bf16[4,64,1024]{2,1,0:T(8,128)(2,1)}, bf16[4,64,1024]{2,1,0:T(8,128)(2,1)}, bf16[4,64,2048]{2,1,0:T(8,128)(2,1)}) custom-call(s32[4]{0:T(128)} %pad_add_fusion.bit_ref, bf16[16,64,512]{2,1,0:T(8,128)(2,1)} %get-tuple-element.130.refs_0_, bf16[256,2048]{1,0:T(8,128)(2,1)} %get-tuple-element.162.refs_2_.refs_1_.refs_0_, ...), custom_call_target="tpu_custom_call" | custom-call | flops 3000000000 | bytes 1 | tf_op jit(solution)/shard_map/pallas_call | solution.py:492
  103.8 1.5 collective-permute-start.21
  105.9 16.0 %shard_map.286 = (f32[256,1024]{1,0:T(8,128)}, bf16[256,1024]{1,0:T(8,128)(2,1)}, bf16[256,1536]{1,0:T(8,128)(2,1)}, bf16[256,768]{1,0:T(8,128)(2,1)}, bf16[256,768]{1,0:T(8,128)(2,1)}, /*index=5*/f32[4,1024]{1,0:T(4,128)}) custom-call(f32[6,1024]{1,0:T(8,128)} %get-tuple-element.110.mods, f32[2,512]{1,0:T(2,128)} %pad_maximum_fusion.10.mult, ...), custom_call_target="tpu_custom_call" | custom-call | flops 1 | bytes 1 | tf_op jit(solution)/shard_map/pallas_call | solution.py:492
  123.3 5.6 %shard_map.287 = (bf16[4,64,1024]{2,1,0:T(8,128)(2,1)}, bf16[4,64,1024]{2,1,0:T(8,128)(2,1)}, bf16[4,64,2048]{2,1,0:T(8,128)(2,1)}) custom-call(s32[4]{0:T(128)} %pad_add_fusion.bit_ref, bf16[16,64,512]{2,1,0:T(8,128)(2,1)} %get-tuple-element.127.refs_0_, bf16[256,2048]{1,0:T(8,128)(2,1)} %get-tuple-element.135.refs_2_.refs_0_.refs_1_, ...), custom_call_target="tpu_custom_call" | custom-call | flops 1 | bytes 1 | tf_op jit(solution)/shard_map/pallas_call | solution.py:492
  132.4 1.5 collective-permute-start.19
  135.6 6.8 %shard_map.288 = (f32[1,1024]{1,0:T(1,128)}, f32[1,1024]{1,0:T(1,128)}, f32[1,1536]{1,0:T(1,128)}, f32[1,512]{1,0:T(1,128)}, bf16[16,64,512]{2,1,0:T(8,128)(2,1)...) custom-call(s32[4]{0:T(128)} %pad_add_fusion.bit_ref, ...), custom_call_target="tpu_custom_call" | custom-call | flops 1 | bytes 1 | tf_op jit(solution)/shard_map/pallas_call | solution.py:492
  142.4 2.7 %shard_map.289 = (bf16[2,64,2048]{2,1,0:T(8,128)(2,1)}, bf16[2,64,2048]{2,1,0:T(8,128)(2,1)}) custom-call(s32[4]{0:T(128)} %pad_add_fusion.bit_ref, bf16[4,64,2048]{2,1,0:T(8,128)(2,1)} %get-tuple-element.149.own, bf16[4,64,1024]{2,1,0:T(8,128)(2,1)} %copy-done.24, bf16[4,64,1024]{2,1,0:T(8,128)(2,1)} %copy-done.25), custom_call_target="tpu_custom_call" | custom-call | flops 1 | bytes 1 | tf_op jit(solution)/shard_map/pallas_call | solution.py:492
  145.2 1.5 collective-permute-start.26
  146.7 1.5 collective-permute-start.29
  148.8 8.5 %shard_map.290 = (bf16[256,1024]{1,0:T(8,128)(2,1)}, f32[1,1024]{1,0:T(1,128)}) custom-call(f32[6,1024]{1,0:T(8,128)} %get-tuple-element.110.mods, f32[1,1024]{1,0:T(1,128)} %broadcast_select_fusion.5.fc2_bias, bf16[256,2048]{1,0:T(8,128)(2,1)} %get-tuple-element.162.refs_2_.refs_1_.refs_0_, bf16[2048,1024]{1,0:T(8,128)(2,1)} %refs_1_.3, ...), custom_call_target="tpu_custom_call" | custom-call | flops 1 | bytes 1 | tf_op jit(solution)/shard_map/pallas_call | solution.py:492
  159.2 2.2 shard_map.291
  161.4 2.4 collective-permute-start.31
  163.7 7.6 %shard_map.292 = (bf16[256,1024]{1,0:T(8,128)(2,1)}, f32[2,1024]{1,0:T(2,128)}) custom-call(f32[6,1024]{1,0:T(8,128)} %get-tuple-element.110.mods, bf16[256,1536]{1,0:T(8,128)(2,1)} %get-tuple-element.167.refs_2_.refs_0_, bf16[256,768]{1,0:T(8,128)(2,1)} %get-tuple-element.153.refs_1_, bf16[256,768]{1,0:T(8,128)(2,1)} %get-tuple-element.154.refs_2_, ...), custom_call_target="tpu_custom_call" | custom-call | flops 1 | bytes 1 | tf_op jit(solution)/shard_map/pallas_call | solution.py:492
  173.6 1.6 collective-permute-start.28
  175.6 1.4 reshape.359
  178.2 2.7 %all-to-all-start.2 = ((bf16[32,32,512]{2,1,0:T(8,128)(2,1)}), bf16[32,32,512]{2,1,0:T(8,128)(2,1)S(1)}, u32[]{:S(2)}, u32[]{:S(2)}) async-start(bf16[32,32,512]{2,1,0:T(8,128)(2,1)} %pad_maximum_fusion), calls=%async_computation.2 | async-start | bytes 2097152 | tf_op jit(solution)/shard_map/all_to_all | solution.py:584
  183.1 6.4 %shard_map.293 = (bf16[4,64,1024]{2,1,0:T(8,128)(2,1)}, bf16[4,64,1024]{2,1,0:T(8,128)(2,1)}, bf16[4,64,2048]{2,1,0:T(8,128)(2,1)}) custom-call(s32[4]{0:T(128)} %pad_add_fusion.bit_ref, bf16[16,64,512]{2,1,0:T(8,128)(2,1)} %get-tuple-element.180.refs_0_, bf16[16,64,512]{2,1,0:T(8,128)(2,1)} %get-tuple-element.181.refs_1_, ...), custom_call_target="tpu_custom_call" | custom-call | flops 1 | bytes 1 | tf_op jit(solution)/shard_map/pallas_call | solution.py:492
  189.5 2.7 %collective-permute-start.32 = (bf16[16392]{0:T(1024)(128)(2,1)S(1)}, bf16[16392]{0:T(1024)(128)(2,1)S(1)}, u32[]{:S(2)}, u32[]{:S(2)}) collective-permute-start(bf16[16392]{0:T(1024)(128)(2,1)S(1)} %pad_maximum_fusion.5), channel_id=1, source_target_pairs={{0,16},{2,18},{4,20},{6,22},{8,24},{10,26},{12,28},{14,30},{16,0},... | collective-permute-start | bytes 98360 | tf_op jit(solution)/shard_map/ppermute | solution.py:559
  193.1 1.5 collective-permute-start.34
  194.6 1.5 collective-permute-start.35
  196.1 2.8 %shard_map.294 = (bf16[2,64,2048]{2,1,0:T(8,128)(2,1)}, bf16[2,64,2048]{2,1,0:T(8,128)(2,1)}) custom-call(s32[4]{0:T(128)} %pad_add_fusion.bit_ref, bf16[4,64,2048]{2,1,0:T(8,128)(2,1)} %get-tuple-element.187.own, bf16[4,64,1024]{2,1,0:T(8,128)(2,1)} %copy-done.21, bf16[4,64,1024]{2,1,0:T(8,128)(2,1)} %copy-done.22), custom_call_target="tpu_custom_call" | custom-call | flops 1 | bytes 1 | tf_op jit(solution)/shard_map/pallas_call | solution.py:492
  198.8 1.5 collective-permute-start.33
  200.4 8.3 %collective-permute-done.32 = bf16[16392]{0:T(1024)(128)(2,1)S(1)} collective-permute-done((bf16[16392]{0:T(1024)(128)(2,1)S(1)}, bf16[16392]{0:T(1024)(128)(2,1)S(1)}, u32[]{:S(2)}, u32[]{:S(2)}) %collective-permute-start.32) | collective-permute-done | bytes 32816 | tf_op jit(solution)/shard_map/ppermute | solution.py:559
  208.8 7.0 %collective-permute-done.33.refs_0_ = bf16[2,64,2048]{2,1,0:T(8,128)(2,1)S(1)} collective-permute-done((bf16[2,64,2048]{2,1,0:T(8,128)(2,1)}, bf16[2,64,2048]{2,1,0:T(8,128)(2,1)S(1)}, u32[]{:S(2)}, u32[]{:S(2)}) %collective-permute-start.33) | collective-permute-done | bytes 524320 | tf_op jit(solution)/shard_map/ppermute | solution.py:559
  216.8 2.7 %shard_map.295 = (bf16[2,64,2048]{2,1,0:T(8,128)(2,1)}, bf16[2,64,2048]{2,1,0:T(8,128)(2,1)}) custom-call(s32[4]{0:T(128)} %pad_add_fusion.bit_ref, bf16[4,64,2048]{2,1,0:T(8,128)(2,1)} %get-tuple-element.192.own, bf16[4,64,1024]{2,1,0:T(8,128)(2,1)} %copy-done.27, bf16[4,64,1024]{2,1,0:T(8,128)(2,1)} %copy-done.28), custom_call_target="tpu_custom_call" | custom-call | flops 1 | bytes 1 | tf_op jit(solution)/shard_map/pallas_call | solution.py:492
  219.5 2.2 shard_map.296
  221.7 2.3 collective-permute-start.38
  226.8 1.4 collective-permute-done.36
  229.5 3.8 %collective-permute-done.37 = bf16[53256]{0:T(1024)(128)(2,1)S(1)} collective-permute-done((bf16[53256]{0:T(1024)(128)(2,1)S(1)}, bf16[53256]{0:T(1024)(128)(2,1)S(1)}, u32[]{:S(2)}, u32[]{:S(2)}) %collective-permute-start.37) | collective-permute-done | bytes 106544 | tf_op jit(solution)/shard_map/ppermute | solution.py:559
  236.3 4.1 %collective-permute-done.38.refs_0_ = bf16[2,64,2048]{2,1,0:T(8,128)(2,1)S(1)} collective-permute-done((bf16[2,64,2048]{2,1,0:T(8,128)(2,1)}, bf16[2,64,2048]{2,1,0:T(8,128)(2,1)S(1)}, u32[]{:S(2)}, u32[]{:S(2)}) %collective-permute-start.38) | collective-permute-done | bytes 524320 | tf_op jit(solution)/shard_map/ppermute | solution.py:559
  241.2 2.2 shard_map.297
  246.4 1.2 copy.97
  248.7 10.4 %collective-permute-done.41 = bf16[1,64,2048]{2,1,0:T(8,128)(2,1)S(1)} collective-permute-done((bf16[1,64,2048]{2,1,0:T(8,128)(2,1)}, bf16[1,64,2048]{2,1,0:T(8,128)(2,1)S(1)}, u32[]{:S(2)}, u32[]{:S(2)}) %collective-permute-start.41) | collective-permute-done | bytes 262176 | tf_op jit(solution)/shard_map/ppermute | solution.py:559
  (304 shorter events, 52.4 us)
Async XLA Ops:
  0.7 37.5 %collective-permute-start.5 = (bf16[1024,2048]{1,0:T(8,128)(2,1)}, bf16[1024,2048]{1,0:T(8,128)(2,1)}, u32[]{:S(2)}, u32[]{:S(2)}) collective-permute-start(bf16[1024,2048]{1,0:T(8,128)(2,1)} %refs_1_.2), channel_id=1, source_target_pairs={{0,1},{1,0},{2,3},{3,2},{4,5},{5,4},{6,7},{7,6},{8,9},{9,8},{10,11... | collective-permute-start | bytes 12582920 | tf_op jit(solution)/shard_map/ppermute | solution.py:556
  5.3 27.7 %all-to-all-start = ((bf16[32,24,512]{2,1,0:T(8,128)(2,1)}), bf16[32,24,512]{2,1,0:T(8,128)(2,1)}, u32[]{:S(2)}, u32[]{:S(2)}) async-start(bf16[32,24,512]{2,1,0:T(8,128)(2,1)} %pad_maximum_fusion.1), calls=%async_computation | async-start | bytes 1572864 | tf_op jit(solution)/shard_map/all_to_all | solution.py:584
  12.6 6.6 %collective-permute-start = (f32[7176]{0:T(1024)S(1)}, f32[7176]{0:T(1024)S(1)}, u32[]{:S(2)}, u32[]{:S(2)}) collective-permute-start(f32[7176]{0:T(1024)S(1)} %concatenate.118), channel_id=1, source_target_pairs={{0,1},{1,0},{2,3},{3,2},{4,5},{5,4},{6,7},{7,6},{8,9},{9,8},{10,11... | collective-permute-start | bytes 86120 | tf_op jit(solution)/shard_map/ppermute | solution.py:556
  14.9 23.3 %copy-start.2 = (bf16[1024,512]{1,0:T(8,128)(2,1)}, bf16[1024,512]{1,0:T(8,128)(2,1)S(1)}, u32[]{:S(2)}) copy-start(bf16[1024,512]{1,0:T(8,128)(2,1)S(1)} %get-tuple-element.266.refs_2_.refs_7_) | copy-start | bytes 3145732
  14.9 23.3 %copy-start.3 = (bf16[1024,512]{1,0:T(8,128)(2,1)}, bf16[1024,512]{1,0:T(8,128)(2,1)S(1)}, u32[]{:S(2)}) copy-start(bf16[1024,512]{1,0:T(8,128)(2,1)S(1)} %get-tuple-element.267.refs_0_.refs_5_) | copy-start | bytes 3145732
  14.9 23.3 %copy-start.4 = (bf16[1024,512]{1,0:T(8,128)(2,1)}, bf16[1024,512]{1,0:T(8,128)(2,1)S(1)}, u32[]{:S(2)}) copy-start(bf16[1024,512]{1,0:T(8,128)(2,1)S(1)} %get-tuple-element.268.refs_1_.refs_6_) | copy-start | bytes 3145732
  14.9 6.0 %collective-permute-start.1 = (bf16[1024,512]{1,0:T(8,128)(2,1)S(1)}, bf16[1024,512]{1,0:T(8,128)(2,1)}, u32[]{:S(2)}, u32[]{:S(2)}) collective-permute-start(bf16[1024,512]{1,0:T(8,128)(2,1)S(1)} %get-tuple-element.267.refs_0_.refs_5_), channel_id=1, source_target_pairs={{0,1},{1,0},{2,3},{3,2},{4,5},{5,4},{6,7},{7,6},{8,9},{9,8},{10,11... | collective-permute-start | bytes 3145736 | tf_op jit(solution)/shard_map/ppermute | solution.py:556
  15.3 22.9 %collective-permute-start.2 = (bf16[1024,512]{1,0:T(8,128)(2,1)S(1)}, bf16[1024,512]{1,0:T(8,128)(2,1)}, u32[]{:S(2)}, u32[]{:S(2)}) collective-permute-start(bf16[1024,512]{1,0:T(8,128)(2,1)S(1)} %get-tuple-element.268.refs_1_.refs_6_), channel_id=1, source_target_pairs={{0,1},{1,0},{2,3},{3,2},{4,5},{5,4},{6,7},{7,6},{8,9},{9,8},{10,11... | collective-permute-start | bytes 3145736 | tf_op jit(solution)/shard_map/ppermute | solution.py:556
  15.5 57.1 %collective-permute-start.12 = (bf16[2048,1024]{1,0:T(8,128)(2,1)}, bf16[2048,1024]{1,0:T(8,128)(2,1)}, u32[]{:S(2)}, u32[]{:S(2)}) collective-permute-start(bf16[2048,1024]{1,0:T(8,128)(2,1)} %refs_1_.3), channel_id=1, source_target_pairs={{0,1},{1,0},{2,3},{3,2},{4,5},{5,4},{6,7},{7,6},{8,9},{9,8},{10,11... | collective-permute-start | bytes 12582920 | tf_op jit(solution)/shard_map/ppermute | solution.py:556
  19.2 19.0 %collective-permute-start.3 = (bf16[1024,512]{1,0:T(8,128)(2,1)S(1)}, bf16[1024,512]{1,0:T(8,128)(2,1)}, u32[]{:S(2)}, u32[]{:S(2)}) collective-permute-start(bf16[1024,512]{1,0:T(8,128)(2,1)S(1)} %get-tuple-element.266.refs_2_.refs_7_), channel_id=1, source_target_pairs={{0,1},{1,0},{2,3},{3,2},{4,5},{5,4},{6,7},{7,6},{8,9},{9,8},{10,11... | collective-permute-start | bytes 3145736 | tf_op jit(solution)/shard_map/ppermute | solution.py:556
  21.0 17.2 %collective-permute-start.4 = (bf16[512,1024]{1,0:T(8,128)(2,1)}, bf16[512,1024]{1,0:T(8,128)(2,1)}, u32[]{:S(2)}, u32[]{:S(2)}) collective-permute-start(bf16[512,1024]{1,0:T(8,128)(2,1)} %refs_8_.3), channel_id=1, source_target_pairs={{0,1},{1,0},{2,3},{3,2},{4,5},{5,4},{6,7},{7,6},{8,9},{9,8},{10,11... | collective-permute-start | bytes 3145736 | tf_op jit(solution)/shard_map/ppermute | solution.py:556
  33.0 22.4 %all-to-all-start.1 = ((bf16[32,16,512]{2,1,0:T(8,128)(2,1)}), bf16[32,16,512]{2,1,0:T(8,128)(2,1)}, u32[]{:S(2)}, u32[]{:S(2)}) async-start(bf16[32,16,512]{2,1,0:T(8,128)(2,1)} %bitcast.135), calls=%async_computation.1 | async-start | bytes 1048576 | tf_op jit(solution)/shard_map/all_to_all | solution.py:584
  58.1 2.0 collective-permute-start.7
  58.4 3.6 %collective-permute-start.8 = (bf16[256,1024]{1,0:T(8,128)(2,1)S(1)}, bf16[256,1024]{1,0:T(8,128)(2,1)S(1)}, u32[]{:S(2)}, u32[]{:S(2)}) collective-permute-start(bf16[256,1024]{1,0:T(8,128)(2,1)S(1)} %copy-done.18), channel_id=1, source_target_pairs={{0,1},{1,0},{2,3},{3,2},{4,5},{5,4},{6,7},{7,6},{8,9},{9,8},{10,11... | collective-permute-start | bytes 1572872 | tf_op jit(solution)/shard_map/ppermute | solution.py:556
  58.7 4.8 %collective-permute-start.9 = (bf16[256,1024]{1,0:T(8,128)(2,1)S(1)}, bf16[256,1024]{1,0:T(8,128)(2,1)}, u32[]{:S(2)}, u32[]{:S(2)}) collective-permute-start(bf16[256,1024]{1,0:T(8,128)(2,1)S(1)} %copy-done.19), channel_id=1, source_target_pairs={{0,1},{1,0},{2,3},{3,2},{4,5},{5,4},{6,7},{7,6},{8,9},{9,8},{10,11... | collective-permute-start | bytes 1572872 | tf_op jit(solution)/shard_map/ppermute | solution.py:556
  58.9 12.2 %collective-permute-start.11 = (bf16[256,512]{1,0:T(8,128)(2,1)}, bf16[256,512]{1,0:T(8,128)(2,1)S(1)}, u32[]{:S(2)}, u32[]{:S(2)}) collective-permute-start(bf16[256,512]{1,0:T(8,128)(2,1)} %get-tuple-element.120), channel_id=1, source_target_pairs={{0,1},{1,0},{2,3},{3,2},{4,5},{5,4},{6,7},{7,6},{8,9},{9,8},{10,11... | collective-permute-start | bytes 786440 | tf_op jit(solution)/shard_map/ppermute | solution.py:556
  60.9 11.6 %collective-permute-start.10 = (bf16[256,1024]{1,0:T(8,128)(2,1)S(1)}, bf16[256,1024]{1,0:T(8,128)(2,1)S(1)}, u32[]{:S(2)}, u32[]{:S(2)}) collective-permute-start(bf16[256,1024]{1,0:T(8,128)(2,1)S(1)} %copy-done.20), channel_id=1, source_target_pairs={{0,1},{1,0},{2,3},{3,2},{4,5},{5,4},{6,7},{7,6},{8,9},{9,8},{10,11... | collective-permute-start | bytes 1572872 | tf_op jit(solution)/shard_map/ppermute | solution.py:556
  62.8 9.8 %collective-permute-start.6 = (bf16[256,1024]{1,0:T(8,128)(2,1)}, bf16[256,1024]{1,0:T(8,128)(2,1)S(1)}, u32[]{:S(2)}, u32[]{:S(2)}) collective-permute-start(bf16[256,1024]{1,0:T(8,128)(2,1)} %get-tuple-element.112.refs_0_), channel_id=1, source_target_pairs={{0,1},{1,0},{2,3},{3,2},{4,5},{5,4},{6,7},{7,6},{8,9},{9,8},{10,11... | collective-permute-start | bytes 1572872 | tf_op jit(solution)/shard_map/ppermute | solution.py:556
  69.3 26.3 %collective-permute-start.17 = (bf16[8,64,1024]{2,1,0:T(8,128)(2,1)}, bf16[8,64,1024]{2,1,0:T(8,128)(2,1)S(1)}, u32[]{:S(2)}, u32[]{:S(2)}) collective-permute-start(bf16[8,64,1024]{2,1,0:T(8,128)(2,1)} %get-tuple-element.117), channel_id=1, source_target_pairs={{0,2},{2,0},{4,6},{6,4},{8,10},{10,8},{12,14},{14,12},{16,18},{18,... | collective-permute-start | bytes 3145736 | tf_op jit(solution)/shard_map/ppermute | solution.py:559
  71.1 26.2 %collective-permute-start.18 = (bf16[8,64,1024]{2,1,0:T(8,128)(2,1)}, bf16[8,64,1024]{2,1,0:T(8,128)(2,1)S(1)}, u32[]{:S(2)}, u32[]{:S(2)}) collective-permute-start(bf16[8,64,1024]{2,1,0:T(8,128)(2,1)} %get-tuple-element.118), channel_id=1, source_target_pairs={{0,4},{2,6},{4,0},{6,2},{8,12},{10,14},{12,8},{14,10},{16,20},{18,... | collective-permute-start | bytes 3145736 | tf_op jit(solution)/shard_map/ppermute | solution.py:559
  80.0 2.2 collective-permute-start.13
  80.1 2.9 %collective-permute-start.14 = (bf16[256,1024]{1,0:T(8,128)(2,1)}, bf16[256,1024]{1,0:T(8,128)(2,1)S(1)}, u32[]{:S(2)}, u32[]{:S(2)}) collective-permute-start(bf16[256,1024]{1,0:T(8,128)(2,1)} %get-tuple-element.126.refs_3_), channel_id=1, source_target_pairs={{0,1},{1,0},{2,3},{3,2},{4,5},{5,4},{6,7},{7,6},{8,9},{9,8},{10,11... | collective-permute-start | bytes 1572872 | tf_op jit(solution)/shard_map/ppermute | solution.py:556
  89.4 32.5 %collective-permute-start.15 = (bf16[8,64,1024]{2,1,0:T(8,128)(2,1)}, bf16[8,64,1024]{2,1,0:T(8,128)(2,1)S(1)}, u32[]{:S(2)}, u32[]{:S(2)}) collective-permute-start(bf16[8,64,1024]{2,1,0:T(8,128)(2,1)} %get-tuple-element.128), channel_id=1, source_target_pairs={{0,2},{2,0},{4,6},{6,4},{8,10},{10,8},{12,14},{14,12},{16,18},{18,... | collective-permute-start | bytes 3145736 | tf_op jit(solution)/shard_map/ppermute | solution.py:559
  90.0 31.9 %collective-permute-start.16 = (bf16[8,64,1024]{2,1,0:T(8,128)(2,1)}, bf16[8,64,1024]{2,1,0:T(8,128)(2,1)S(1)}, u32[]{:S(2)}, u32[]{:S(2)}) collective-permute-start(bf16[8,64,1024]{2,1,0:T(8,128)(2,1)} %get-tuple-element.129), channel_id=1, source_target_pairs={{0,4},{2,6},{4,0},{6,2},{8,12},{10,14},{12,8},{14,10},{16,20},{18,... | collective-permute-start | bytes 3145736 | tf_op jit(solution)/shard_map/ppermute | solution.py:559
  103.8 26.4 %collective-permute-start.21 = (bf16[4,64,1024]{2,1,0:T(8,128)(2,1)}, bf16[4,64,1024]{2,1,0:T(8,128)(2,1)S(1)}, u32[]{:S(2)}, u32[]{:S(2)}) collective-permute-start(bf16[4,64,1024]{2,1,0:T(8,128)(2,1)} %get-tuple-element.133), channel_id=1, source_target_pairs={{0,4},{2,6},{4,0},{6,2},{8,12},{10,14},{12,8},{14,10},{16,20},{18,... | collective-permute-start | bytes 1572872 | tf_op jit(solution)/shard_map/ppermute | solution.py:559
  105.3 24.8 %collective-permute-start.22 = (bf16[4,64,1024]{2,1,0:T(8,128)(2,1)}, bf16[4,64,1024]{2,1,0:T(8,128)(2,1)S(1)}, u32[]{:S(2)}, u32[]{:S(2)}) collective-permute-start(bf16[4,64,1024]{2,1,0:T(8,128)(2,1)} %get-tuple-element.134), channel_id=1, source_target_pairs={{0,2},{2,0},{4,6},{6,4},{8,10},{10,8},{12,14},{14,12},{16,18},{18,... | collective-permute-start | bytes 1572872 | tf_op jit(solution)/shard_map/ppermute | solution.py:559
  130.1 4.6 %collective-permute-start.25 = (bf16[256,1024]{1,0:T(8,128)(2,1)S(1)}, bf16[256,1024]{1,0:T(8,128)(2,1)}, u32[]{:S(2)}, u32[]{:S(2)}) collective-permute-start(bf16[256,1024]{1,0:T(8,128)(2,1)S(1)} %copy-done.26), channel_id=1, source_target_pairs={{0,1},{1,0},{2,3},{3,2},{4,5},{5,4},{6,7},{7,6},{8,9},{9,8},{10,11... | collective-permute-start | bytes 1572872 | tf_op jit(solution)/shard_map/ppermute | solution.py:556
  130.2 4.5 %collective-permute-start.23 = (bf16[256,768]{1,0:T(8,128)(2,1)}, bf16[256,768]{1,0:T(8,128)(2,1)S(1)}, u32[]{:S(2)}, u32[]{:S(2)}) collective-permute-start(bf16[256,768]{1,0:T(8,128)(2,1)} %get-tuple-element.153.refs_1_), channel_id=1, source_target_pairs={{0,1},{1,0},{2,3},{3,2},{4,5},{5,4},{6,7},{7,6},{8,9},{9,8},{10,11... | collective-permute-start | bytes 1179656 | tf_op jit(solution)/shard_map/ppermute | solution.py:556
  130.7 4.0 %collective-permute-start.24 = (bf16[256,768]{1,0:T(8,128)(2,1)}, bf16[256,768]{1,0:T(8,128)(2,1)S(1)}, u32[]{:S(2)}, u32[]{:S(2)}) collective-permute-start(bf16[256,768]{1,0:T(8,128)(2,1)} %get-tuple-element.154.refs_2_), channel_id=1, source_target_pairs={{0,1},{1,0},{2,3},{3,2},{4,5},{5,4},{6,7},{7,6},{8,9},{9,8},{10,11... | collective-permute-start | bytes 1179656 | tf_op jit(solution)/shard_map/ppermute | solution.py:556
  132.4 15.8 %collective-permute-start.19 = (bf16[4,64,1024]{2,1,0:T(8,128)(2,1)}, bf16[4,64,1024]{2,1,0:T(8,128)(2,1)S(1)}, u32[]{:S(2)}, u32[]{:S(2)}) collective-permute-start(bf16[4,64,1024]{2,1,0:T(8,128)(2,1)} %get-tuple-element.147), channel_id=1, source_target_pairs={{0,4},{2,6},{4,0},{6,2},{8,12},{10,14},{12,8},{14,10},{16,20},{18,... | collective-permute-start | bytes 1572872 | tf_op jit(solution)/shard_map/ppermute | solution.py:559
  133.9 14.8 %collective-permute-start.20 = (bf16[4,64,1024]{2,1,0:T(8,128)(2,1)}, bf16[4,64,1024]{2,1,0:T(8,128)(2,1)S(1)}, u32[]{:S(2)}, u32[]{:S(2)}) collective-permute-start(bf16[4,64,1024]{2,1,0:T(8,128)(2,1)} %get-tuple-element.148), channel_id=1, source_target_pairs={{0,2},{2,0},{4,6},{6,4},{8,10},{10,8},{12,14},{14,12},{16,18},{18,... | collective-permute-start | bytes 1572872 | tf_op jit(solution)/shard_map/ppermute | solution.py:559
  145.2 14.0 %collective-permute-start.26 = (bf16[2,64,2048]{2,1,0:T(8,128)(2,1)}, bf16[2,64,2048]{2,1,0:T(8,128)(2,1)}, u32[]{:S(2)}, u32[]{:S(2)}) collective-permute-start(bf16[2,64,2048]{2,1,0:T(8,128)(2,1)} %get-tuple-element.161), channel_id=1, source_target_pairs={{0,8},{2,10},{4,12},{6,14},{8,0},{10,2},{12,4},{14,6},{16,24},{18,... | collective-permute-start | bytes 1572872 | tf_op jit(solution)/shard_map/ppermute | solution.py:559
  146.6 26.9 %collective-permute-start.27 = (f32[8]{0:T(128)S(1)}, f32[8]{0:T(128)S(1)}, u32[]{:S(2)}, u32[]{:S(2)}) collective-permute-start(f32[8]{0:T(128)S(1)} %slice_bitcast_fusion.3), channel_id=1, source_target_pairs={{0,1},{1,0},{2,3},{3,2},{4,5},{5,4},{6,7},{7,6},{8,9},{9,8},{10,11... | collective-permute-start | bytes 104 | tf_op jit(solution)/shard_map/ppermute | solution.py:556
  146.7 35.1 %collective-permute-start.29 = (bf16[8,64,1024]{2,1,0:T(8,128)(2,1)}, bf16[8,64,1024]{2,1,0:T(8,128)(2,1)S(1)}, u32[]{:S(2)}, u32[]{:S(2)}) collective-permute-start(bf16[8,64,1024]{2,1,0:T(8,128)(2,1)} %get-tuple-element.157), channel_id=1, source_target_pairs={{0,2},{2,0},{4,6},{6,4},{8,10},{10,8},{12,14},{14,12},{16,18},{18,... | collective-permute-start | bytes 3145736 | tf_op jit(solution)/shard_map/ppermute | solution.py:559
  148.2 33.6 %collective-permute-start.30 = (bf16[8,64,1024]{2,1,0:T(8,128)(2,1)}, bf16[8,64,1024]{2,1,0:T(8,128)(2,1)S(1)}, u32[]{:S(2)}, u32[]{:S(2)}) collective-permute-start(bf16[8,64,1024]{2,1,0:T(8,128)(2,1)} %get-tuple-element.158), channel_id=1, source_target_pairs={{0,4},{2,6},{4,0},{6,2},{8,12},{10,14},{12,8},{14,10},{16,20},{18,... | collective-permute-start | bytes 3145736 | tf_op jit(solution)/shard_map/ppermute | solution.py:559
  161.4 20.4 %collective-permute-start.31 = (bf16[1,64,2048]{2,1,0:T(8,128)(2,1)}, bf16[1,64,2048]{2,1,0:T(8,128)(2,1)S(1)}, u32[]{:S(2)}, u32[]{:S(2)}) collective-permute-start(bf16[1,64,2048]{2,1,0:T(8,128)(2,1)} %get-tuple-element.166), channel_id=1, source_target_pairs={{0,16},{2,18},{4,20},{6,22},{8,24},{10,26},{12,28},{14,30},{16,0},... | collective-permute-start | bytes 786440 | tf_op jit(solution)/shard_map/ppermute | solution.py:559
  173.6 7.3 %collective-permute-start.28 = (bf16[10248]{0:T(1024)(128)(2,1)S(1)}, bf16[10248]{0:T(1024)(128)(2,1)S(1)}, u32[]{:S(2)}, u32[]{:S(2)}) collective-permute-start(bf16[10248]{0:T(1024)(128)(2,1)S(1)} %get-tuple-element.294), channel_id=1, source_target_pairs={{0,8},{2,10},{4,12},{6,14},{8,0},{10,2},{12,4},{14,6},{16,24},{18,... | collective-permute-start | bytes 61496 | tf_op jit(solution)/shard_map/ppermute | solution.py:559
  178.2 37.6 %all-to-all-start.2 = ((bf16[32,32,512]{2,1,0:T(8,128)(2,1)}), bf16[32,32,512]{2,1,0:T(8,128)(2,1)S(1)}, u32[]{:S(2)}, u32[]{:S(2)}) async-start(bf16[32,32,512]{2,1,0:T(8,128)(2,1)} %pad_maximum_fusion), calls=%async_computation.2 | async-start | bytes 2097152 | tf_op jit(solution)/shard_map/all_to_all | solution.py:584
  189.5 19.1 %collective-permute-start.32 = (bf16[16392]{0:T(1024)(128)(2,1)S(1)}, bf16[16392]{0:T(1024)(128)(2,1)S(1)}, u32[]{:S(2)}, u32[]{:S(2)}) collective-permute-start(bf16[16392]{0:T(1024)(128)(2,1)S(1)} %pad_maximum_fusion.5), channel_id=1, source_target_pairs={{0,16},{2,18},{4,20},{6,22},{8,24},{10,26},{12,28},{14,30},{16,0},... | collective-permute-start | bytes 98360 | tf_op jit(solution)/shard_map/ppermute | solution.py:559
  193.1 22.7 %collective-permute-start.34 = (bf16[4,64,1024]{2,1,0:T(8,128)(2,1)}, bf16[4,64,1024]{2,1,0:T(8,128)(2,1)S(1)}, u32[]{:S(2)}, u32[]{:S(2)}) collective-permute-start(bf16[4,64,1024]{2,1,0:T(8,128)(2,1)} %get-tuple-element.184), channel_id=1, source_target_pairs={{0,4},{2,6},{4,0},{6,2},{8,12},{10,14},{12,8},{14,10},{16,20},{18,... | collective-permute-start | bytes 1572872 | tf_op jit(solution)/shard_map/ppermute | solution.py:559
  194.6 21.2 %collective-permute-start.35 = (bf16[4,64,1024]{2,1,0:T(8,128)(2,1)}, bf16[4,64,1024]{2,1,0:T(8,128)(2,1)S(1)}, u32[]{:S(2)}, u32[]{:S(2)}) collective-permute-start(bf16[4,64,1024]{2,1,0:T(8,128)(2,1)} %get-tuple-element.185), channel_id=1, source_target_pairs={{0,2},{2,0},{4,6},{6,4},{8,10},{10,8},{12,14},{14,12},{16,18},{18,... | collective-permute-start | bytes 1572872 | tf_op jit(solution)/shard_map/ppermute | solution.py:559
  198.8 16.9 %collective-permute-start.33 = (bf16[2,64,2048]{2,1,0:T(8,128)(2,1)}, bf16[2,64,2048]{2,1,0:T(8,128)(2,1)S(1)}, u32[]{:S(2)}, u32[]{:S(2)}) collective-permute-start(bf16[2,64,2048]{2,1,0:T(8,128)(2,1)} %get-tuple-element.191), channel_id=1, source_target_pairs={{0,8},{2,10},{4,12},{6,14},{8,0},{10,2},{12,4},{14,6},{16,24},{18,... | collective-permute-start | bytes 1572872 | tf_op jit(solution)/shard_map/ppermute | solution.py:559
  221.7 14.6 %collective-permute-start.39 = (bf16[1,64,2048]{2,1,0:T(8,128)(2,1)}, bf16[1,64,2048]{2,1,0:T(8,128)(2,1)S(1)}, u32[]{:S(2)}, u32[]{:S(2)}) collective-permute-start(bf16[1,64,2048]{2,1,0:T(8,128)(2,1)} %get-tuple-element.197), channel_id=1, source_target_pairs={{0,16},{2,18},{4,20},{6,22},{8,24},{10,26},{12,28},{14,30},{16,0},... | collective-permute-start | bytes 786440 | tf_op jit(solution)/shard_map/ppermute | solution.py:559
  221.7 18.7 %collective-permute-start.38 = (bf16[2,64,2048]{2,1,0:T(8,128)(2,1)}, bf16[2,64,2048]{2,1,0:T(8,128)(2,1)S(1)}, u32[]{:S(2)}, u32[]{:S(2)}) collective-permute-start(bf16[2,64,2048]{2,1,0:T(8,128)(2,1)} %get-tuple-element.195), channel_id=1, source_target_pairs={{0,8},{2,10},{4,12},{6,14},{8,0},{10,2},{12,4},{14,6},{16,24},{18,... | collective-permute-start | bytes 1572872 | tf_op jit(solution)/shard_map/ppermute | solution.py:559
  224.0 4.3 %collective-permute-start.36 = (bf16[28680]{0:T(1024)(128)(2,1)S(1)}, bf16[28680]{0:T(1024)(128)(2,1)S(1)}, u32[]{:S(2)}, u32[]{:S(2)}) collective-permute-start(bf16[28680]{0:T(1024)(128)(2,1)S(1)} %pad_maximum_fusion.4), channel_id=1, source_target_pairs={{0,2},{2,0},{4,6},{6,4},{8,10},{10,8},{12,14},{14,12},{16,18},{18,... | collective-permute-start | bytes 172088 | tf_op jit(solution)/shard_map/ppermute | solution.py:559
  228.5 4.8 %collective-permute-start.37 = (bf16[53256]{0:T(1024)(128)(2,1)S(1)}, bf16[53256]{0:T(1024)(128)(2,1)S(1)}, u32[]{:S(2)}, u32[]{:S(2)}) collective-permute-start(bf16[53256]{0:T(1024)(128)(2,1)S(1)} %pad_maximum_fusion.3), channel_id=1, source_target_pairs={{0,4},{2,6},{4,0},{6,2},{8,12},{10,14},{12,8},{14,10},{16,20},{18,... | collective-permute-start | bytes 319544 | tf_op jit(solution)/shard_map/ppermute | solution.py:559
  243.4 1.4 collective-permute-start.40
  244.3 14.8 %collective-permute-start.41 = (bf16[1,64,2048]{2,1,0:T(8,128)(2,1)}, bf16[1,64,2048]{2,1,0:T(8,128)(2,1)S(1)}, u32[]{:S(2)}, u32[]{:S(2)}) collective-permute-start(bf16[1,64,2048]{2,1,0:T(8,128)(2,1)} %get-tuple-element.201), channel_id=1, source_target_pairs={{0,16},{2,18},{4,20},{6,22},{8,24},{10,26},{12,28},{14,30},{16,0},... | collective-permute-start | bytes 786440 | tf_op jit(solution)/shard_map/ppermute | solution.py:559
  (55 other events, 313.6 us)

commit v2 on v1

--- a/solution.py
+++ b/solution.py
@@ -183,11 +183,12 @@
     wait_all(leaving)
 
 
-def hidden_back_kernel(grad_ref, *refs):
-    ins, outs, held, rest = split_refs(refs, [4, 3, 3])
-    slope_s, fc2_w, in_sems, out_sems = rest
-    slope0, slope1, fc2_0, fc2_1 = ins
+def hidden_back_kernel(grad_ref, mods, fc2_bias, *refs):
+    ins, outs, held, rest = split_refs(refs, [9, 5, 3])
+    slope_s, fc2_w, act0, act1a, act1b, grad_out_ref, middle_ref, in_sems, out_sems = rest
+    slope0, slope1, fc2_0, fc2_1 = ins[:4]
     pre0, pre1a, pre1b = held
+    output, mod_out = outs[3:]
     cut = pre1a.shape[1]
     pairs = []
     for side in (1, 0):
@@ -195,6 +196,7 @@
         for at in (slice(0, cut), slice(cut, 2 * cut)):
             pairs.append((fc2.at[at, :], fc2_w.at[side, at, :]))
             pairs.append((slope.at[:, at], slope_s.at[side, :, at]))
+    pairs += list(zip(ins[4:], (act0, act1a, act1b, grad_out_ref, middle_ref)))
     copies = start_copies(pairs, in_sems)
     leaving = []
     for side, pre, at, first_col in (
@@ -215,6 +217,16 @@
         if step < 2 or step == 3:
             index = {0: 1, 1: 2, 3: 0}[step]
             leaving += start_copies([(held[index], outs[index])], out_sems.at[pl.ds(index, 1)])
+    wait_all(copies[8:])
+    for at in tiles(middle_ref.shape[1], 512):
+        value = (
+            dot(act0[...], fc2_w[0, :, at])
+            + dot(act1a[...], fc2_w[1, :cut, at])
+            + dot(act1b[...], fc2_w[1, cut:, at])
+            + fc2_bias[:, at]
+        )
+        output[:, at] = (middle_ref[:, at] + mods[1:2, at] * value).astype(bf16)
+        mod_out[0:1, at] = jnp.sum(grad_out_ref[:, at].astype(f32) * value, axis=0, keepdims=True)
     wait_all(leaving)
 
 
@@ -310,25 +322,6 @@
     wait_all(leaving)
 
 
-def branch_kernel(mods, fc2_bias, *refs):
-    ins, outs, got, rest = split_refs(refs, [7, 2, 7])
-    output, mod_out = outs
-    (in_sems,) = rest
-    copies = start_copies(list(zip(ins, got)), in_sems)
-    act0, fc2_0, act1a, act1b, fc2_1, grad_out_ref, middle_ref = got
-    wait_all(copies)
-    cut = act1a.shape[1]
-    for at in tiles(middle_ref.shape[1], 512):
-        value = (
-            dot(act0[...], fc2_0[:, at])
-            + dot(act1a[...], fc2_1[:cut, at])
-            + dot(act1b[...], fc2_1[cut:, at])
-            + fc2_bias[:, at]
-        )
-        output[:, at] = (middle_ref[:, at] + mods[1:2, at] * value).astype(bf16)
-        mod_out[0:1, at] = jnp.sum(grad_out_ref[:, at].astype(f32) * value, axis=0, keepdims=True)
-
-
 def input_back_kernel(mods, *refs):
     ins, outs, got, rest = split_refs(refs, [11, 2, 11])
     tokens_grad, mod_out = outs
@@ -336,10 +329,11 @@
     copies = start_copies(list(zip(ins, got)), in_sems)
     qkv_grad0, qkv1a, qkv1b, x_ref, middle_grad = got[:5]
     weights = got[5:]
-    wait_all(copies)
     width = x_ref.shape[1]
     half, cut = width // 2, qkv1a.shape[1]
+    wait_all(copies[:4])
     normed, spread = normalize(x_ref[...].astype(f32))
+    wait_all(copies[4:])
     for at in tiles(width, 512):
         total = jnp.zeros((x_ref.shape[0], at.stop - at.start), f32)
         for part in range(3):
@@ -795,18 +789,24 @@
     fc2_came = travel(fc2_sent)
 
     pre_kept = [array(row_len, hidden)] + [array(row_len, hidden // 2)] * 2
-    pre0, *pre1 = local_call(
+    branch_ins = [act0, *act1, grad_out, middle]
+    pre0, *pre1, output, branch_mods = local_call(
         hidden_back_kernel,
         56,
-        pre_kept,
+        pre_kept + [array(row_len, width), array(1, width, kind=f32)],
         scratch(pre_kept)
-        + [vmem((2, row_len, hidden), bf16), vmem((2, hidden, width), bf16), dma((8,)), dma((3,))],
-        "vhhhh",
+        + [vmem((2, row_len, hidden), bf16), vmem((2, hidden, width), bf16)]
+        + scratch(branch_ins)
+        + [dma((13,)), dma((3,))],
+        "vvv" + "h" * 9,
         after(grad_branch, fc2_sent, h1_far, h2_far, mixed_far),
+        mods,
+        fc2_shift[None],
         slope0,
         slope1,
         *fc2_w,
-        out_kind="h",
+        *branch_ins,
+        out_kind="hhhvv",
     )
     _, fc1_right, fc1_rest, fc1_sent = scatter_start(
         source(h2, h2_far, pre0, pre1)
@@ -859,28 +859,17 @@
     fc1_own, fc1_sent = scatter_second(fc1_rest, after(fc1_came, attn_grad))
     ready = after((qkv1a, qkv1b, attn_grad), fc2_came, fc1_sent)
     fc1_came = travel(fc1_sent[::-1])[::-1]
+    fc2_own, fc2_sent = scatter_more(2, fc2_own, fc2_came)
+    fc2_came = (flip(fc2_sent, 2),)
     qkv_left, qkv_right, qkv_rest, qkv_sent = scatter_start(
-        source(h1, h1_far, qkv_grad0, ready[:2]),
+        after(source(h1, h1_far, qkv_grad0, ready[:2]), fc2_sent),
         (attn_grad, swap(ready[2]), mixed0, mixed_far),
     )
     qkv_came = travel(qkv_sent)
-    fc2_own, fc2_sent = scatter_more(2, fc2_own, after(fc2_came, qkv_sent))
-    fc2_came = (flip(fc2_sent, 2),)
-    branch_ins = [after(act0, fc1_came, fc2_sent), fc2_w[0], *act1, fc2_w[1], grad_out, middle]
-    output, branch_mods = local_call(
-        branch_kernel,
-        56,
-        [array(row_len, width), array(1, width, kind=f32)],
-        scratch(branch_ins) + [dma((7,))],
-        "vv" + "h" * 7,
-        mods,
-        fc2_shift[None],
-        *branch_ins,
-    )
-    fc2_own, fc2_sent = scatter_more(3, fc2_own, after(fc2_came, output))
+    fc2_own, fc2_sent = scatter_more(3, fc2_own, after(fc2_came, qkv_sent))
     fc2_came = (flip(fc2_sent, 3),)
     end_ins = [
-        after(qkv_grad0, fc2_sent),
+        after(qkv_grad0, fc1_came, fc2_sent),
         qkv1a,
         qkv1b,
         resident,
@@ -929,7 +918,7 @@
     gathered, bias_sum = double(row_grads.reshape(6 * width), bias_sum, 2)
     returned = exchange(
         jnp.concatenate(
-            [to_target(values) for values in after((output, tokens_grad), row_grads)], axis=1
+            [to_target(values) for values in after((output, tokens_grad))], axis=1
         )
     )
     qkv_own, qkv_sent = scatter_second(

time: 265 us -> 258 us (0.974)
  Pallas kernels: 107 us -> 101 us
    pallas_call x17 -> x16, Pallas kernels: 107 us -> 101 us  [local_call(): pl.pallas_call(kernel, out_shape=outs, in_specs=[places[kind] for kind in...]
    ppermute x22, waiting for transfers between devices: 43.9 us -> 39.9 us  [flip(): lax.ppermute(values, 'dp', [(i, i ^ 1 << bit) for i in range(groups)])]
    ppermute x20, waiting for transfers between devices: 4.43 us -> 7.14 us  [swap(): return lax.ppermute(values, 'mp', [(0, 1), (1, 0)])]
  transfers between devices with their start and end apart: 45 -> 45, of which waited for: 16 -> 16; matrix products, arithmetic and copies ran while one was open for 14% -> 15% of each run, Pallas kernels for 38% -> 37%
where the time goes in v2:
time: 258 us; the launch traced here: 254 us
  Pallas kernels  101 us (39%)
  waiting for transfers between devices  58.1 us (23%)
  starting transfers between devices  46.5 us (18%)
  local copies, waits for them, and re-layouts  29.7 us (12%)
  other arithmetic  12.6 us (5%)
  matrix products  3.75 us (1%)
    pallas_call x16, Pallas kernels, local_call(): pl.pallas_call(kernel, out_shape=outs, in_specs=[places[kind] for kind in...  101 us
    ppermute x22, waiting for transfers between devices, flip(): lax.ppermute(values, 'dp', [(i, i ^ 1 << bit) for i in range(groups)])  39.9 us
    ppermute x22, starting transfers between devices, flip(): lax.ppermute(values, 'dp', [(i, i ^ 1 << bit) for i in range(groups)])  28.1 us
    all_to_all x3, starting transfers between devices, exchange(): lax.all_to_all(values, ('dp', 'mp'), split_axis=0, concat_axis=0, tiled=T...  13.7 us
    all_to_all x3, waiting for transfers between devices, exchange(): lax.all_to_all(values, ('dp', 'mp'), split_axis=0, concat_axis=0, tiled=T...  11.1 us
    unnamed x133, local copies, waits for them, and re-layouts  9.82 us
    ppermute x20, waiting for transfers between devices, swap(): return lax.ppermute(values, 'mp', [(0, 1), (1, 0)])  7.14 us
  transfers between devices with their start and end apart: 45, of which 16 were waited for; matrix products, arithmetic and copies ran while one was open for 15% of the time, Pallas kernels for 37%

profile of v2, /device:TPU:0, one launch (start us, length us, event | category | flops | bytes accessed | tf_op | source)
XLA Modules:
  0.0 253.8 jit_solution(4951878565468540349)
XLA Ops:
  5.3 7.1 %all-to-all-start = ((bf16[32,24,512]{2,1,0:T(8,128)(2,1)}), bf16[32,24,512]{2,1,0:T(8,128)(2,1)}, u32[]{:S(2)}, u32[]{:S(2)}) async-start(bf16[32,24,512]{2,1,0:T(8,128)(2,1)} %pad_maximum_fusion.1), calls=%async_computation | async-start | bytes 1572864 | tf_op jit(solution)/shard_map/all_to_all | solution.py:578
  12.8 2.1 slice_bitcast_fusion
  17.3 1.9 copy.64
  21.9 11.1 %all-to-all-done.arrived = bf16[32,24,512]{2,1,0:T(8,128)(2,1)} async-done(((bf16[32,24,512]{2,1,0:T(8,128)(2,1)}), bf16[32,24,512]{2,1,0:T(8,128)(2,1)}, u32[]{:S(2)}, u32[]{:S(2)}) %all-to-all-start) | async-done | bytes 786464 | tf_op jit(solution)/shard_map/all_to_all | solution.py:578
  33.0 3.9 %all-to-all-start.1 = ((bf16[32,16,512]{2,1,0:T(8,128)(2,1)}), bf16[32,16,512]{2,1,0:T(8,128)(2,1)}, u32[]{:S(2)}, u32[]{:S(2)}) async-start(bf16[32,16,512]{2,1,0:T(8,128)(2,1)} %bitcast.135), calls=%async_computation.1 | async-start | bytes 1048576 | tf_op jit(solution)/shard_map/all_to_all | solution.py:578
  38.2 17.2 %shard_map.281 = (bf16[256,1024]{1,0:T(8,128)(2,1)}, bf16[2,256,512]{2,1,0:T(8,128)(2,1)}, bf16[2,256,512]{2,1,0:T(8,128)(2,1)}, bf16[2,256,512]{2,1,0:T(8,128)(...) custom-call(bf16[32,24,512]{2,1,0:T(8,128)(2,1)} %all-to-all-done.ar, ...), custom_call_target="tpu_custom_call" | custom-call | flops 1 | bytes 1 | tf_op jit(solution)/shard_map/pallas_call | solution.py:486
  55.5 1.7 copy.65
  60.3 1.7 collective-permute-done.7.refs_3_.refs_2_
  62.8 5.7 %shard_map.282 = (f32[1,1024]{1,0:T(1,128)}, f32[1,2048]{1,0:T(1,128)}, bf16[16,64,512]{2,1,0:T(8,128)(2,1)}, bf16[8,64,1024]{2,1,0:T(8,128)(2,1)}, bf16[8,64,1024]{2,1,0:T(8,128)(2,1)}) custom-call(s32[4]{0:T(128)} %pad_add_fusion.bit_ref, bf16[256,1024]{1,0:T(8,128)(2,1)} %copy-done.6, bf16[256,1024]{1,0:T(8,128)(2,1)} %copy-done.39, ...), custom_call_target="tpu_custom_call" | custom-call | flops 1 | bytes 1 | tf_op jit(solution)/shard_map/pallas_call | solution.py:486
  68.6 1.8 collective-permute-start.13
  70.3 1.5 collective-permute-start.14
  72.4 10.1 %shard_map.283 = (bf16[256,2048]{1,0:T(8,128)(2,1)}, bf16[256,1024]{1,0:T(8,128)(2,1)}, bf16[256,1024]{1,0:T(8,128)(2,1)}, bf16[256,1024]{1,0:T(8,128)(2,1)}, f32[1,1024]{1,0:T(1,128)}) custom-call(bf16[256,1024]{1,0:T(8,128)(2,1)} %copy-done.6, f32[6,1024]{1,0:T(8,128)} %get-tuple-element.112.mods, f32[1,1024]{1,0:T(1,128)} %broadcast_select_fusion.5.fc2_bias, ...), custom_call_target="tpu_custom_call" | custom-call | flops 1 | bytes 1 | tf_op jit(solution)/shard_map/pallas_call | solution.py:486
  83.1 1.6 collective-permute-done.15.refs_3_.refs_2_
  86.3 5.7 %shard_map.284 = (f32[1,1024]{1,0:T(1,128)}, f32[1,2048]{1,0:T(1,128)}, bf16[16,64,512]{2,1,0:T(8,128)(2,1)}, bf16[8,64,1024]{2,1,0:T(8,128)(2,1)}, bf16[8,64,1024]{2,1,0:T(8,128)(2,1)}) custom-call(s32[4]{0:T(128)} %pad_add_fusion.bit_ref, bf16[256,1024]{1,0:T(8,128)(2,1)} %get-tuple-element.121.refs_0_, bf16[256,1024]{1,0:T(8,128)(2,1)} %collective-permute-done.10.refs_1_, ...), custom_call_target="tpu_custom_call" | custom-call | flops 1 | bytes 1 | tf_op jit(solution)/shard_map/pallas_call | solution.py:486
  94.3 1.8 collective-permute-done.14.refs_5_
  97.0 5.4 %shard_map.285 = (bf16[4,64,1024]{2,1,0:T(8,128)(2,1)}, bf16[4,64,1024]{2,1,0:T(8,128)(2,1)}, bf16[4,64,2048]{2,1,0:T(8,128)(2,1)}) custom-call(s32[4]{0:T(128)} %pad_add_fusion.bit_ref, bf16[16,64,512]{2,1,0:T(8,128)(2,1)} %get-tuple-element.129.refs_0_, bf16[256,2048]{1,0:T(8,128)(2,1)} %get-tuple-element.114.refs_2_.refs_4_.refs_1_, ...), custom_call_target="tpu_custom_call" | custom-call | flops 3000000000 | bytes 1 | tf_op jit(solution)/shard_map/pallas_call | solution.py:486
  102.5 2.0 collective-permute-start.21
  104.8 16.1 %shard_map.286 = (f32[256,1024]{1,0:T(8,128)}, bf16[256,1024]{1,0:T(8,128)(2,1)}, bf16[256,1536]{1,0:T(8,128)(2,1)}, bf16[256,768]{1,0:T(8,128)(2,1)}, bf16[256,768]{1,0:T(8,128)(2,1)}, /*index=5*/f32[4,1024]{1,0:T(4,128)}) custom-call(f32[6,1024]{1,0:T(8,128)} %get-tuple-element.112.mods, f32[2,512]{1,0:T(2,128)} %pad_maximum_fusion.10.mult, ...), custom_call_target="tpu_custom_call" | custom-call | flops 1 | bytes 1 | tf_op jit(solution)/shard_map/pallas_call | solution.py:486
  122.3 5.5 %shard_map.287 = (bf16[4,64,1024]{2,1,0:T(8,128)(2,1)}, bf16[4,64,1024]{2,1,0:T(8,128)(2,1)}, bf16[4,64,2048]{2,1,0:T(8,128)(2,1)}) custom-call(s32[4]{0:T(128)} %pad_add_fusion.bit_ref, bf16[16,64,512]{2,1,0:T(8,128)(2,1)} %get-tuple-element.147.refs_0_, bf16[256,2048]{1,0:T(8,128)(2,1)} %get-tuple-element.138.refs_2_.refs_0_.refs_1_, ...), custom_call_target="tpu_custom_call" | custom-call | flops 1 | bytes 1 | tf_op jit(solution)/shard_map/pallas_call | solution.py:486
  127.8 1.6 collective-permute-done.21.refs_0_
  131.1 2.7 %shard_map.288 = (bf16[2,64,2048]{2,1,0:T(8,128)(2,1)}, bf16[2,64,2048]{2,1,0:T(8,128)(2,1)}) custom-call(s32[4]{0:T(128)} %pad_add_fusion.bit_ref, bf16[4,64,2048]{2,1,0:T(8,128)(2,1)} %get-tuple-element.153.own, bf16[4,64,1024]{2,1,0:T(8,128)(2,1)} %copy-done.24, bf16[4,64,1024]{2,1,0:T(8,128)(2,1)} %copy-done.25), custom_call_target="tpu_custom_call" | custom-call | flops 1 | bytes 1 | tf_op jit(solution)/shard_map/pallas_call | solution.py:486
  133.8 1.5 collective-permute-start.23
  135.5 1.5 collective-permute-start.19
  137.5 1.9 collective-permute-done.25.refs_4_
  140.4 6.9 %shard_map.289 = (f32[1,1024]{1,0:T(1,128)}, f32[1,1024]{1,0:T(1,128)}, f32[1,1536]{1,0:T(1,128)}, f32[1,512]{1,0:T(1,128)}, bf16[16,64,512]{2,1,0:T(8,128)(2,1)...) custom-call(s32[4]{0:T(128)} %pad_add_fusion.bit_ref, ...), custom_call_target="tpu_custom_call" | custom-call | flops 1 | bytes 1 | tf_op jit(solution)/shard_map/pallas_call | solution.py:486
  147.2 1.5 collective-permute-start.29
  149.6 2.2 shard_map.290
  153.2 2.5 collective-permute-start.31
  155.7 7.5 %shard_map.291 = (bf16[256,1024]{1,0:T(8,128)(2,1)}, f32[2,1024]{1,0:T(2,128)}) custom-call(f32[6,1024]{1,0:T(8,128)} %get-tuple-element.112.mods, bf16[256,1536]{1,0:T(8,128)(2,1)} %get-tuple-element.171.refs_2_.refs_0_, bf16[256,768]{1,0:T(8,128)(2,1)} %get-tuple-element.158.refs_1_, bf16[256,768]{1,0:T(8,128)(2,1)} %get-tuple-element.159.refs_2_, ...), custom_call_target="tpu_custom_call" | custom-call | flops 1 | bytes 1 | tf_op jit(solution)/shard_map/pallas_call | solution.py:486
  166.6 1.5 collective-permute-start.28
  168.6 1.4 reshape.359
  171.2 2.7 %all-to-all-start.2 = ((bf16[32,32,512]{2,1,0:T(8,128)(2,1)}), bf16[32,32,512]{2,1,0:T(8,128)(2,1)S(1)}, u32[]{:S(2)}, u32[]{:S(2)}) async-start(bf16[32,32,512]{2,1,0:T(8,128)(2,1)} %pad_maximum_fusion), calls=%async_computation.2 | async-start | bytes 2097152 | tf_op jit(solution)/shard_map/all_to_all | solution.py:578
  176.1 6.5 %shard_map.292 = (bf16[4,64,1024]{2,1,0:T(8,128)(2,1)}, bf16[4,64,1024]{2,1,0:T(8,128)(2,1)}, bf16[4,64,2048]{2,1,0:T(8,128)(2,1)}) custom-call(s32[4]{0:T(128)} %pad_add_fusion.bit_ref, bf16[16,64,512]{2,1,0:T(8,128)(2,1)} %get-tuple-element.184.refs_0_, bf16[16,64,512]{2,1,0:T(8,128)(2,1)} %get-tuple-element.185.refs_1_, ...), custom_call_target="tpu_custom_call" | custom-call | flops 1 | bytes 1 | tf_op jit(solution)/shard_map/pallas_call | solution.py:486
  182.6 2.7 %collective-permute-start.32 = (bf16[16392]{0:T(1024)(128)(2,1)S(1)}, bf16[16392]{0:T(1024)(128)(2,1)S(1)}, u32[]{:S(2)}, u32[]{:S(2)}) collective-permute-start(bf16[16392]{0:T(1024)(128)(2,1)S(1)} %pad_maximum_fusion.5), channel_id=1, source_target_pairs={{0,16},{2,18},{4,20},{6,22},{8,24},{10,26},{12,28},{14,30},{16,0},... | collective-permute-start | bytes 98360 | tf_op jit(solution)/shard_map/ppermute | solution.py:553
  186.1 1.5 collective-permute-start.34
  187.6 1.5 collective-permute-start.35
  189.1 2.7 %shard_map.293 = (bf16[2,64,2048]{2,1,0:T(8,128)(2,1)}, bf16[2,64,2048]{2,1,0:T(8,128)(2,1)}) custom-call(s32[4]{0:T(128)} %pad_add_fusion.bit_ref, bf16[4,64,2048]{2,1,0:T(8,128)(2,1)} %get-tuple-element.191.own, bf16[4,64,1024]{2,1,0:T(8,128)(2,1)} %copy-done.20, bf16[4,64,1024]{2,1,0:T(8,128)(2,1)} %copy-done.21), custom_call_target="tpu_custom_call" | custom-call | flops 1 | bytes 1 | tf_op jit(solution)/shard_map/pallas_call | solution.py:486
  191.8 1.5 collective-permute-start.33
  193.3 8.3 %collective-permute-done.32 = bf16[16392]{0:T(1024)(128)(2,1)S(1)} collective-permute-done((bf16[16392]{0:T(1024)(128)(2,1)S(1)}, bf16[16392]{0:T(1024)(128)(2,1)S(1)}, u32[]{:S(2)}, u32[]{:S(2)}) %collective-permute-start.32) | collective-permute-done | bytes 32816 | tf_op jit(solution)/shard_map/ppermute | solution.py:553
  201.8 7.0 %collective-permute-done.33.refs_0_ = bf16[2,64,2048]{2,1,0:T(8,128)(2,1)S(1)} collective-permute-done((bf16[2,64,2048]{2,1,0:T(8,128)(2,1)}, bf16[2,64,2048]{2,1,0:T(8,128)(2,1)S(1)}, u32[]{:S(2)}, u32[]{:S(2)}) %collective-permute-start.33) | collective-permute-done | bytes 524320 | tf_op jit(solution)/shard_map/ppermute | solution.py:553
  209.8 2.7 %shard_map.294 = (bf16[2,64,2048]{2,1,0:T(8,128)(2,1)}, bf16[2,64,2048]{2,1,0:T(8,128)(2,1)}) custom-call(s32[4]{0:T(128)} %pad_add_fusion.bit_ref, bf16[4,64,2048]{2,1,0:T(8,128)(2,1)} %get-tuple-element.196.own, bf16[4,64,1024]{2,1,0:T(8,128)(2,1)} %copy-done.27, bf16[4,64,1024]{2,1,0:T(8,128)(2,1)} %copy-done.28), custom_call_target="tpu_custom_call" | custom-call | flops 1 | bytes 1 | tf_op jit(solution)/shard_map/pallas_call | solution.py:486
  212.4 2.2 shard_map.295
  214.6 2.3 collective-permute-start.38
  219.7 1.4 collective-permute-done.36
  222.4 3.8 %collective-permute-done.37 = bf16[53256]{0:T(1024)(128)(2,1)S(1)} collective-permute-done((bf16[53256]{0:T(1024)(128)(2,1)S(1)}, bf16[53256]{0:T(1024)(128)(2,1)S(1)}, u32[]{:S(2)}, u32[]{:S(2)}) %collective-permute-start.37) | collective-permute-done | bytes 106544 | tf_op jit(solution)/shard_map/ppermute | solution.py:553
  229.2 4.1 %collective-permute-done.38.refs_0_ = bf16[2,64,2048]{2,1,0:T(8,128)(2,1)S(1)} collective-permute-done((bf16[2,64,2048]{2,1,0:T(8,128)(2,1)}, bf16[2,64,2048]{2,1,0:T(8,128)(2,1)S(1)}, u32[]{:S(2)}, u32[]{:S(2)}) %collective-permute-start.38) | collective-permute-done | bytes 524320 | tf_op jit(solution)/shard_map/ppermute | solution.py:553
  234.1 2.2 shard_map.296
  241.6 10.4 %collective-permute-done.41 = bf16[1,64,2048]{2,1,0:T(8,128)(2,1)S(1)} collective-permute-done((bf16[1,64,2048]{2,1,0:T(8,128)(2,1)}, bf16[1,64,2048]{2,1,0:T(8,128)(2,1)S(1)}, u32[]{:S(2)}, u32[]{:S(2)}) %collective-permute-start.41) | collective-permute-done | bytes 262176 | tf_op jit(solution)/shard_map/ppermute | solution.py:553
  (303 shorter events, 51.8 us)
Async XLA Ops:
  0.7 37.5 %collective-permute-start.5 = (bf16[1024,2048]{1,0:T(8,128)(2,1)}, bf16[1024,2048]{1,0:T(8,128)(2,1)}, u32[]{:S(2)}, u32[]{:S(2)}) collective-permute-start(bf16[1024,2048]{1,0:T(8,128)(2,1)} %refs_1_.1), channel_id=1, source_target_pairs={{0,1},{1,0},{2,3},{3,2},{4,5},{5,4},{6,7},{7,6},{8,9},{9,8},{10,11... | collective-permute-start | bytes 12582920 | tf_op jit(solution)/shard_map/ppermute | solution.py:550
  5.3 27.7 %all-to-all-start = ((bf16[32,24,512]{2,1,0:T(8,128)(2,1)}), bf16[32,24,512]{2,1,0:T(8,128)(2,1)}, u32[]{:S(2)}, u32[]{:S(2)}) async-start(bf16[32,24,512]{2,1,0:T(8,128)(2,1)} %pad_maximum_fusion.1), calls=%async_computation | async-start | bytes 1572864 | tf_op jit(solution)/shard_map/all_to_all | solution.py:578
  12.6 6.6 %collective-permute-start = (f32[7176]{0:T(1024)S(1)}, f32[7176]{0:T(1024)S(1)}, u32[]{:S(2)}, u32[]{:S(2)}) collective-permute-start(f32[7176]{0:T(1024)S(1)} %concatenate.118), channel_id=1, source_target_pairs={{0,1},{1,0},{2,3},{3,2},{4,5},{5,4},{6,7},{7,6},{8,9},{9,8},{10,11... | collective-permute-start | bytes 86120 | tf_op jit(solution)/shard_map/ppermute | solution.py:550
  14.9 23.3 %copy-start.2 = (bf16[1024,512]{1,0:T(8,128)(2,1)}, bf16[1024,512]{1,0:T(8,128)(2,1)S(1)}, u32[]{:S(2)}) copy-start(bf16[1024,512]{1,0:T(8,128)(2,1)S(1)} %get-tuple-element.270.refs_2_.refs_7_) | copy-start | bytes 3145732
  14.9 23.3 %copy-start.3 = (bf16[1024,512]{1,0:T(8,128)(2,1)}, bf16[1024,512]{1,0:T(8,128)(2,1)S(1)}, u32[]{:S(2)}) copy-start(bf16[1024,512]{1,0:T(8,128)(2,1)S(1)} %get-tuple-element.271.refs_0_.refs_5_) | copy-start | bytes 3145732
  14.9 23.3 %copy-start.4 = (bf16[1024,512]{1,0:T(8,128)(2,1)}, bf16[1024,512]{1,0:T(8,128)(2,1)S(1)}, u32[]{:S(2)}) copy-start(bf16[1024,512]{1,0:T(8,128)(2,1)S(1)} %get-tuple-element.272.refs_1_.refs_6_) | copy-start | bytes 3145732
  14.9 6.1 %collective-permute-start.1 = (bf16[1024,512]{1,0:T(8,128)(2,1)S(1)}, bf16[1024,512]{1,0:T(8,128)(2,1)}, u32[]{:S(2)}, u32[]{:S(2)}) collective-permute-start(bf16[1024,512]{1,0:T(8,128)(2,1)S(1)} %get-tuple-element.271.refs_0_.refs_5_), channel_id=1, source_target_pairs={{0,1},{1,0},{2,3},{3,2},{4,5},{5,4},{6,7},{7,6},{8,9},{9,8},{10,11... | collective-permute-start | bytes 3145736 | tf_op jit(solution)/shard_map/ppermute | solution.py:550
  15.3 22.9 %collective-permute-start.2 = (bf16[1024,512]{1,0:T(8,128)(2,1)S(1)}, bf16[1024,512]{1,0:T(8,128)(2,1)}, u32[]{:S(2)}, u32[]{:S(2)}) collective-permute-start(bf16[1024,512]{1,0:T(8,128)(2,1)S(1)} %get-tuple-element.272.refs_1_.refs_6_), channel_id=1, source_target_pairs={{0,1},{1,0},{2,3},{3,2},{4,5},{5,4},{6,7},{7,6},{8,9},{9,8},{10,11... | collective-permute-start | bytes 3145736 | tf_op jit(solution)/shard_map/ppermute | solution.py:550
  15.5 56.9 %collective-permute-start.12 = (bf16[2048,1024]{1,0:T(8,128)(2,1)}, bf16[2048,1024]{1,0:T(8,128)(2,1)}, u32[]{:S(2)}, u32[]{:S(2)}) collective-permute-start(bf16[2048,1024]{1,0:T(8,128)(2,1)} %refs_2_.1), channel_id=1, source_target_pairs={{0,1},{1,0},{2,3},{3,2},{4,5},{5,4},{6,7},{7,6},{8,9},{9,8},{10,11... | collective-permute-start | bytes 12582920 | tf_op jit(solution)/shard_map/ppermute | solution.py:550
  19.2 19.0 %collective-permute-start.3 = (bf16[1024,512]{1,0:T(8,128)(2,1)S(1)}, bf16[1024,512]{1,0:T(8,128)(2,1)}, u32[]{:S(2)}, u32[]{:S(2)}) collective-permute-start(bf16[1024,512]{1,0:T(8,128)(2,1)S(1)} %get-tuple-element.270.refs_2_.refs_7_), channel_id=1, source_target_pairs={{0,1},{1,0},{2,3},{3,2},{4,5},{5,4},{6,7},{7,6},{8,9},{9,8},{10,11... | collective-permute-start | bytes 3145736 | tf_op jit(solution)/shard_map/ppermute | solution.py:550
  21.0 17.2 %collective-permute-start.4 = (bf16[512,1024]{1,0:T(8,128)(2,1)}, bf16[512,1024]{1,0:T(8,128)(2,1)}, u32[]{:S(2)}, u32[]{:S(2)}) collective-permute-start(bf16[512,1024]{1,0:T(8,128)(2,1)} %refs_8_.3), channel_id=1, source_target_pairs={{0,1},{1,0},{2,3},{3,2},{4,5},{5,4},{6,7},{7,6},{8,9},{9,8},{10,11... | collective-permute-start | bytes 3145736 | tf_op jit(solution)/shard_map/ppermute | solution.py:550
  33.0 22.5 %all-to-all-start.1 = ((bf16[32,16,512]{2,1,0:T(8,128)(2,1)}), bf16[32,16,512]{2,1,0:T(8,128)(2,1)}, u32[]{:S(2)}, u32[]{:S(2)}) async-start(bf16[32,16,512]{2,1,0:T(8,128)(2,1)} %bitcast.135), calls=%async_computation.1 | async-start | bytes 1048576 | tf_op jit(solution)/shard_map/all_to_all | solution.py:578
  58.2 2.0 collective-permute-start.6
  58.4 3.6 %collective-permute-start.7 = (bf16[256,1024]{1,0:T(8,128)(2,1)S(1)}, bf16[256,1024]{1,0:T(8,128)(2,1)S(1)}, u32[]{:S(2)}, u32[]{:S(2)}) collective-permute-start(bf16[256,1024]{1,0:T(8,128)(2,1)S(1)} %copy-done.22), channel_id=1, source_target_pairs={{0,1},{1,0},{2,3},{3,2},{4,5},{5,4},{6,7},{7,6},{8,9},{9,8},{10,11... | collective-permute-start | bytes 1572872 | tf_op jit(solution)/shard_map/ppermute | solution.py:550
  58.7 4.0 %collective-permute-start.8 = (bf16[256,1024]{1,0:T(8,128)(2,1)}, bf16[256,1024]{1,0:T(8,128)(2,1)}, u32[]{:S(2)}, u32[]{:S(2)}) collective-permute-start(bf16[256,1024]{1,0:T(8,128)(2,1)} %get-tuple-element.117.refs_6_), channel_id=1, source_target_pairs={{0,1},{1,0},{2,3},{3,2},{4,5},{5,4},{6,7},{7,6},{8,9},{9,8},{10,11... | collective-permute-start | bytes 1572872 | tf_op jit(solution)/shard_map/ppermute | solution.py:550
  58.9 11.4 %collective-permute-start.11 = (bf16[256,512]{1,0:T(8,128)(2,1)}, bf16[256,512]{1,0:T(8,128)(2,1)S(1)}, u32[]{:S(2)}, u32[]{:S(2)}) collective-permute-start(bf16[256,512]{1,0:T(8,128)(2,1)} %get-tuple-element.122), channel_id=1, source_target_pairs={{0,1},{1,0},{2,3},{3,2},{4,5},{5,4},{6,7},{7,6},{8,9},{9,8},{10,11... | collective-permute-start | bytes 786440 | tf_op jit(solution)/shard_map/ppermute | solution.py:550
  60.1 12.3 %collective-permute-start.10 = (bf16[256,1024]{1,0:T(8,128)(2,1)S(1)}, bf16[256,1024]{1,0:T(8,128)(2,1)}, u32[]{:S(2)}, u32[]{:S(2)}) collective-permute-start(bf16[256,1024]{1,0:T(8,128)(2,1)S(1)} %copy-done.37), channel_id=1, source_target_pairs={{0,1},{1,0},{2,3},{3,2},{4,5},{5,4},{6,7},{7,6},{8,9},{9,8},{10,11... | collective-permute-start | bytes 1572872 | tf_op jit(solution)/shard_map/ppermute | solution.py:550
  62.0 10.4 %collective-permute-start.9 = (bf16[256,1024]{1,0:T(8,128)(2,1)S(1)}, bf16[256,1024]{1,0:T(8,128)(2,1)S(1)}, u32[]{:S(2)}, u32[]{:S(2)}) collective-permute-start(bf16[256,1024]{1,0:T(8,128)(2,1)S(1)} %copy-done.18), channel_id=1, source_target_pairs={{0,1},{1,0},{2,3},{3,2},{4,5},{5,4},{6,7},{7,6},{8,9},{9,8},{10,11... | collective-permute-start | bytes 1572872 | tf_op jit(solution)/shard_map/ppermute | solution.py:550
  68.6 25.7 %collective-permute-start.13 = (bf16[8,64,1024]{2,1,0:T(8,128)(2,1)}, bf16[8,64,1024]{2,1,0:T(8,128)(2,1)S(1)}, u32[]{:S(2)}, u32[]{:S(2)}) collective-permute-start(bf16[8,64,1024]{2,1,0:T(8,128)(2,1)} %get-tuple-element.118), channel_id=1, source_target_pairs={{0,2},{2,0},{4,6},{6,4},{8,10},{10,8},{12,14},{14,12},{16,18},{18,... | collective-permute-start | bytes 3145736 | tf_op jit(solution)/shard_map/ppermute | solution.py:553
  70.3 25.7 %collective-permute-start.14 = (bf16[8,64,1024]{2,1,0:T(8,128)(2,1)}, bf16[8,64,1024]{2,1,0:T(8,128)(2,1)S(1)}, u32[]{:S(2)}, u32[]{:S(2)}) collective-permute-start(bf16[8,64,1024]{2,1,0:T(8,128)(2,1)} %get-tuple-element.119), channel_id=1, source_target_pairs={{0,4},{2,6},{4,0},{6,2},{8,12},{10,14},{12,8},{14,10},{16,20},{18,... | collective-permute-start | bytes 3145736 | tf_op jit(solution)/shard_map/ppermute | solution.py:553
  82.5 2.2 collective-permute-start.15
  82.6 2.9 %collective-permute-start.16 = (bf16[256,1024]{1,0:T(8,128)(2,1)}, bf16[256,1024]{1,0:T(8,128)(2,1)S(1)}, u32[]{:S(2)}, u32[]{:S(2)}) collective-permute-start(bf16[256,1024]{1,0:T(8,128)(2,1)} %get-tuple-element.131.refs_3_), channel_id=1, source_target_pairs={{0,1},{1,0},{2,3},{3,2},{4,5},{5,4},{6,7},{7,6},{8,9},{9,8},{10,11... | collective-permute-start | bytes 1572872 | tf_op jit(solution)/shard_map/ppermute | solution.py:550
  92.0 28.9 %collective-permute-start.17 = (bf16[8,64,1024]{2,1,0:T(8,128)(2,1)}, bf16[8,64,1024]{2,1,0:T(8,128)(2,1)S(1)}, u32[]{:S(2)}, u32[]{:S(2)}) collective-permute-start(bf16[8,64,1024]{2,1,0:T(8,128)(2,1)} %get-tuple-element.132), channel_id=1, source_target_pairs={{0,2},{2,0},{4,6},{6,4},{8,10},{10,8},{12,14},{14,12},{16,18},{18,... | collective-permute-start | bytes 3145736 | tf_op jit(solution)/shard_map/ppermute | solution.py:553
  92.6 28.3 %collective-permute-start.18 = (bf16[8,64,1024]{2,1,0:T(8,128)(2,1)}, bf16[8,64,1024]{2,1,0:T(8,128)(2,1)S(1)}, u32[]{:S(2)}, u32[]{:S(2)}) collective-permute-start(bf16[8,64,1024]{2,1,0:T(8,128)(2,1)} %get-tuple-element.133), channel_id=1, source_target_pairs={{0,4},{2,6},{4,0},{6,2},{8,12},{10,14},{12,8},{14,10},{16,20},{18,... | collective-permute-start | bytes 3145736 | tf_op jit(solution)/shard_map/ppermute | solution.py:553
  102.5 26.9 %collective-permute-start.21 = (bf16[4,64,1024]{2,1,0:T(8,128)(2,1)}, bf16[4,64,1024]{2,1,0:T(8,128)(2,1)S(1)}, u32[]{:S(2)}, u32[]{:S(2)}) collective-permute-start(bf16[4,64,1024]{2,1,0:T(8,128)(2,1)} %get-tuple-element.136), channel_id=1, source_target_pairs={{0,4},{2,6},{4,0},{6,2},{8,12},{10,14},{12,8},{14,10},{16,20},{18,... | collective-permute-start | bytes 1572872 | tf_op jit(solution)/shard_map/ppermute | solution.py:553
  104.5 24.9 %collective-permute-start.22 = (bf16[4,64,1024]{2,1,0:T(8,128)(2,1)}, bf16[4,64,1024]{2,1,0:T(8,128)(2,1)S(1)}, u32[]{:S(2)}, u32[]{:S(2)}) collective-permute-start(bf16[4,64,1024]{2,1,0:T(8,128)(2,1)} %get-tuple-element.137), channel_id=1, source_target_pairs={{0,2},{2,0},{4,6},{6,4},{8,10},{10,8},{12,14},{14,12},{16,18},{18,... | collective-permute-start | bytes 1572872 | tf_op jit(solution)/shard_map/ppermute | solution.py:553
  129.4 8.1 %collective-permute-start.24 = (bf16[256,768]{1,0:T(8,128)(2,1)S(1)}, bf16[256,768]{1,0:T(8,128)(2,1)S(1)}, u32[]{:S(2)}, u32[]{:S(2)}) collective-permute-start(bf16[256,768]{1,0:T(8,128)(2,1)S(1)} %copy-done.40), channel_id=1, source_target_pairs={{0,1},{1,0},{2,3},{3,2},{4,5},{5,4},{6,7},{7,6},{8,9},{9,8},{10,11... | collective-permute-start | bytes 1179656 | tf_op jit(solution)/shard_map/ppermute | solution.py:550
  130.7 8.9 %collective-permute-start.26 = (bf16[256,1024]{1,0:T(8,128)(2,1)S(1)}, bf16[256,1024]{1,0:T(8,128)(2,1)S(1)}, u32[]{:S(2)}, u32[]{:S(2)}) collective-permute-start(bf16[256,1024]{1,0:T(8,128)(2,1)S(1)} %copy-done.23), channel_id=1, source_target_pairs={{0,1},{1,0},{2,3},{3,2},{4,5},{5,4},{6,7},{7,6},{8,9},{9,8},{10,11... | collective-permute-start | bytes 1572872 | tf_op jit(solution)/shard_map/ppermute | solution.py:550
  133.8 15.0 %collective-permute-start.23 = (bf16[2,64,2048]{2,1,0:T(8,128)(2,1)}, bf16[2,64,2048]{2,1,0:T(8,128)(2,1)S(1)}, u32[]{:S(2)}, u32[]{:S(2)}) collective-permute-start(bf16[2,64,2048]{2,1,0:T(8,128)(2,1)} %get-tuple-element.155), channel_id=1, source_target_pairs={{0,8},{2,10},{4,12},{6,14},{8,0},{10,2},{12,4},{14,6},{16,24},{18,... | collective-permute-start | bytes 1572872 | tf_op jit(solution)/shard_map/ppermute | solution.py:553
  135.5 17.7 %collective-permute-start.19 = (bf16[4,64,1024]{2,1,0:T(8,128)(2,1)}, bf16[4,64,1024]{2,1,0:T(8,128)(2,1)S(1)}, u32[]{:S(2)}, u32[]{:S(2)}) collective-permute-start(bf16[4,64,1024]{2,1,0:T(8,128)(2,1)} %get-tuple-element.151), channel_id=1, source_target_pairs={{0,4},{2,6},{4,0},{6,2},{8,12},{10,14},{12,8},{14,10},{16,20},{18,... | collective-permute-start | bytes 1572872 | tf_op jit(solution)/shard_map/ppermute | solution.py:553
  136.9 18.8 %collective-permute-start.20 = (bf16[4,64,1024]{2,1,0:T(8,128)(2,1)}, bf16[4,64,1024]{2,1,0:T(8,128)(2,1)S(1)}, u32[]{:S(2)}, u32[]{:S(2)}) collective-permute-start(bf16[4,64,1024]{2,1,0:T(8,128)(2,1)} %get-tuple-element.152), channel_id=1, source_target_pairs={{0,2},{2,0},{4,6},{6,4},{8,10},{10,8},{12,14},{14,12},{16,18},{18,... | collective-permute-start | bytes 1572872 | tf_op jit(solution)/shard_map/ppermute | solution.py:553
  137.5 1.9 collective-permute-start.25
  139.4 27.2 %collective-permute-start.27 = (f32[8]{0:T(128)S(1)}, f32[8]{0:T(128)S(1)}, u32[]{:S(2)}, u32[]{:S(2)}) collective-permute-start(f32[8]{0:T(128)S(1)} %slice_bitcast_fusion.3), channel_id=1, source_target_pairs={{0,1},{1,0},{2,3},{3,2},{4,5},{5,4},{6,7},{7,6},{8,9},{9,8},{10,11... | collective-permute-start | bytes 104 | tf_op jit(solution)/shard_map/ppermute | solution.py:550
  147.2 27.5 %collective-permute-start.29 = (bf16[8,64,1024]{2,1,0:T(8,128)(2,1)}, bf16[8,64,1024]{2,1,0:T(8,128)(2,1)S(1)}, u32[]{:S(2)}, u32[]{:S(2)}) collective-permute-start(bf16[8,64,1024]{2,1,0:T(8,128)(2,1)} %get-tuple-element.167), channel_id=1, source_target_pairs={{0,2},{2,0},{4,6},{6,4},{8,10},{10,8},{12,14},{14,12},{16,18},{18,... | collective-permute-start | bytes 3145736 | tf_op jit(solution)/shard_map/ppermute | solution.py:553
  148.8 26.0 %collective-permute-start.30 = (bf16[8,64,1024]{2,1,0:T(8,128)(2,1)}, bf16[8,64,1024]{2,1,0:T(8,128)(2,1)S(1)}, u32[]{:S(2)}, u32[]{:S(2)}) collective-permute-start(bf16[8,64,1024]{2,1,0:T(8,128)(2,1)} %get-tuple-element.168), channel_id=1, source_target_pairs={{0,4},{2,6},{4,0},{6,2},{8,12},{10,14},{12,8},{14,10},{16,20},{18,... | collective-permute-start | bytes 3145736 | tf_op jit(solution)/shard_map/ppermute | solution.py:553
  153.2 21.6 %collective-permute-start.31 = (bf16[1,64,2048]{2,1,0:T(8,128)(2,1)}, bf16[1,64,2048]{2,1,0:T(8,128)(2,1)S(1)}, u32[]{:S(2)}, u32[]{:S(2)}) collective-permute-start(bf16[1,64,2048]{2,1,0:T(8,128)(2,1)} %get-tuple-element.170), channel_id=1, source_target_pairs={{0,16},{2,18},{4,20},{6,22},{8,24},{10,26},{12,28},{14,30},{16,0},... | collective-permute-start | bytes 786440 | tf_op jit(solution)/shard_map/ppermute | solution.py:553
  166.6 7.2 %collective-permute-start.28 = (bf16[10248]{0:T(1024)(128)(2,1)S(1)}, bf16[10248]{0:T(1024)(128)(2,1)S(1)}, u32[]{:S(2)}, u32[]{:S(2)}) collective-permute-start(bf16[10248]{0:T(1024)(128)(2,1)S(1)} %get-tuple-element.298), channel_id=1, source_target_pairs={{0,8},{2,10},{4,12},{6,14},{8,0},{10,2},{12,4},{14,6},{16,24},{18,... | collective-permute-start | bytes 61496 | tf_op jit(solution)/shard_map/ppermute | solution.py:553
  171.2 37.6 %all-to-all-start.2 = ((bf16[32,32,512]{2,1,0:T(8,128)(2,1)}), bf16[32,32,512]{2,1,0:T(8,128)(2,1)S(1)}, u32[]{:S(2)}, u32[]{:S(2)}) async-start(bf16[32,32,512]{2,1,0:T(8,128)(2,1)} %pad_maximum_fusion), calls=%async_computation.2 | async-start | bytes 2097152 | tf_op jit(solution)/shard_map/all_to_all | solution.py:578
  182.6 19.1 %collective-permute-start.32 = (bf16[16392]{0:T(1024)(128)(2,1)S(1)}, bf16[16392]{0:T(1024)(128)(2,1)S(1)}, u32[]{:S(2)}, u32[]{:S(2)}) collective-permute-start(bf16[16392]{0:T(1024)(128)(2,1)S(1)} %pad_maximum_fusion.5), channel_id=1, source_target_pairs={{0,16},{2,18},{4,20},{6,22},{8,24},{10,26},{12,28},{14,30},{16,0},... | collective-permute-start | bytes 98360 | tf_op jit(solution)/shard_map/ppermute | solution.py:553
  186.1 22.6 %collective-permute-start.34 = (bf16[4,64,1024]{2,1,0:T(8,128)(2,1)}, bf16[4,64,1024]{2,1,0:T(8,128)(2,1)S(1)}, u32[]{:S(2)}, u32[]{:S(2)}) collective-permute-start(bf16[4,64,1024]{2,1,0:T(8,128)(2,1)} %get-tuple-element.188), channel_id=1, source_target_pairs={{0,4},{2,6},{4,0},{6,2},{8,12},{10,14},{12,8},{14,10},{16,20},{18,... | collective-permute-start | bytes 1572872 | tf_op jit(solution)/shard_map/ppermute | solution.py:553
  187.6 21.1 %collective-permute-start.35 = (bf16[4,64,1024]{2,1,0:T(8,128)(2,1)}, bf16[4,64,1024]{2,1,0:T(8,128)(2,1)S(1)}, u32[]{:S(2)}, u32[]{:S(2)}) collective-permute-start(bf16[4,64,1024]{2,1,0:T(8,128)(2,1)} %get-tuple-element.189), channel_id=1, source_target_pairs={{0,2},{2,0},{4,6},{6,4},{8,10},{10,8},{12,14},{14,12},{16,18},{18,... | collective-permute-start | bytes 1572872 | tf_op jit(solution)/shard_map/ppermute | solution.py:553
  191.8 16.9 %collective-permute-start.33 = (bf16[2,64,2048]{2,1,0:T(8,128)(2,1)}, bf16[2,64,2048]{2,1,0:T(8,128)(2,1)S(1)}, u32[]{:S(2)}, u32[]{:S(2)}) collective-permute-start(bf16[2,64,2048]{2,1,0:T(8,128)(2,1)} %get-tuple-element.195), channel_id=1, source_target_pairs={{0,8},{2,10},{4,12},{6,14},{8,0},{10,2},{12,4},{14,6},{16,24},{18,... | collective-permute-start | bytes 1572872 | tf_op jit(solution)/shard_map/ppermute | solution.py:553
  214.6 14.6 %collective-permute-start.39 = (bf16[1,64,2048]{2,1,0:T(8,128)(2,1)}, bf16[1,64,2048]{2,1,0:T(8,128)(2,1)S(1)}, u32[]{:S(2)}, u32[]{:S(2)}) collective-permute-start(bf16[1,64,2048]{2,1,0:T(8,128)(2,1)} %get-tuple-element.201), channel_id=1, source_target_pairs={{0,16},{2,18},{4,20},{6,22},{8,24},{10,26},{12,28},{14,30},{16,0},... | collective-permute-start | bytes 786440 | tf_op jit(solution)/shard_map/ppermute | solution.py:553
  214.6 18.7 %collective-permute-start.38 = (bf16[2,64,2048]{2,1,0:T(8,128)(2,1)}, bf16[2,64,2048]{2,1,0:T(8,128)(2,1)S(1)}, u32[]{:S(2)}, u32[]{:S(2)}) collective-permute-start(bf16[2,64,2048]{2,1,0:T(8,128)(2,1)} %get-tuple-element.199), channel_id=1, source_target_pairs={{0,8},{2,10},{4,12},{6,14},{8,0},{10,2},{12,4},{14,6},{16,24},{18,... | collective-permute-start | bytes 1572872 | tf_op jit(solution)/shard_map/ppermute | solution.py:553
  216.9 4.3 %collective-permute-start.36 = (bf16[28680]{0:T(1024)(128)(2,1)S(1)}, bf16[28680]{0:T(1024)(128)(2,1)S(1)}, u32[]{:S(2)}, u32[]{:S(2)}) collective-permute-start(bf16[28680]{0:T(1024)(128)(2,1)S(1)} %pad_maximum_fusion.4), channel_id=1, source_target_pairs={{0,2},{2,0},{4,6},{6,4},{8,10},{10,8},{12,14},{14,12},{16,18},{18,... | collective-permute-start | bytes 172088 | tf_op jit(solution)/shard_map/ppermute | solution.py:553
  221.4 4.8 %collective-permute-start.37 = (bf16[53256]{0:T(1024)(128)(2,1)S(1)}, bf16[53256]{0:T(1024)(128)(2,1)S(1)}, u32[]{:S(2)}, u32[]{:S(2)}) collective-permute-start(bf16[53256]{0:T(1024)(128)(2,1)S(1)} %pad_maximum_fusion.3), channel_id=1, source_target_pairs={{0,4},{2,6},{4,0},{6,2},{8,12},{10,14},{12,8},{14,10},{16,20},{18,... | collective-permute-start | bytes 319544 | tf_op jit(solution)/shard_map/ppermute | solution.py:553
  236.4 1.4 collective-permute-start.40
  237.2 14.8 %collective-permute-start.41 = (bf16[1,64,2048]{2,1,0:T(8,128)(2,1)}, bf16[1,64,2048]{2,1,0:T(8,128)(2,1)S(1)}, u32[]{:S(2)}, u32[]{:S(2)}) collective-permute-start(bf16[1,64,2048]{2,1,0:T(8,128)(2,1)} %get-tuple-element.205), channel_id=1, source_target_pairs={{0,16},{2,18},{4,20},{6,22},{8,24},{10,26},{12,28},{14,30},{16,0},... | collective-permute-start | bytes 786440 | tf_op jit(solution)/shard_map/ppermute | solution.py:553
  (55 other events, 278.2 us)

commit v3 on v2

--- a/solution.py
+++ b/solution.py
@@ -884,6 +884,7 @@
         "v" + "h" * 11,
         mods,
         *end_ins,
+        flops=int(2e9),
     )
 
     row_grads = jnp.stack(
@@ -915,29 +916,27 @@
         both = jnp.where(mine == 0, jnp.stack([gathered, theirs]), jnp.stack([theirs, gathered]))
         return both, rounded.astype(f32) + came[count:].astype(f32)
 
-    gathered, bias_sum = double(row_grads.reshape(6 * width), bias_sum, 2)
     returned = exchange(
-        jnp.concatenate(
-            [to_target(values) for values in after((output, tokens_grad))], axis=1
-        )
-    )
-    qkv_own, qkv_sent = scatter_second(
-        qkv_rest, after(qkv_came, fc1_came, fc2_came, gathered)
-    )
+        jnp.concatenate([to_target(values) for values in (output, tokens_grad)], axis=1)
+    )
+    qkv_own, qkv_sent = scatter_second(qkv_rest, after(qkv_came, fc1_came, fc2_came, tokens_grad))
     qkv_came = travel(qkv_sent[::-1])[::-1]
     fc1_own, fc1_sent = scatter_more(2, fc1_own, after(fc1_came, qkv_sent))
     fc1_came = (flip(fc1_sent, 2),)
-    gathered = after(gathered, qkv_sent)
-    for bit in range(3, bits):
+    gathered = after(row_grads, qkv_sent).reshape(6 * width)
+    for bit in (2, 0):
         gathered, bias_sum = double(gathered, bias_sum, bit)
     qkv_own, qkv_sent = scatter_more(2, qkv_own, after(qkv_came, fc1_came, gathered, returned))
     qkv_came = (flip(qkv_sent, 2),)
     fc1_own, fc1_sent = scatter_more(3, fc1_own, after(fc1_came, qkv_sent))
     fc1_came = (flip(fc1_sent, 3),)
     gathered = after(gathered, fc1_sent)
-    for bit in range(2):
+    for bit in [1] + list(range(3, bits)):
         gathered, bias_sum = double(gathered, bias_sum, bit)
-    gathered = gathered.transpose(*range(2, bits), 0, 1, bits).reshape(groups, 6 * width)
+    order = list(range(bits - 1, 2, -1)) + [1, 0, 2]
+    gathered = gathered.transpose(
+        *[order.index(bit) for bit in range(bits - 1, -1, -1)], bits
+    ).reshape(groups, 6 * width)
     qkv_own, qkv_sent = scatter_more(3, qkv_own, after(qkv_came, fc1_came, gathered))
     qkv_came = (flip(qkv_sent, 3),)
     gathered = after(gathered, qkv_sent)

time: 258 us -> 254 us (0.984)
  waiting for transfers between devices: 58.1 us -> 55.1 us
    unnamed x133 -> x131, local copies, waits for them, and re-layouts: 9.82 us -> 11.3 us
  transfers between devices with their start and end apart: 45 -> 45, of which waited for: 16 -> 14; matrix products, arithmetic and copies ran while one was open for 15% -> 14% of each run, Pallas kernels for 37% -> 38%
where the time goes in v3:
time: 254 us; the launch traced here: 250 us
  Pallas kernels  101 us (40%)
  waiting for transfers between devices  55.1 us (22%)
  starting transfers between devices  45.1 us (18%)
  local copies, waits for them, and re-layouts  29.5 us (12%)
  other arithmetic  13.2 us (5%)
  matrix products  3.75 us (1%)
    pallas_call x16, Pallas kernels, local_call(): pl.pallas_call(kernel, out_shape=outs, in_specs=[places[kind] for kind in...  101 us
    ppermute x22, waiting for transfers between devices, flip(): lax.ppermute(values, 'dp', [(i, i ^ 1 << bit) for i in range(groups)])  39.4 us
    ppermute x22, starting transfers between devices, flip(): lax.ppermute(values, 'dp', [(i, i ^ 1 << bit) for i in range(groups)])  26.3 us
    all_to_all x3, starting transfers between devices, exchange(): lax.all_to_all(values, ('dp', 'mp'), split_axis=0, concat_axis=0, tiled=T...  13.9 us
    unnamed x131, local copies, waits for them, and re-layouts  11.3 us
    all_to_all x3, waiting for transfers between devices, exchange(): lax.all_to_all(values, ('dp', 'mp'), split_axis=0, concat_axis=0, tiled=T...  11.1 us
  transfers between devices with their start and end apart: 45, of which 14 were waited for; matrix products, arithmetic and copies ran while one was open for 14% of the time, Pallas kernels for 38%

profile of v3, /device:TPU:0, one launch (start us, length us, event | category | flops | bytes accessed | tf_op | source)
XLA Modules:
  0.0 249.8 jit_solution(14619744249905659154)
XLA Ops:
  5.3 7.1 %all-to-all-start = ((bf16[32,24,512]{2,1,0:T(8,128)(2,1)}), bf16[32,24,512]{2,1,0:T(8,128)(2,1)}, u32[]{:S(2)}, u32[]{:S(2)}) async-start(bf16[32,24,512]{2,1,0:T(8,128)(2,1)} %pad_maximum_fusion.1), calls=%async_computation | async-start | bytes 1572864 | tf_op jit(solution)/shard_map/all_to_all | solution.py:578
  12.8 2.1 slice_bitcast_fusion
  17.3 1.9 copy.66
  21.9 11.1 %all-to-all-done.arrived = bf16[32,24,512]{2,1,0:T(8,128)(2,1)} async-done(((bf16[32,24,512]{2,1,0:T(8,128)(2,1)}), bf16[32,24,512]{2,1,0:T(8,128)(2,1)}, u32[]{:S(2)}, u32[]{:S(2)}) %all-to-all-start) | async-done | bytes 786464 | tf_op jit(solution)/shard_map/all_to_all | solution.py:578
  33.0 3.9 %all-to-all-start.1 = ((bf16[32,16,512]{2,1,0:T(8,128)(2,1)}), bf16[32,16,512]{2,1,0:T(8,128)(2,1)}, u32[]{:S(2)}, u32[]{:S(2)}) async-start(bf16[32,16,512]{2,1,0:T(8,128)(2,1)} %bitcast.135), calls=%async_computation.1 | async-start | bytes 1048576 | tf_op jit(solution)/shard_map/all_to_all | solution.py:578
  38.2 17.2 %shard_map.281 = (bf16[256,1024]{1,0:T(8,128)(2,1)}, bf16[2,256,512]{2,1,0:T(8,128)(2,1)}, bf16[2,256,512]{2,1,0:T(8,128)(2,1)}, bf16[2,256,512]{2,1,0:T(8,128)(...) custom-call(bf16[32,24,512]{2,1,0:T(8,128)(2,1)} %all-to-all-done.ar, ...), custom_call_target="tpu_custom_call" | custom-call | flops 1 | bytes 1 | tf_op jit(solution)/shard_map/pallas_call | solution.py:486
  55.5 1.7 copy.67
  60.3 1.3 collective-permute-done.7.refs_3_.refs_2_
  63.3 5.7 %shard_map.282 = (f32[1,1024]{1,0:T(1,128)}, f32[1,2048]{1,0:T(1,128)}, bf16[16,64,512]{2,1,0:T(8,128)(2,1)}, bf16[8,64,1024]{2,1,0:T(8,128)(2,1)}, bf16[8,64,1024]{2,1,0:T(8,128)(2,1)}) custom-call(s32[4]{0:T(128)} %pad_add_fusion.bit_ref, bf16[256,1024]{1,0:T(8,128)(2,1)} %copy-done.6, bf16[256,1024]{1,0:T(8,128)(2,1)} %copy-done.34, ...), custom_call_target="tpu_custom_call" | custom-call | flops 1 | bytes 1 | tf_op jit(solution)/shard_map/pallas_call | solution.py:486
  69.0 1.7 collective-permute-start.13
  70.7 1.5 collective-permute-start.14
  72.8 10.1 %shard_map.283 = (bf16[256,2048]{1,0:T(8,128)(2,1)}, bf16[256,1024]{1,0:T(8,128)(2,1)}, bf16[256,1024]{1,0:T(8,128)(2,1)}, bf16[256,1024]{1,0:T(8,128)(2,1)}, f32[1,1024]{1,0:T(1,128)}) custom-call(bf16[256,1024]{1,0:T(8,128)(2,1)} %copy-done.6, f32[6,1024]{1,0:T(8,128)} %get-tuple-element.110.mods, f32[1,1024]{1,0:T(1,128)} %broadcast_select_fusion.6.fc2_bias, ...), custom_call_target="tpu_custom_call" | custom-call | flops 1 | bytes 1 | tf_op jit(solution)/shard_map/pallas_call | solution.py:486
  83.5 1.6 collective-permute-done.15.refs_3_.refs_2_
  86.6 5.7 %shard_map.284 = (f32[1,1024]{1,0:T(1,128)}, f32[1,2048]{1,0:T(1,128)}, bf16[16,64,512]{2,1,0:T(8,128)(2,1)}, bf16[8,64,1024]{2,1,0:T(8,128)(2,1)}, bf16[8,64,1024]{2,1,0:T(8,128)(2,1)}) custom-call(s32[4]{0:T(128)} %pad_add_fusion.bit_ref, bf16[256,1024]{1,0:T(8,128)(2,1)} %get-tuple-element.119.refs_0_, bf16[256,1024]{1,0:T(8,128)(2,1)} %collective-permute-done.10.refs_1_, ...), custom_call_target="tpu_custom_call" | custom-call | flops 1 | bytes 1 | tf_op jit(solution)/shard_map/pallas_call | solution.py:486
  93.3 1.3 collective-permute-done.13.refs_4_
  94.7 1.8 collective-permute-done.14.refs_5_
  97.4 5.5 %shard_map.285 = (bf16[4,64,1024]{2,1,0:T(8,128)(2,1)}, bf16[4,64,1024]{2,1,0:T(8,128)(2,1)}, bf16[4,64,2048]{2,1,0:T(8,128)(2,1)}) custom-call(s32[4]{0:T(128)} %pad_add_fusion.bit_ref, bf16[16,64,512]{2,1,0:T(8,128)(2,1)} %get-tuple-element.127.refs_0_, bf16[256,2048]{1,0:T(8,128)(2,1)} %get-tuple-element.112.refs_2_.refs_4_.refs_1_, ...), custom_call_target="tpu_custom_call" | custom-call | flops 3000000000 | bytes 1 | tf_op jit(solution)/shard_map/pallas_call | solution.py:486
  102.9 2.1 collective-permute-start.21
  105.3 16.1 %shard_map.286 = (f32[256,1024]{1,0:T(8,128)}, bf16[256,1024]{1,0:T(8,128)(2,1)}, bf16[256,1536]{1,0:T(8,128)(2,1)}, bf16[256,768]{1,0:T(8,128)(2,1)}, bf16[256,768]{1,0:T(8,128)(2,1)}, /*index=5*/f32[4,1024]{1,0:T(4,128)}) custom-call(f32[6,1024]{1,0:T(8,128)} %get-tuple-element.110.mods, f32[2,512]{1,0:T(2,128)} %pad_maximum_fusion.10.mult, ...), custom_call_target="tpu_custom_call" | custom-call | flops 1 | bytes 1 | tf_op jit(solution)/shard_map/pallas_call | solution.py:486
  122.7 5.5 %shard_map.287 = (bf16[4,64,1024]{2,1,0:T(8,128)(2,1)}, bf16[4,64,1024]{2,1,0:T(8,128)(2,1)}, bf16[4,64,2048]{2,1,0:T(8,128)(2,1)}) custom-call(s32[4]{0:T(128)} %pad_add_fusion.bit_ref, bf16[16,64,512]{2,1,0:T(8,128)(2,1)} %get-tuple-element.145.refs_0_, bf16[256,2048]{1,0:T(8,128)(2,1)} %get-tuple-element.136.refs_2_.refs_0_.refs_1_, ...), custom_call_target="tpu_custom_call" | custom-call | flops 1 | bytes 1 | tf_op jit(solution)/shard_map/pallas_call | solution.py:486
  128.3 1.5 collective-permute-done.21.refs_0_
  130.7 2.7 %shard_map.288 = (bf16[2,64,2048]{2,1,0:T(8,128)(2,1)}, bf16[2,64,2048]{2,1,0:T(8,128)(2,1)}) custom-call(s32[4]{0:T(128)} %pad_add_fusion.bit_ref, bf16[4,64,2048]{2,1,0:T(8,128)(2,1)} %get-tuple-element.151.own, bf16[4,64,1024]{2,1,0:T(8,128)(2,1)} %copy-done.25, bf16[4,64,1024]{2,1,0:T(8,128)(2,1)} %copy-done.26), custom_call_target="tpu_custom_call" | custom-call | flops 1 | bytes 1 | tf_op jit(solution)/shard_map/pallas_call | solution.py:486
  133.5 1.5 collective-permute-start.23
  134.9 1.5 collective-permute-start.19
  139.4 7.0 %shard_map.289 = (f32[1,1024]{1,0:T(1,128)}, f32[1,1024]{1,0:T(1,128)}, f32[1,1536]{1,0:T(1,128)}, f32[1,512]{1,0:T(1,128)}, bf16[16,64,512]{2,1,0:T(8,128)(2,1)...) custom-call(s32[4]{0:T(128)} %pad_add_fusion.bit_ref, ...), custom_call_target="tpu_custom_call" | custom-call | flops 1 | bytes 1 | tf_op jit(solution)/shard_map/pallas_call | solution.py:486
  146.4 1.5 collective-permute-start.27
  148.8 2.2 shard_map.290
  150.9 2.4 collective-permute-start.29
  154.1 7.5 %shard_map.291 = (bf16[256,1024]{1,0:T(8,128)(2,1)}, f32[2,1024]{1,0:T(2,128)}) custom-call(f32[6,1024]{1,0:T(8,128)} %get-tuple-element.110.mods, bf16[256,1536]{1,0:T(8,128)(2,1)} %get-tuple-element.169.refs_2_.refs_0_, bf16[256,768]{1,0:T(8,128)(2,1)} %get-tuple-element.156.refs_1_, bf16[256,768]{1,0:T(8,128)(2,1)} %get-tuple-element.157.refs_2_, ...), custom_call_target="tpu_custom_call" | custom-call | flops 2000000000 | bytes 1 | tf_op jit(solution)/shard_map/pallas_call | solution.py:486
  161.6 1.4 reshape.409
  164.2 2.8 %all-to-all-start.2 = ((bf16[32,32,512]{2,1,0:T(8,128)(2,1)}), bf16[32,32,512]{2,1,0:T(8,128)(2,1)S(1)}, u32[]{:S(2)}, u32[]{:S(2)}) async-start(bf16[32,32,512]{2,1,0:T(8,128)(2,1)} %pad_maximum_fusion), calls=%async_computation.2 | async-start | bytes 2097152 | tf_op jit(solution)/shard_map/all_to_all | solution.py:578
  168.3 9.3 %collective-permute-done.27.refs_7_ = bf16[8,64,1024]{2,1,0:T(8,128)(2,1)S(1)} collective-permute-done((bf16[8,64,1024]{2,1,0:T(8,128)(2,1)}, bf16[8,64,1024]{2,1,0:T(8,128)(2,1)S(1)}, u32[]{:S(2)}, u32[]{:S(2)}) %collective-permute-start.27) | collective-permute-done | bytes 1048608 | tf_op jit(solution)/shard_map/ppermute | solution.py:553
  179.0 6.3 %shard_map.292 = (bf16[4,64,1024]{2,1,0:T(8,128)(2,1)}, bf16[4,64,1024]{2,1,0:T(8,128)(2,1)}, bf16[4,64,2048]{2,1,0:T(8,128)(2,1)}) custom-call(s32[4]{0:T(128)} %pad_add_fusion.bit_ref, bf16[16,64,512]{2,1,0:T(8,128)(2,1)} %get-tuple-element.176.refs_0_, bf16[16,64,512]{2,1,0:T(8,128)(2,1)} %get-tuple-element.177.refs_1_, ...), custom_call_target="tpu_custom_call" | custom-call | flops 1 | bytes 1 | tf_op jit(solution)/shard_map/pallas_call | solution.py:486
  187.1 1.9 add_bitcast_fusion
  190.0 2.7 %shard_map.293 = (bf16[2,64,2048]{2,1,0:T(8,128)(2,1)}, bf16[2,64,2048]{2,1,0:T(8,128)(2,1)}) custom-call(s32[4]{0:T(128)} %pad_add_fusion.bit_ref, bf16[4,64,2048]{2,1,0:T(8,128)(2,1)} %get-tuple-element.187.own, bf16[4,64,1024]{2,1,0:T(8,128)(2,1)} %collective-permute-done.19.refs_0_, bf16[4,64,1024]{2,1,0:T(8,128)(2,1)} %collective-permute-done.20.refs_1_), custom_call_target="tpu_custom_call" | custom-call | flops 1 | bytes 1 | tf_op jit(solution)/shard_map/pallas_call | solution.py:486
  192.7 1.5 collective-permute-start.33
  194.5 1.3 collective-permute-start.32
  195.8 3.7 %collective-permute-done.32 = bf16[16392]{0:T(1024)(128)(2,1)S(1)} collective-permute-done((bf16[16392]{0:T(1024)(128)(2,1)S(1)}, bf16[16392]{0:T(1024)(128)(2,1)S(1)}, u32[]{:S(2)}, u32[]{:S(2)}) %collective-permute-start.32) | collective-permute-done | bytes 32816 | tf_op jit(solution)/shard_map/ppermute | solution.py:553
  199.7 3.8 %collective-permute-done.33.refs_0_ = bf16[2,64,2048]{2,1,0:T(8,128)(2,1)S(1)} collective-permute-done((bf16[2,64,2048]{2,1,0:T(8,128)(2,1)}, bf16[2,64,2048]{2,1,0:T(8,128)(2,1)S(1)}, u32[]{:S(2)}, u32[]{:S(2)}) %collective-permute-start.33) | collective-permute-done | bytes 524320 | tf_op jit(solution)/shard_map/ppermute | solution.py:553
  204.5 2.7 %shard_map.294 = (bf16[2,64,2048]{2,1,0:T(8,128)(2,1)}, bf16[2,64,2048]{2,1,0:T(8,128)(2,1)}) custom-call(s32[4]{0:T(128)} %pad_add_fusion.bit_ref, bf16[4,64,2048]{2,1,0:T(8,128)(2,1)} %get-tuple-element.192.own, bf16[4,64,1024]{2,1,0:T(8,128)(2,1)} %copy-done.22, bf16[4,64,1024]{2,1,0:T(8,128)(2,1)} %copy-done.23), custom_call_target="tpu_custom_call" | custom-call | flops 1 | bytes 1 | tf_op jit(solution)/shard_map/pallas_call | solution.py:486
  207.2 2.2 shard_map.295
  210.5 1.5 collective-permute-start.38
  212.1 1.5 collective-permute-start.36
  217.1 7.9 %collective-permute-done.37 = bf16[53256]{0:T(1024)(128)(2,1)S(1)} collective-permute-done((bf16[53256]{0:T(1024)(128)(2,1)S(1)}, bf16[53256]{0:T(1024)(128)(2,1)S(1)}, u32[]{:S(2)}, u32[]{:S(2)}) %collective-permute-start.37) | collective-permute-done | bytes 106544 | tf_op jit(solution)/shard_map/ppermute | solution.py:553
  228.7 2.2 shard_map.296
  231.8 3.4 %collective-permute-start.41 = (bf16[1,64,2048]{2,1,0:T(8,128)(2,1)}, bf16[1,64,2048]{2,1,0:T(8,128)(2,1)S(1)}, u32[]{:S(2)}, u32[]{:S(2)}) collective-permute-start(bf16[1,64,2048]{2,1,0:T(8,128)(2,1)} %get-tuple-element.201), channel_id=1, source_target_pairs={{0,16},{2,18},{4,20},{6,22},{8,24},{10,26},{12,28},{14,30},{16,0},... | collective-permute-start | bytes 786440 | tf_op jit(solution)/shard_map/ppermute | solution.py:553
  236.7 1.2 copy.99
  239.0 9.0 %collective-permute-done.41 = bf16[1,64,2048]{2,1,0:T(8,128)(2,1)S(1)} collective-permute-done((bf16[1,64,2048]{2,1,0:T(8,128)(2,1)}, bf16[1,64,2048]{2,1,0:T(8,128)(2,1)S(1)}, u32[]{:S(2)}, u32[]{:S(2)}) %collective-permute-start.41) | collective-permute-done | bytes 262176 | tf_op jit(solution)/shard_map/ppermute | solution.py:553
  (306 shorter events, 48.9 us)
Async XLA Ops:
  0.7 37.5 %collective-permute-start.5 = (bf16[1024,2048]{1,0:T(8,128)(2,1)}, bf16[1024,2048]{1,0:T(8,128)(2,1)}, u32[]{:S(2)}, u32[]{:S(2)}) collective-permute-start(bf16[1024,2048]{1,0:T(8,128)(2,1)} %refs_1_.1), channel_id=1, source_target_pairs={{0,1},{1,0},{2,3},{3,2},{4,5},{5,4},{6,7},{7,6},{8,9},{9,8},{10,11... | collective-permute-start | bytes 12582920 | tf_op jit(solution)/shard_map/ppermute | solution.py:550
  5.3 27.7 %all-to-all-start = ((bf16[32,24,512]{2,1,0:T(8,128)(2,1)}), bf16[32,24,512]{2,1,0:T(8,128)(2,1)}, u32[]{:S(2)}, u32[]{:S(2)}) async-start(bf16[32,24,512]{2,1,0:T(8,128)(2,1)} %pad_maximum_fusion.1), calls=%async_computation | async-start | bytes 1572864 | tf_op jit(solution)/shard_map/all_to_all | solution.py:578
  12.6 6.6 %collective-permute-start = (f32[7176]{0:T(1024)S(1)}, f32[7176]{0:T(1024)S(1)}, u32[]{:S(2)}, u32[]{:S(2)}) collective-permute-start(f32[7176]{0:T(1024)S(1)} %concatenate.132), channel_id=1, source_target_pairs={{0,1},{1,0},{2,3},{3,2},{4,5},{5,4},{6,7},{7,6},{8,9},{9,8},{10,11... | collective-permute-start | bytes 86120 | tf_op jit(solution)/shard_map/ppermute | solution.py:550
  14.9 23.3 %copy-start.2 = (bf16[1024,512]{1,0:T(8,128)(2,1)}, bf16[1024,512]{1,0:T(8,128)(2,1)S(1)}, u32[]{:S(2)}) copy-start(bf16[1024,512]{1,0:T(8,128)(2,1)S(1)} %get-tuple-element.266.refs_2_.refs_7_) | copy-start | bytes 3145732
  14.9 23.3 %copy-start.3 = (bf16[1024,512]{1,0:T(8,128)(2,1)}, bf16[1024,512]{1,0:T(8,128)(2,1)S(1)}, u32[]{:S(2)}) copy-start(bf16[1024,512]{1,0:T(8,128)(2,1)S(1)} %get-tuple-element.267.refs_0_.refs_5_) | copy-start | bytes 3145732
  14.9 23.3 %copy-start.4 = (bf16[1024,512]{1,0:T(8,128)(2,1)}, bf16[1024,512]{1,0:T(8,128)(2,1)S(1)}, u32[]{:S(2)}) copy-start(bf16[1024,512]{1,0:T(8,128)(2,1)S(1)} %get-tuple-element.268.refs_1_.refs_6_) | copy-start | bytes 3145732
  14.9 6.1 %collective-permute-start.1 = (bf16[1024,512]{1,0:T(8,128)(2,1)S(1)}, bf16[1024,512]{1,0:T(8,128)(2,1)}, u32[]{:S(2)}, u32[]{:S(2)}) collective-permute-start(bf16[1024,512]{1,0:T(8,128)(2,1)S(1)} %get-tuple-element.267.refs_0_.refs_5_), channel_id=1, source_target_pairs={{0,1},{1,0},{2,3},{3,2},{4,5},{5,4},{6,7},{7,6},{8,9},{9,8},{10,11... | collective-permute-start | bytes 3145736 | tf_op jit(solution)/shard_map/ppermute | solution.py:550
  15.3 22.9 %collective-permute-start.2 = (bf16[1024,512]{1,0:T(8,128)(2,1)S(1)}, bf16[1024,512]{1,0:T(8,128)(2,1)}, u32[]{:S(2)}, u32[]{:S(2)}) collective-permute-start(bf16[1024,512]{1,0:T(8,128)(2,1)S(1)} %get-tuple-element.268.refs_1_.refs_6_), channel_id=1, source_target_pairs={{0,1},{1,0},{2,3},{3,2},{4,5},{5,4},{6,7},{7,6},{8,9},{9,8},{10,11... | collective-permute-start | bytes 3145736 | tf_op jit(solution)/shard_map/ppermute | solution.py:550
  15.5 57.3 %collective-permute-start.12 = (bf16[2048,1024]{1,0:T(8,128)(2,1)}, bf16[2048,1024]{1,0:T(8,128)(2,1)}, u32[]{:S(2)}, u32[]{:S(2)}) collective-permute-start(bf16[2048,1024]{1,0:T(8,128)(2,1)} %refs_2_.1), channel_id=1, source_target_pairs={{0,1},{1,0},{2,3},{3,2},{4,5},{5,4},{6,7},{7,6},{8,9},{9,8},{10,11... | collective-permute-start | bytes 12582920 | tf_op jit(solution)/shard_map/ppermute | solution.py:550
  19.2 19.0 %collective-permute-start.3 = (bf16[1024,512]{1,0:T(8,128)(2,1)S(1)}, bf16[1024,512]{1,0:T(8,128)(2,1)}, u32[]{:S(2)}, u32[]{:S(2)}) collective-permute-start(bf16[1024,512]{1,0:T(8,128)(2,1)S(1)} %get-tuple-element.266.refs_2_.refs_7_), channel_id=1, source_target_pairs={{0,1},{1,0},{2,3},{3,2},{4,5},{5,4},{6,7},{7,6},{8,9},{9,8},{10,11... | collective-permute-start | bytes 3145736 | tf_op jit(solution)/shard_map/ppermute | solution.py:550
  21.0 17.2 %collective-permute-start.4 = (bf16[512,1024]{1,0:T(8,128)(2,1)}, bf16[512,1024]{1,0:T(8,128)(2,1)}, u32[]{:S(2)}, u32[]{:S(2)}) collective-permute-start(bf16[512,1024]{1,0:T(8,128)(2,1)} %refs_8_.3), channel_id=1, source_target_pairs={{0,1},{1,0},{2,3},{3,2},{4,5},{5,4},{6,7},{7,6},{8,9},{9,8},{10,11... | collective-permute-start | bytes 3145736 | tf_op jit(solution)/shard_map/ppermute | solution.py:550
  33.0 22.5 %all-to-all-start.1 = ((bf16[32,16,512]{2,1,0:T(8,128)(2,1)}), bf16[32,16,512]{2,1,0:T(8,128)(2,1)}, u32[]{:S(2)}, u32[]{:S(2)}) async-start(bf16[32,16,512]{2,1,0:T(8,128)(2,1)} %bitcast.135), calls=%async_computation.1 | async-start | bytes 1048576 | tf_op jit(solution)/shard_map/all_to_all | solution.py:578
  58.1 2.0 collective-permute-start.6
  58.4 3.2 %collective-permute-start.7 = (bf16[256,1024]{1,0:T(8,128)(2,1)S(1)}, bf16[256,1024]{1,0:T(8,128)(2,1)S(1)}, u32[]{:S(2)}, u32[]{:S(2)}) collective-permute-start(bf16[256,1024]{1,0:T(8,128)(2,1)S(1)} %copy-done.20), channel_id=1, source_target_pairs={{0,1},{1,0},{2,3},{3,2},{4,5},{5,4},{6,7},{7,6},{8,9},{9,8},{10,11... | collective-permute-start | bytes 1572872 | tf_op jit(solution)/shard_map/ppermute | solution.py:550
  58.7 4.5 %collective-permute-start.8 = (bf16[256,1024]{1,0:T(8,128)(2,1)}, bf16[256,1024]{1,0:T(8,128)(2,1)}, u32[]{:S(2)}, u32[]{:S(2)}) collective-permute-start(bf16[256,1024]{1,0:T(8,128)(2,1)} %get-tuple-element.115.refs_6_), channel_id=1, source_target_pairs={{0,1},{1,0},{2,3},{3,2},{4,5},{5,4},{6,7},{7,6},{8,9},{9,8},{10,11... | collective-permute-start | bytes 1572872 | tf_op jit(solution)/shard_map/ppermute | solution.py:550
  58.9 11.8 %collective-permute-start.11 = (bf16[256,512]{1,0:T(8,128)(2,1)S(1)}, bf16[256,512]{1,0:T(8,128)(2,1)S(1)}, u32[]{:S(2)}, u32[]{:S(2)}) collective-permute-start(bf16[256,512]{1,0:T(8,128)(2,1)S(1)} %copy-done.55), channel_id=1, source_target_pairs={{0,1},{1,0},{2,3},{3,2},{4,5},{5,4},{6,7},{7,6},{8,9},{9,8},{10,11... | collective-permute-start | bytes 786440 | tf_op jit(solution)/shard_map/ppermute | solution.py:550
  60.1 12.7 %collective-permute-start.10 = (bf16[256,1024]{1,0:T(8,128)(2,1)}, bf16[256,1024]{1,0:T(8,128)(2,1)}, u32[]{:S(2)}, u32[]{:S(2)}) collective-permute-start(bf16[256,1024]{1,0:T(8,128)(2,1)} %get-tuple-element.119.refs_0_), channel_id=1, source_target_pairs={{0,1},{1,0},{2,3},{3,2},{4,5},{5,4},{6,7},{7,6},{8,9},{9,8},{10,11... | collective-permute-start | bytes 1572872 | tf_op jit(solution)/shard_map/ppermute | solution.py:550
  62.4 10.4 %collective-permute-start.9 = (bf16[256,1024]{1,0:T(8,128)(2,1)S(1)}, bf16[256,1024]{1,0:T(8,128)(2,1)S(1)}, u32[]{:S(2)}, u32[]{:S(2)}) collective-permute-start(bf16[256,1024]{1,0:T(8,128)(2,1)S(1)} %copy-done.18), channel_id=1, source_target_pairs={{0,1},{1,0},{2,3},{3,2},{4,5},{5,4},{6,7},{7,6},{8,9},{9,8},{10,11... | collective-permute-start | bytes 1572872 | tf_op jit(solution)/shard_map/ppermute | solution.py:550
  69.0 25.7 %collective-permute-start.13 = (bf16[8,64,1024]{2,1,0:T(8,128)(2,1)}, bf16[8,64,1024]{2,1,0:T(8,128)(2,1)S(1)}, u32[]{:S(2)}, u32[]{:S(2)}) collective-permute-start(bf16[8,64,1024]{2,1,0:T(8,128)(2,1)} %get-tuple-element.116), channel_id=1, source_target_pairs={{0,2},{2,0},{4,6},{6,4},{8,10},{10,8},{12,14},{14,12},{16,18},{18,... | collective-permute-start | bytes 3145736 | tf_op jit(solution)/shard_map/ppermute | solution.py:553
  70.7 25.7 %collective-permute-start.14 = (bf16[8,64,1024]{2,1,0:T(8,128)(2,1)}, bf16[8,64,1024]{2,1,0:T(8,128)(2,1)S(1)}, u32[]{:S(2)}, u32[]{:S(2)}) collective-permute-start(bf16[8,64,1024]{2,1,0:T(8,128)(2,1)} %get-tuple-element.117), channel_id=1, source_target_pairs={{0,4},{2,6},{4,0},{6,2},{8,12},{10,14},{12,8},{14,10},{16,20},{18,... | collective-permute-start | bytes 3145736 | tf_op jit(solution)/shard_map/ppermute | solution.py:553
  82.9 2.2 collective-permute-start.15
  83.0 2.9 %collective-permute-start.16 = (bf16[256,1024]{1,0:T(8,128)(2,1)}, bf16[256,1024]{1,0:T(8,128)(2,1)S(1)}, u32[]{:S(2)}, u32[]{:S(2)}) collective-permute-start(bf16[256,1024]{1,0:T(8,128)(2,1)} %get-tuple-element.129.refs_3_), channel_id=1, source_target_pairs={{0,1},{1,0},{2,3},{3,2},{4,5},{5,4},{6,7},{7,6},{8,9},{9,8},{10,11... | collective-permute-start | bytes 1572872 | tf_op jit(solution)/shard_map/ppermute | solution.py:550
  92.4 29.0 %collective-permute-start.17 = (bf16[8,64,1024]{2,1,0:T(8,128)(2,1)}, bf16[8,64,1024]{2,1,0:T(8,128)(2,1)S(1)}, u32[]{:S(2)}, u32[]{:S(2)}) collective-permute-start(bf16[8,64,1024]{2,1,0:T(8,128)(2,1)} %get-tuple-element.130), channel_id=1, source_target_pairs={{0,2},{2,0},{4,6},{6,4},{8,10},{10,8},{12,14},{14,12},{16,18},{18,... | collective-permute-start | bytes 3145736 | tf_op jit(solution)/shard_map/ppermute | solution.py:553
  93.0 28.4 %collective-permute-start.18 = (bf16[8,64,1024]{2,1,0:T(8,128)(2,1)}, bf16[8,64,1024]{2,1,0:T(8,128)(2,1)S(1)}, u32[]{:S(2)}, u32[]{:S(2)}) collective-permute-start(bf16[8,64,1024]{2,1,0:T(8,128)(2,1)} %get-tuple-element.131), channel_id=1, source_target_pairs={{0,4},{2,6},{4,0},{6,2},{8,12},{10,14},{12,8},{14,10},{16,20},{18,... | collective-permute-start | bytes 3145736 | tf_op jit(solution)/shard_map/ppermute | solution.py:553
  102.9 26.9 %collective-permute-start.21 = (bf16[4,64,1024]{2,1,0:T(8,128)(2,1)}, bf16[4,64,1024]{2,1,0:T(8,128)(2,1)S(1)}, u32[]{:S(2)}, u32[]{:S(2)}) collective-permute-start(bf16[4,64,1024]{2,1,0:T(8,128)(2,1)} %get-tuple-element.134), channel_id=1, source_target_pairs={{0,4},{2,6},{4,0},{6,2},{8,12},{10,14},{12,8},{14,10},{16,20},{18,... | collective-permute-start | bytes 1572872 | tf_op jit(solution)/shard_map/ppermute | solution.py:553
  105.0 24.8 %collective-permute-start.22 = (bf16[4,64,1024]{2,1,0:T(8,128)(2,1)}, bf16[4,64,1024]{2,1,0:T(8,128)(2,1)S(1)}, u32[]{:S(2)}, u32[]{:S(2)}) collective-permute-start(bf16[4,64,1024]{2,1,0:T(8,128)(2,1)} %get-tuple-element.135), channel_id=1, source_target_pairs={{0,2},{2,0},{4,6},{6,4},{8,10},{10,8},{12,14},{14,12},{16,18},{18,... | collective-permute-start | bytes 1572872 | tf_op jit(solution)/shard_map/ppermute | solution.py:553
  129.8 8.7 %collective-permute-start.26 = (bf16[256,1024]{1,0:T(8,128)(2,1)S(1)}, bf16[256,1024]{1,0:T(8,128)(2,1)S(1)}, u32[]{:S(2)}, u32[]{:S(2)}) collective-permute-start(bf16[256,1024]{1,0:T(8,128)(2,1)S(1)} %copy-done.21), channel_id=1, source_target_pairs={{0,1},{1,0},{2,3},{3,2},{4,5},{5,4},{6,7},{7,6},{8,9},{9,8},{10,11... | collective-permute-start | bytes 1572872 | tf_op jit(solution)/shard_map/ppermute | solution.py:550
  129.9 6.5 %collective-permute-start.24 = (bf16[256,768]{1,0:T(8,128)(2,1)S(1)}, bf16[256,768]{1,0:T(8,128)(2,1)S(1)}, u32[]{:S(2)}, u32[]{:S(2)}) collective-permute-start(bf16[256,768]{1,0:T(8,128)(2,1)S(1)} %copy-done.35), channel_id=1, source_target_pairs={{0,1},{1,0},{2,3},{3,2},{4,5},{5,4},{6,7},{7,6},{8,9},{9,8},{10,11... | collective-permute-start | bytes 1179656 | tf_op jit(solution)/shard_map/ppermute | solution.py:550
  130.4 8.1 %collective-permute-start.25 = (bf16[256,768]{1,0:T(8,128)(2,1)}, bf16[256,768]{1,0:T(8,128)(2,1)S(1)}, u32[]{:S(2)}, u32[]{:S(2)}) collective-permute-start(bf16[256,768]{1,0:T(8,128)(2,1)} %get-tuple-element.157.refs_2_), channel_id=1, source_target_pairs={{0,1},{1,0},{2,3},{3,2},{4,5},{5,4},{6,7},{7,6},{8,9},{9,8},{10,11... | collective-permute-start | bytes 1179656 | tf_op jit(solution)/shard_map/ppermute | solution.py:550
  133.5 15.2 %collective-permute-start.23 = (bf16[2,64,2048]{2,1,0:T(8,128)(2,1)}, bf16[2,64,2048]{2,1,0:T(8,128)(2,1)}, u32[]{:S(2)}, u32[]{:S(2)}) collective-permute-start(bf16[2,64,2048]{2,1,0:T(8,128)(2,1)} %get-tuple-element.153), channel_id=1, source_target_pairs={{0,8},{2,10},{4,12},{6,14},{8,0},{10,2},{12,4},{14,6},{16,24},{18,... | collective-permute-start | bytes 1572872 | tf_op jit(solution)/shard_map/ppermute | solution.py:553
  134.9 16.0 %collective-permute-start.19 = (bf16[4,64,1024]{2,1,0:T(8,128)(2,1)}, bf16[4,64,1024]{2,1,0:T(8,128)(2,1)}, u32[]{:S(2)}, u32[]{:S(2)}) collective-permute-start(bf16[4,64,1024]{2,1,0:T(8,128)(2,1)} %get-tuple-element.149), channel_id=1, source_target_pairs={{0,4},{2,6},{4,0},{6,2},{8,12},{10,14},{12,8},{14,10},{16,20},{18,... | collective-permute-start | bytes 1572872 | tf_op jit(solution)/shard_map/ppermute | solution.py:553
  136.4 17.0 %collective-permute-start.20 = (bf16[4,64,1024]{2,1,0:T(8,128)(2,1)}, bf16[4,64,1024]{2,1,0:T(8,128)(2,1)}, u32[]{:S(2)}, u32[]{:S(2)}) collective-permute-start(bf16[4,64,1024]{2,1,0:T(8,128)(2,1)} %get-tuple-element.150), channel_id=1, source_target_pairs={{0,2},{2,0},{4,6},{6,4},{8,10},{10,8},{12,14},{14,12},{16,18},{18,... | collective-permute-start | bytes 1572872 | tf_op jit(solution)/shard_map/ppermute | solution.py:553
  146.4 31.3 %collective-permute-start.27 = (bf16[8,64,1024]{2,1,0:T(8,128)(2,1)}, bf16[8,64,1024]{2,1,0:T(8,128)(2,1)S(1)}, u32[]{:S(2)}, u32[]{:S(2)}) collective-permute-start(bf16[8,64,1024]{2,1,0:T(8,128)(2,1)} %get-tuple-element.165), channel_id=1, source_target_pairs={{0,2},{2,0},{4,6},{6,4},{8,10},{10,8},{12,14},{14,12},{16,18},{18,... | collective-permute-start | bytes 3145736 | tf_op jit(solution)/shard_map/ppermute | solution.py:553
  147.9 29.7 %collective-permute-start.28 = (bf16[8,64,1024]{2,1,0:T(8,128)(2,1)}, bf16[8,64,1024]{2,1,0:T(8,128)(2,1)S(1)}, u32[]{:S(2)}, u32[]{:S(2)}) collective-permute-start(bf16[8,64,1024]{2,1,0:T(8,128)(2,1)} %get-tuple-element.166), channel_id=1, source_target_pairs={{0,4},{2,6},{4,0},{6,2},{8,12},{10,14},{12,8},{14,10},{16,20},{18,... | collective-permute-start | bytes 3145736 | tf_op jit(solution)/shard_map/ppermute | solution.py:553
  148.7 37.8 %collective-permute-start.30 = (f32[8]{0:T(128)S(1)}, f32[8]{0:T(128)S(1)}, u32[]{:S(2)}, u32[]{:S(2)}) collective-permute-start(f32[8]{0:T(128)S(1)} %slice_bitcast_fusion.3), channel_id=1, source_target_pairs={{0,1},{1,0},{2,3},{3,2},{4,5},{5,4},{6,7},{7,6},{8,9},{9,8},{10,11... | collective-permute-start | bytes 104 | tf_op jit(solution)/shard_map/ppermute | solution.py:550
  150.9 17.4 %collective-permute-start.29 = (bf16[1,64,2048]{2,1,0:T(8,128)(2,1)}, bf16[1,64,2048]{2,1,0:T(8,128)(2,1)S(1)}, u32[]{:S(2)}, u32[]{:S(2)}) collective-permute-start(bf16[1,64,2048]{2,1,0:T(8,128)(2,1)} %get-tuple-element.168), channel_id=1, source_target_pairs={{0,16},{2,18},{4,20},{6,22},{8,24},{10,26},{12,28},{14,30},{16,0},... | collective-permute-start | bytes 786440 | tf_op jit(solution)/shard_map/ppermute | solution.py:553
  164.2 39.3 %all-to-all-start.2 = ((bf16[32,32,512]{2,1,0:T(8,128)(2,1)}), bf16[32,32,512]{2,1,0:T(8,128)(2,1)S(1)}, u32[]{:S(2)}, u32[]{:S(2)}) async-start(bf16[32,32,512]{2,1,0:T(8,128)(2,1)} %pad_maximum_fusion), calls=%async_computation.2 | async-start | bytes 2097152 | tf_op jit(solution)/shard_map/all_to_all | solution.py:578
  186.5 7.7 %collective-permute-start.31 = (bf16[10248]{0:T(1024)(128)(2,1)S(1)}, bf16[10248]{0:T(1024)(128)(2,1)S(1)}, u32[]{:S(2)}, u32[]{:S(2)}) collective-permute-start(bf16[10248]{0:T(1024)(128)(2,1)S(1)} %get-tuple-element.294), channel_id=1, source_target_pairs={{0,8},{2,10},{4,12},{6,14},{8,0},{10,2},{12,4},{14,6},{16,24},{18,... | collective-permute-start | bytes 61496 | tf_op jit(solution)/shard_map/ppermute | solution.py:553
  189.0 14.5 %collective-permute-start.34 = (bf16[4,64,1024]{2,1,0:T(8,128)(2,1)}, bf16[4,64,1024]{2,1,0:T(8,128)(2,1)S(1)}, u32[]{:S(2)}, u32[]{:S(2)}) collective-permute-start(bf16[4,64,1024]{2,1,0:T(8,128)(2,1)} %get-tuple-element.180), channel_id=1, source_target_pairs={{0,4},{2,6},{4,0},{6,2},{8,12},{10,14},{12,8},{14,10},{16,20},{18,... | collective-permute-start | bytes 1572872 | tf_op jit(solution)/shard_map/ppermute | solution.py:553
  189.1 14.4 %collective-permute-start.35 = (bf16[4,64,1024]{2,1,0:T(8,128)(2,1)}, bf16[4,64,1024]{2,1,0:T(8,128)(2,1)S(1)}, u32[]{:S(2)}, u32[]{:S(2)}) collective-permute-start(bf16[4,64,1024]{2,1,0:T(8,128)(2,1)} %get-tuple-element.181), channel_id=1, source_target_pairs={{0,2},{2,0},{4,6},{6,4},{8,10},{10,8},{12,14},{14,12},{16,18},{18,... | collective-permute-start | bytes 1572872 | tf_op jit(solution)/shard_map/ppermute | solution.py:553
  192.7 10.8 %collective-permute-start.33 = (bf16[2,64,2048]{2,1,0:T(8,128)(2,1)}, bf16[2,64,2048]{2,1,0:T(8,128)(2,1)S(1)}, u32[]{:S(2)}, u32[]{:S(2)}) collective-permute-start(bf16[2,64,2048]{2,1,0:T(8,128)(2,1)} %get-tuple-element.191), channel_id=1, source_target_pairs={{0,8},{2,10},{4,12},{6,14},{8,0},{10,2},{12,4},{14,6},{16,24},{18,... | collective-permute-start | bytes 1572872 | tf_op jit(solution)/shard_map/ppermute | solution.py:553
  194.5 5.1 %collective-permute-start.32 = (bf16[16392]{0:T(1024)(128)(2,1)S(1)}, bf16[16392]{0:T(1024)(128)(2,1)S(1)}, u32[]{:S(2)}, u32[]{:S(2)}) collective-permute-start(bf16[16392]{0:T(1024)(128)(2,1)S(1)} %pad_maximum_fusion.5), channel_id=1, source_target_pairs={{0,2},{2,0},{4,6},{6,4},{8,10},{10,8},{12,14},{14,12},{16,18},{18,... | collective-permute-start | bytes 98360 | tf_op jit(solution)/shard_map/ppermute | solution.py:553
  209.4 18.6 %collective-permute-start.39 = (bf16[1,64,2048]{2,1,0:T(8,128)(2,1)}, bf16[1,64,2048]{2,1,0:T(8,128)(2,1)S(1)}, u32[]{:S(2)}, u32[]{:S(2)}) collective-permute-start(bf16[1,64,2048]{2,1,0:T(8,128)(2,1)} %get-tuple-element.197), channel_id=1, source_target_pairs={{0,16},{2,18},{4,20},{6,22},{8,24},{10,26},{12,28},{14,30},{16,0},... | collective-permute-start | bytes 786440 | tf_op jit(solution)/shard_map/ppermute | solution.py:553
  210.5 17.4 %collective-permute-start.38 = (bf16[2,64,2048]{2,1,0:T(8,128)(2,1)}, bf16[2,64,2048]{2,1,0:T(8,128)(2,1)S(1)}, u32[]{:S(2)}, u32[]{:S(2)}) collective-permute-start(bf16[2,64,2048]{2,1,0:T(8,128)(2,1)} %get-tuple-element.195), channel_id=1, source_target_pairs={{0,8},{2,10},{4,12},{6,14},{8,0},{10,2},{12,4},{14,6},{16,24},{18,... | collective-permute-start | bytes 1572872 | tf_op jit(solution)/shard_map/ppermute | solution.py:553
  212.1 4.3 %collective-permute-start.36 = (bf16[28680]{0:T(1024)(128)(2,1)S(1)}, bf16[28680]{0:T(1024)(128)(2,1)S(1)}, u32[]{:S(2)}, u32[]{:S(2)}) collective-permute-start(bf16[28680]{0:T(1024)(128)(2,1)S(1)} %pad_maximum_fusion.4), channel_id=1, source_target_pairs={{0,4},{2,6},{4,0},{6,2},{8,12},{10,14},{12,8},{14,10},{16,20},{18,... | collective-permute-start | bytes 172088 | tf_op jit(solution)/shard_map/ppermute | solution.py:553
  216.6 8.5 %collective-permute-start.37 = (bf16[53256]{0:T(1024)(128)(2,1)S(1)}, bf16[53256]{0:T(1024)(128)(2,1)S(1)}, u32[]{:S(2)}, u32[]{:S(2)}) collective-permute-start(bf16[53256]{0:T(1024)(128)(2,1)S(1)} %pad_maximum_fusion.3), channel_id=1, source_target_pairs={{0,16},{2,18},{4,20},{6,22},{8,24},{10,26},{12,28},{14,30},{16,0},... | collective-permute-start | bytes 319544 | tf_op jit(solution)/shard_map/ppermute | solution.py:553
  231.0 4.2 %collective-permute-start.40 = (bf16[16,6144]{1,0:T(8,128)(2,1)S(1)}, bf16[16,6144]{1,0:T(8,128)(2,1)S(1)}, u32[]{:S(2)}, u32[]{:S(2)}) collective-permute-start(bf16[16,6144]{1,0:T(8,128)(2,1)S(1)} %reshape.417), channel_id=1, source_target_pairs={{0,1},{1,0},{2,3},{3,2},{4,5},{5,4},{6,7},{7,6},{8,9},{9,8},{10,11... | collective-permute-start | bytes 589832 | tf_op jit(solution)/shard_map/ppermute | solution.py:550
  231.8 16.2 %collective-permute-start.41 = (bf16[1,64,2048]{2,1,0:T(8,128)(2,1)}, bf16[1,64,2048]{2,1,0:T(8,128)(2,1)S(1)}, u32[]{:S(2)}, u32[]{:S(2)}) collective-permute-start(bf16[1,64,2048]{2,1,0:T(8,128)(2,1)} %get-tuple-element.201), channel_id=1, source_target_pairs={{0,16},{2,18},{4,20},{6,22},{8,24},{10,26},{12,28},{14,30},{16,0},... | collective-permute-start | bytes 786440 | tf_op jit(solution)/shard_map/ppermute | solution.py:553
  (54 other events, 257.0 us)

commit v4 on v3

--- a/solution.py
+++ b/solution.py
@@ -666,7 +666,7 @@
     ]
     h1, qn, kn, vn, rq, rk, probs, mixed0, mixed1, attn, middle, h2, act0, *more = local_call(
         functools.partial(forward_kernel, share if whole_tiles else 0),
-        56,
+        61,
         kept + [array(row_len, width), array(6, width, kind=f32)],
         scratch(kept)
         + [
@@ -708,7 +708,7 @@
         ] * 2
         outs = local_call(
             functools.partial(grad_kernel, pieces),
-            56,
+            61,
             [array(1, width, kind=f32)] * count
             + [array(1, source[2].shape[1], kind=f32) for source in sources]
             + kept,
@@ -740,7 +740,7 @@
         kept = [array(groups // 4, part, columns)] * 2 + [array(groups // 4, part, 2 * columns)]
         sent_a, sent_b, own = local_call(
             functools.partial(second_kernel, pieces),
-            56,
+            61,
             kept,
             scratch(ins)
             + scratch(kept)
@@ -761,7 +761,7 @@
         rows, _, columns = own.shape
         sent, own = local_call(
             functools.partial(third_kernel, bit),
-            56,
+            61,
             [
                 array(rows // 2, part, columns),
                 array(rows // 2, part, columns, kind=f32 if bit == bits - 1 else bf16),
@@ -792,7 +792,7 @@
     branch_ins = [act0, *act1, grad_out, middle]
     pre0, *pre1, output, branch_mods = local_call(
         hidden_back_kernel,
-        56,
+        61,
         pre_kept + [array(row_len, width), array(1, width, kind=f32)],
         scratch(pre_kept)
         + [vmem((2, row_len, hidden), bf16), vmem((2, hidden, width), bf16)]
@@ -845,7 +845,7 @@
     ]
     middle_grad, attn_grad, qkv_grad0, qkv1a, qkv1b, row_mods = local_call(
         row_back_kernel,
-        56,
+        61,
         row_kept,
         scratch(row_kept)
         + scratch(row_ins)
@@ -878,7 +878,7 @@
     ]
     tokens_grad, end_mods = local_call(
         input_back_kernel,
-        56,
+        61,
         [array(row_len, width), array(2, width, kind=f32)],
         scratch(end_ins) + [vmem((row_len, width), f32), dma((11,))],
         "v" + "h" * 11,

time: 254 us -> 253 us (level)
    unnamed x131 -> x101, local copies, waits for them, and re-layouts: 11.3 us -> 8.43 us
  transfers between devices with their start and end apart: 45 -> 45, of which waited for: 14 -> 14; matrix products, arithmetic and copies ran while one was open for 14% -> 15% of each run, Pallas kernels for 38% -> 38%
where the time goes in v4:
time: 253 us; the launch traced here: 249 us
  Pallas kernels  101 us (40%)
  waiting for transfers between devices  55.8 us (22%)
  starting transfers between devices  45.3 us (18%)
  local copies, waits for them, and re-layouts  27.7 us (11%)
  other arithmetic  14.1 us (6%)
  matrix products  3.18 us (1%)
    pallas_call x16, Pallas kernels, local_call(): pl.pallas_call(kernel, out_shape=outs, in_specs=[places[kind] for kind in...  101 us
    ppermute x22, waiting for transfers between devices, flip(): lax.ppermute(values, 'dp', [(i, i ^ 1 << bit) for i in range(groups)])  40.6 us
    ppermute x22, starting transfers between devices, flip(): lax.ppermute(values, 'dp', [(i, i ^ 1 << bit) for i in range(groups)])  26.8 us
    all_to_all x3, starting transfers between devices, exchange(): lax.all_to_all(values, ('dp', 'mp'), split_axis=0, concat_axis=0, tiled=T...  13.7 us
    all_to_all x3, waiting for transfers between devices, exchange(): lax.all_to_all(values, ('dp', 'mp'), split_axis=0, concat_axis=0, tiled=T...  10.3 us
    unnamed x101, local copies, waits for them, and re-layouts  8.43 us
  transfers between devices with their start and end apart: 45, of which 14 were waited for; matrix products, arithmetic and copies ran while one was open for 15% of the time, Pallas kernels for 38%

profile of v4, /device:TPU:0, one launch (start us, length us, event | category | flops | bytes accessed | tf_op | source)
XLA Modules:
  0.0 249.0 jit_solution(6288126916227500413)
XLA Ops:
  4.7 7.0 %all-to-all-start = ((bf16[32,24,512]{2,1,0:T(8,128)(2,1)}), bf16[32,24,512]{2,1,0:T(8,128)(2,1)S(1)}, u32[]{:S(2)}, u32[]{:S(2)}) async-start(bf16[32,24,512]{2,1,0:T(8,128)(2,1)} %pad_maximum_fusion.1), calls=%async_computation | async-start | bytes 1572864 | tf_op jit(solution)/shard_map/all_to_all | solution.py:578
  12.2 3.0 %slice_bitcast_fusion = (bf16[1024,512]{1,0:T(8,128)(2,1)S(1)}, bf16[1024,512]{1,0:T(8,128)(2,1)S(1)}, bf16[1024,512]{1,0:T(8,128)(2,1)}) fusion(bf16[1024,3,512]{2,0,1:T(8,128)(2,1)} %param.25), kind=kLoop, calls=%fused_computation.3 | loop fusion | bytes 6291456 | tf_op jit(solution)/shard_map/squeeze | solution.py:601
  17.5 1.9 copy.66
  22.1 10.2 %all-to-all-done.arrived = bf16[32,24,512]{2,1,0:T(8,128)(2,1)S(1)} async-done(((bf16[32,24,512]{2,1,0:T(8,128)(2,1)}), bf16[32,24,512]{2,1,0:T(8,128)(2,1)S(1)}, u32[]{:S(2)}, u32[]{:S(2)}) %all-to-all-start) | async-done | bytes 786464 | tf_op jit(solution)/shard_map/all_to_all | solution.py:578
  32.4 3.9 %all-to-all-start.1 = ((bf16[32,16,512]{2,1,0:T(8,128)(2,1)}), bf16[32,16,512]{2,1,0:T(8,128)(2,1)}, u32[]{:S(2)}, u32[]{:S(2)}) async-start(bf16[32,16,512]{2,1,0:T(8,128)(2,1)} %bitcast.135), calls=%async_computation.1 | async-start | bytes 1048576 | tf_op jit(solution)/shard_map/all_to_all | solution.py:578
  37.6 17.1 %shard_map.281 = (bf16[256,1024]{1,0:T(8,128)(2,1)}, bf16[2,256,512]{2,1,0:T(8,128)(2,1)}, bf16[2,256,512]{2,1,0:T(8,128)(2,1)}, bf16[2,256,512]{2,1,0:T(8,128)(...) custom-call(bf16[32,24,512]{2,1,0:T(8,128)(2,1)} %copy-done.6, ...), custom_call_target="tpu_custom_call" | custom-call | flops 1 | bytes 1 | tf_op jit(solution)/shard_map/pallas_call | solution.py:486
  54.7 1.7 copy.67
  59.6 1.7 collective-permute-done.7.refs_3_.refs_2_
  62.8 5.7 %shard_map.282 = (f32[1,1024]{1,0:T(1,128)}, f32[1,2048]{1,0:T(1,128)}, bf16[16,64,512]{2,1,0:T(8,128)(2,1)}, bf16[8,64,1024]{2,1,0:T(8,128)(2,1)}, bf16[8,64,1024]{2,1,0:T(8,128)(2,1)}) custom-call(s32[4]{0:T(128)} %pad_add_fusion.bit_ref, bf16[256,1024]{1,0:T(8,128)(2,1)} %copy-done.5, bf16[256,1024]{1,0:T(8,128)(2,1)} %copy-done.26, ...), custom_call_target="tpu_custom_call" | custom-call | flops 1 | bytes 1 | tf_op jit(solution)/shard_map/pallas_call | solution.py:486
  68.5 1.8 collective-permute-start.13
  70.3 1.5 collective-permute-start.14
  72.4 10.1 %shard_map.283 = (bf16[256,2048]{1,0:T(8,128)(2,1)}, bf16[256,1024]{1,0:T(8,128)(2,1)}, bf16[256,1024]{1,0:T(8,128)(2,1)}, bf16[256,1024]{1,0:T(8,128)(2,1)}, f32[1,1024]{1,0:T(1,128)}) custom-call(bf16[256,1024]{1,0:T(8,128)(2,1)} %copy-done.5, f32[6,1024]{1,0:T(8,128)} %get-tuple-element.110.mods, f32[1,1024]{1,0:T(1,128)} %broadcast_select_fusion.6.fc2_bias, ...), custom_call_target="tpu_custom_call" | custom-call | flops 1 | bytes 1 | tf_op jit(solution)/shard_map/pallas_call | solution.py:486
  83.1 1.6 collective-permute-done.15.refs_3_.refs_2_
  86.2 5.7 %shard_map.284 = (f32[1,1024]{1,0:T(1,128)}, f32[1,2048]{1,0:T(1,128)}, bf16[16,64,512]{2,1,0:T(8,128)(2,1)}, bf16[8,64,1024]{2,1,0:T(8,128)(2,1)}, bf16[8,64,1024]{2,1,0:T(8,128)(2,1)}) custom-call(s32[4]{0:T(128)} %pad_add_fusion.bit_ref, bf16[256,1024]{1,0:T(8,128)(2,1)} %get-tuple-element.119.refs_0_, bf16[256,1024]{1,0:T(8,128)(2,1)} %collective-permute-done.10.refs_1_, ...), custom_call_target="tpu_custom_call" | custom-call | flops 1 | bytes 1 | tf_op jit(solution)/shard_map/pallas_call | solution.py:486
  93.0 1.4 collective-permute-done.13.refs_4_
  94.3 1.7 collective-permute-done.14.refs_5_
  96.1 5.4 %shard_map.285 = (bf16[4,64,1024]{2,1,0:T(8,128)(2,1)}, bf16[4,64,1024]{2,1,0:T(8,128)(2,1)}, bf16[4,64,2048]{2,1,0:T(8,128)(2,1)}) custom-call(s32[4]{0:T(128)} %pad_add_fusion.bit_ref, bf16[16,64,512]{2,1,0:T(8,128)(2,1)} %get-tuple-element.127.refs_0_, bf16[256,2048]{1,0:T(8,128)(2,1)} %get-tuple-element.112.refs_2_.refs_4_.refs_1_, ...), custom_call_target="tpu_custom_call" | custom-call | flops 3000000000 | bytes 1 | tf_op jit(solution)/shard_map/pallas_call | solution.py:486
  101.5 2.1 collective-permute-start.21
  103.6 16.0 %shard_map.286 = (f32[256,1024]{1,0:T(8,128)}, bf16[256,1024]{1,0:T(8,128)(2,1)}, bf16[256,1536]{1,0:T(8,128)(2,1)}, bf16[256,768]{1,0:T(8,128)(2,1)}, bf16[256,768]{1,0:T(8,128)(2,1)}, /*index=5*/f32[4,1024]{1,0:T(4,128)}) custom-call(f32[6,1024]{1,0:T(8,128)} %get-tuple-element.110.mods, f32[2,512]{1,0:T(2,128)} %pad_maximum_fusion.10.mult, ...), custom_call_target="tpu_custom_call" | custom-call | flops 1 | bytes 1 | tf_op jit(solution)/shard_map/pallas_call | solution.py:486
  121.0 5.4 %shard_map.287 = (bf16[4,64,1024]{2,1,0:T(8,128)(2,1)}, bf16[4,64,1024]{2,1,0:T(8,128)(2,1)}, bf16[4,64,2048]{2,1,0:T(8,128)(2,1)}) custom-call(s32[4]{0:T(128)} %pad_add_fusion.bit_ref, bf16[16,64,512]{2,1,0:T(8,128)(2,1)} %get-tuple-element.145.refs_0_, bf16[256,2048]{1,0:T(8,128)(2,1)} %get-tuple-element.136.refs_2_.refs_0_.refs_1_, ...), custom_call_target="tpu_custom_call" | custom-call | flops 1 | bytes 1 | tf_op jit(solution)/shard_map/pallas_call | solution.py:486
  126.5 2.9 %collective-permute-done.21.refs_0_ = bf16[4,64,1024]{2,1,0:T(8,128)(2,1)S(1)} collective-permute-done((bf16[4,64,1024]{2,1,0:T(8,128)(2,1)}, bf16[4,64,1024]{2,1,0:T(8,128)(2,1)S(1)}, u32[]{:S(2)}, u32[]{:S(2)}) %collective-permute-start.21) | collective-permute-done | bytes 524320 | tf_op jit(solution)/shard_map/ppermute | solution.py:553
  130.1 2.7 %shard_map.288 = (bf16[2,64,2048]{2,1,0:T(8,128)(2,1)}, bf16[2,64,2048]{2,1,0:T(8,128)(2,1)}) custom-call(s32[4]{0:T(128)} %pad_add_fusion.bit_ref, bf16[4,64,2048]{2,1,0:T(8,128)(2,1)} %get-tuple-element.151.own, bf16[4,64,1024]{2,1,0:T(8,128)(2,1)} %copy-done.21, bf16[4,64,1024]{2,1,0:T(8,128)(2,1)} %collective-permute-done.22.refs_1_), custom_call_target="tpu_custom_call" | custom-call | flops 1 | bytes 1 | tf_op jit(solution)/shard_map/pallas_call | solution.py:486
  132.9 1.5 collective-permute-start.23
  134.4 1.4 collective-permute-start.19
  136.5 1.4 reshape.407
  138.8 7.0 %shard_map.289 = (f32[1,1024]{1,0:T(1,128)}, f32[1,1024]{1,0:T(1,128)}, f32[1,1536]{1,0:T(1,128)}, f32[1,512]{1,0:T(1,128)}, bf16[16,64,512]{2,1,0:T(8,128)(2,1)...) custom-call(s32[4]{0:T(128)} %pad_add_fusion.bit_ref, ...), custom_call_target="tpu_custom_call" | custom-call | flops 1 | bytes 1 | tf_op jit(solution)/shard_map/pallas_call | solution.py:486
  145.8 1.5 collective-permute-start.27
  148.2 2.2 shard_map.290
  150.3 2.4 collective-permute-start.29
  153.5 7.5 %shard_map.291 = (bf16[256,1024]{1,0:T(8,128)(2,1)}, f32[2,1024]{1,0:T(2,128)}) custom-call(f32[6,1024]{1,0:T(8,128)} %get-tuple-element.110.mods, bf16[256,1536]{1,0:T(8,128)(2,1)} %get-tuple-element.169.refs_2_.refs_0_, bf16[256,768]{1,0:T(8,128)(2,1)} %get-tuple-element.156.refs_1_, bf16[256,768]{1,0:T(8,128)(2,1)} %get-tuple-element.157.refs_2_, ...), custom_call_target="tpu_custom_call" | custom-call | flops 2000000000 | bytes 1 | tf_op jit(solution)/shard_map/pallas_call | solution.py:486
  160.9 1.4 reshape.409
  163.6 2.8 %all-to-all-start.2 = ((bf16[32,32,512]{2,1,0:T(8,128)(2,1)}), bf16[32,32,512]{2,1,0:T(8,128)(2,1)S(1)}, u32[]{:S(2)}, u32[]{:S(2)}) async-start(bf16[32,32,512]{2,1,0:T(8,128)(2,1)} %pad_maximum_fusion), calls=%async_computation.2 | async-start | bytes 2097152 | tf_op jit(solution)/shard_map/all_to_all | solution.py:578
  167.7 9.5 %collective-permute-done.27.refs_7_ = bf16[8,64,1024]{2,1,0:T(8,128)(2,1)S(1)} collective-permute-done((bf16[8,64,1024]{2,1,0:T(8,128)(2,1)}, bf16[8,64,1024]{2,1,0:T(8,128)(2,1)S(1)}, u32[]{:S(2)}, u32[]{:S(2)}) %collective-permute-start.27) | collective-permute-done | bytes 1048608 | tf_op jit(solution)/shard_map/ppermute | solution.py:553
  178.2 6.3 %shard_map.292 = (bf16[4,64,1024]{2,1,0:T(8,128)(2,1)}, bf16[4,64,1024]{2,1,0:T(8,128)(2,1)}, bf16[4,64,2048]{2,1,0:T(8,128)(2,1)}) custom-call(s32[4]{0:T(128)} %pad_add_fusion.bit_ref, bf16[16,64,512]{2,1,0:T(8,128)(2,1)} %get-tuple-element.176.refs_0_, bf16[16,64,512]{2,1,0:T(8,128)(2,1)} %get-tuple-element.177.refs_1_, ...), custom_call_target="tpu_custom_call" | custom-call | flops 1 | bytes 1 | tf_op jit(solution)/shard_map/pallas_call | solution.py:486
  185.8 1.9 add_bitcast_fusion
  189.2 2.7 %shard_map.293 = (bf16[2,64,2048]{2,1,0:T(8,128)(2,1)}, bf16[2,64,2048]{2,1,0:T(8,128)(2,1)}) custom-call(s32[4]{0:T(128)} %pad_add_fusion.bit_ref, bf16[4,64,2048]{2,1,0:T(8,128)(2,1)} %get-tuple-element.187.own, bf16[4,64,1024]{2,1,0:T(8,128)(2,1)} %collective-permute-done.19.refs_0_, bf16[4,64,1024]{2,1,0:T(8,128)(2,1)} %collective-permute-done.20.refs_1_), custom_call_target="tpu_custom_call" | custom-call | flops 1 | bytes 1 | tf_op jit(solution)/shard_map/pallas_call | solution.py:486
  192.0 2.0 collective-permute-start.33
  195.1 3.5 %collective-permute-done.32 = bf16[16392]{0:T(1024)(128)(2,1)S(1)} collective-permute-done((bf16[16392]{0:T(1024)(128)(2,1)S(1)}, bf16[16392]{0:T(1024)(128)(2,1)S(1)}, u32[]{:S(2)}, u32[]{:S(2)}) %collective-permute-start.32) | collective-permute-done | bytes 32816 | tf_op jit(solution)/shard_map/ppermute | solution.py:553
  198.8 3.9 %collective-permute-done.33.refs_0_ = bf16[2,64,2048]{2,1,0:T(8,128)(2,1)} collective-permute-done((bf16[2,64,2048]{2,1,0:T(8,128)(2,1)}, bf16[2,64,2048]{2,1,0:T(8,128)(2,1)}, u32[]{:S(2)}, u32[]{:S(2)}) %collective-permute-start.33) | collective-permute-done | bytes 524320 | tf_op jit(solution)/shard_map/ppermute | solution.py:553
  203.7 2.7 %shard_map.294 = (bf16[2,64,2048]{2,1,0:T(8,128)(2,1)}, bf16[2,64,2048]{2,1,0:T(8,128)(2,1)}) custom-call(s32[4]{0:T(128)} %pad_add_fusion.bit_ref, bf16[4,64,2048]{2,1,0:T(8,128)(2,1)} %get-tuple-element.192.own, bf16[4,64,1024]{2,1,0:T(8,128)(2,1)} %copy-done.19, bf16[4,64,1024]{2,1,0:T(8,128)(2,1)} %copy-done.20), custom_call_target="tpu_custom_call" | custom-call | flops 1 | bytes 1 | tf_op jit(solution)/shard_map/pallas_call | solution.py:486
  206.4 2.2 shard_map.295
  209.7 2.0 collective-permute-start.38
  214.6 1.4 collective-permute-done.36
  217.0 7.1 %collective-permute-done.37 = bf16[53256]{0:T(1024)(128)(2,1)S(1)} collective-permute-done((bf16[53256]{0:T(1024)(128)(2,1)S(1)}, bf16[53256]{0:T(1024)(128)(2,1)S(1)}, u32[]{:S(2)}, u32[]{:S(2)}) %collective-permute-start.37) | collective-permute-done | bytes 106544 | tf_op jit(solution)/shard_map/ppermute | solution.py:553
  227.0 2.2 shard_map.296
  229.2 1.8 add_bitcast_fusion.1
  231.0 3.4 %collective-permute-start.41 = (bf16[1,64,2048]{2,1,0:T(8,128)(2,1)}, bf16[1,64,2048]{2,1,0:T(8,128)(2,1)S(1)}, u32[]{:S(2)}, u32[]{:S(2)}) collective-permute-start(bf16[1,64,2048]{2,1,0:T(8,128)(2,1)} %get-tuple-element.201), channel_id=1, source_target_pairs={{0,16},{2,18},{4,20},{6,22},{8,24},{10,26},{12,28},{14,30},{16,0},... | collective-permute-start | bytes 786440 | tf_op jit(solution)/shard_map/ppermute | solution.py:553
  238.2 9.0 %collective-permute-done.41 = bf16[1,64,2048]{2,1,0:T(8,128)(2,1)S(1)} collective-permute-done((bf16[1,64,2048]{2,1,0:T(8,128)(2,1)}, bf16[1,64,2048]{2,1,0:T(8,128)(2,1)S(1)}, u32[]{:S(2)}, u32[]{:S(2)}) %collective-permute-start.41) | collective-permute-done | bytes 262176 | tf_op jit(solution)/shard_map/ppermute | solution.py:553
  (276 shorter events, 45.6 us)
Async XLA Ops:
  0.7 36.9 %collective-permute-start.5 = (bf16[1024,2048]{1,0:T(8,128)(2,1)}, bf16[1024,2048]{1,0:T(8,128)(2,1)}, u32[]{:S(2)}, u32[]{:S(2)}) collective-permute-start(bf16[1024,2048]{1,0:T(8,128)(2,1)} %refs_1_.1), channel_id=1, source_target_pairs={{0,1},{1,0},{2,3},{3,2},{4,5},{5,4},{6,7},{7,6},{8,9},{9,8},{10,11... | collective-permute-start | bytes 12582920 | tf_op jit(solution)/shard_map/ppermute | solution.py:550
  4.7 27.6 %all-to-all-start = ((bf16[32,24,512]{2,1,0:T(8,128)(2,1)}), bf16[32,24,512]{2,1,0:T(8,128)(2,1)S(1)}, u32[]{:S(2)}, u32[]{:S(2)}) async-start(bf16[32,24,512]{2,1,0:T(8,128)(2,1)} %pad_maximum_fusion.1), calls=%async_computation | async-start | bytes 1572864 | tf_op jit(solution)/shard_map/all_to_all | solution.py:578
  11.9 7.5 %collective-permute-start = (f32[7176]{0:T(1024)S(1)}, f32[7176]{0:T(1024)S(1)}, u32[]{:S(2)}, u32[]{:S(2)}) collective-permute-start(f32[7176]{0:T(1024)S(1)} %concatenate.132), channel_id=1, source_target_pairs={{0,1},{1,0},{2,3},{3,2},{4,5},{5,4},{6,7},{7,6},{8,9},{9,8},{10,11... | collective-permute-start | bytes 86120 | tf_op jit(solution)/shard_map/ppermute | solution.py:550
  15.3 22.3 %copy-start.2 = (bf16[1024,512]{1,0:T(8,128)(2,1)}, bf16[1024,512]{1,0:T(8,128)(2,1)S(1)}, u32[]{:S(2)}) copy-start(bf16[1024,512]{1,0:T(8,128)(2,1)S(1)} %get-tuple-element.266.refs_2_.refs_7_) | copy-start | bytes 3145732
  15.3 22.3 %copy-start.3 = (bf16[1024,512]{1,0:T(8,128)(2,1)}, bf16[1024,512]{1,0:T(8,128)(2,1)S(1)}, u32[]{:S(2)}) copy-start(bf16[1024,512]{1,0:T(8,128)(2,1)S(1)} %get-tuple-element.267.refs_0_.refs_5_) | copy-start | bytes 3145732
  15.3 6.0 %collective-permute-start.1 = (bf16[1024,512]{1,0:T(8,128)(2,1)S(1)}, bf16[1024,512]{1,0:T(8,128)(2,1)}, u32[]{:S(2)}, u32[]{:S(2)}) collective-permute-start(bf16[1024,512]{1,0:T(8,128)(2,1)S(1)} %get-tuple-element.267.refs_0_.refs_5_), channel_id=1, source_target_pairs={{0,1},{1,0},{2,3},{3,2},{4,5},{5,4},{6,7},{7,6},{8,9},{9,8},{10,11... | collective-permute-start | bytes 3145736 | tf_op jit(solution)/shard_map/ppermute | solution.py:550
  15.5 22.0 %collective-permute-start.2 = (bf16[1024,512]{1,0:T(8,128)(2,1)}, bf16[1024,512]{1,0:T(8,128)(2,1)}, u32[]{:S(2)}, u32[]{:S(2)}) collective-permute-start(bf16[1024,512]{1,0:T(8,128)(2,1)} %get-tuple-element.268.refs_1_.refs_6_), channel_id=1, source_target_pairs={{0,1},{1,0},{2,3},{3,2},{4,5},{5,4},{6,7},{7,6},{8,9},{9,8},{10,11... | collective-permute-start | bytes 3145736 | tf_op jit(solution)/shard_map/ppermute | solution.py:550
  15.8 56.6 %collective-permute-start.12 = (bf16[2048,1024]{1,0:T(8,128)(2,1)}, bf16[2048,1024]{1,0:T(8,128)(2,1)}, u32[]{:S(2)}, u32[]{:S(2)}) collective-permute-start(bf16[2048,1024]{1,0:T(8,128)(2,1)} %refs_2_.1), channel_id=1, source_target_pairs={{0,1},{1,0},{2,3},{3,2},{4,5},{5,4},{6,7},{7,6},{8,9},{9,8},{10,11... | collective-permute-start | bytes 12582920 | tf_op jit(solution)/shard_map/ppermute | solution.py:550
  19.4 18.1 %collective-permute-start.3 = (bf16[1024,512]{1,0:T(8,128)(2,1)S(1)}, bf16[1024,512]{1,0:T(8,128)(2,1)}, u32[]{:S(2)}, u32[]{:S(2)}) collective-permute-start(bf16[1024,512]{1,0:T(8,128)(2,1)S(1)} %get-tuple-element.266.refs_2_.refs_7_), channel_id=1, source_target_pairs={{0,1},{1,0},{2,3},{3,2},{4,5},{5,4},{6,7},{7,6},{8,9},{9,8},{10,11... | collective-permute-start | bytes 3145736 | tf_op jit(solution)/shard_map/ppermute | solution.py:550
  21.2 16.3 %collective-permute-start.4 = (bf16[512,1024]{1,0:T(8,128)(2,1)}, bf16[512,1024]{1,0:T(8,128)(2,1)}, u32[]{:S(2)}, u32[]{:S(2)}) collective-permute-start(bf16[512,1024]{1,0:T(8,128)(2,1)} %refs_8_.3), channel_id=1, source_target_pairs={{0,1},{1,0},{2,3},{3,2},{4,5},{5,4},{6,7},{7,6},{8,9},{9,8},{10,11... | collective-permute-start | bytes 3145736 | tf_op jit(solution)/shard_map/ppermute | solution.py:550
  32.4 22.4 %all-to-all-start.1 = ((bf16[32,16,512]{2,1,0:T(8,128)(2,1)}), bf16[32,16,512]{2,1,0:T(8,128)(2,1)}, u32[]{:S(2)}, u32[]{:S(2)}) async-start(bf16[32,16,512]{2,1,0:T(8,128)(2,1)} %bitcast.135), calls=%async_computation.1 | async-start | bytes 1048576 | tf_op jit(solution)/shard_map/all_to_all | solution.py:578
  57.4 2.0 collective-permute-start.6
  57.6 3.6 %collective-permute-start.7 = (bf16[256,1024]{1,0:T(8,128)(2,1)S(1)}, bf16[256,1024]{1,0:T(8,128)(2,1)S(1)}, u32[]{:S(2)}, u32[]{:S(2)}) collective-permute-start(bf16[256,1024]{1,0:T(8,128)(2,1)S(1)} %copy-done.18), channel_id=1, source_target_pairs={{0,1},{1,0},{2,3},{3,2},{4,5},{5,4},{6,7},{7,6},{8,9},{9,8},{10,11... | collective-permute-start | bytes 1572872 | tf_op jit(solution)/shard_map/ppermute | solution.py:550
  58.0 4.8 %collective-permute-start.8 = (bf16[256,1024]{1,0:T(8,128)(2,1)}, bf16[256,1024]{1,0:T(8,128)(2,1)}, u32[]{:S(2)}, u32[]{:S(2)}) collective-permute-start(bf16[256,1024]{1,0:T(8,128)(2,1)} %get-tuple-element.115.refs_6_), channel_id=1, source_target_pairs={{0,1},{1,0},{2,3},{3,2},{4,5},{5,4},{6,7},{7,6},{8,9},{9,8},{10,11... | collective-permute-start | bytes 1572872 | tf_op jit(solution)/shard_map/ppermute | solution.py:550
  58.2 12.1 %collective-permute-start.11 = (bf16[256,512]{1,0:T(8,128)(2,1)}, bf16[256,512]{1,0:T(8,128)(2,1)S(1)}, u32[]{:S(2)}, u32[]{:S(2)}) collective-permute-start(bf16[256,512]{1,0:T(8,128)(2,1)} %get-tuple-element.120), channel_id=1, source_target_pairs={{0,1},{1,0},{2,3},{3,2},{4,5},{5,4},{6,7},{7,6},{8,9},{9,8},{10,11... | collective-permute-start | bytes 786440 | tf_op jit(solution)/shard_map/ppermute | solution.py:550
  59.4 13.0 %collective-permute-start.10 = (bf16[256,1024]{1,0:T(8,128)(2,1)}, bf16[256,1024]{1,0:T(8,128)(2,1)}, u32[]{:S(2)}, u32[]{:S(2)}) collective-permute-start(bf16[256,1024]{1,0:T(8,128)(2,1)} %get-tuple-element.119.refs_0_), channel_id=1, source_target_pairs={{0,1},{1,0},{2,3},{3,2},{4,5},{5,4},{6,7},{7,6},{8,9},{9,8},{10,11... | collective-permute-start | bytes 1572872 | tf_op jit(solution)/shard_map/ppermute | solution.py:550
  62.0 10.3 %collective-permute-start.9 = (bf16[256,1024]{1,0:T(8,128)(2,1)S(1)}, bf16[256,1024]{1,0:T(8,128)(2,1)S(1)}, u32[]{:S(2)}, u32[]{:S(2)}) collective-permute-start(bf16[256,1024]{1,0:T(8,128)(2,1)S(1)} %copy-done.16), channel_id=1, source_target_pairs={{0,1},{1,0},{2,3},{3,2},{4,5},{5,4},{6,7},{7,6},{8,9},{9,8},{10,11... | collective-permute-start | bytes 1572872 | tf_op jit(solution)/shard_map/ppermute | solution.py:550
  68.5 25.8 %collective-permute-start.13 = (bf16[8,64,1024]{2,1,0:T(8,128)(2,1)}, bf16[8,64,1024]{2,1,0:T(8,128)(2,1)}, u32[]{:S(2)}, u32[]{:S(2)}) collective-permute-start(bf16[8,64,1024]{2,1,0:T(8,128)(2,1)} %get-tuple-element.116), channel_id=1, source_target_pairs={{0,2},{2,0},{4,6},{6,4},{8,10},{10,8},{12,14},{14,12},{16,18},{18,... | collective-permute-start | bytes 3145736 | tf_op jit(solution)/shard_map/ppermute | solution.py:553
  70.3 25.8 %collective-permute-start.14 = (bf16[8,64,1024]{2,1,0:T(8,128)(2,1)}, bf16[8,64,1024]{2,1,0:T(8,128)(2,1)}, u32[]{:S(2)}, u32[]{:S(2)}) collective-permute-start(bf16[8,64,1024]{2,1,0:T(8,128)(2,1)} %get-tuple-element.117), channel_id=1, source_target_pairs={{0,4},{2,6},{4,0},{6,2},{8,12},{10,14},{12,8},{14,10},{16,20},{18,... | collective-permute-start | bytes 3145736 | tf_op jit(solution)/shard_map/ppermute | solution.py:553
  82.5 2.2 collective-permute-start.15
  82.6 2.9 %collective-permute-start.16 = (bf16[256,1024]{1,0:T(8,128)(2,1)}, bf16[256,1024]{1,0:T(8,128)(2,1)S(1)}, u32[]{:S(2)}, u32[]{:S(2)}) collective-permute-start(bf16[256,1024]{1,0:T(8,128)(2,1)} %get-tuple-element.129.refs_3_), channel_id=1, source_target_pairs={{0,1},{1,0},{2,3},{3,2},{4,5},{5,4},{6,7},{7,6},{8,9},{9,8},{10,11... | collective-permute-start | bytes 1572872 | tf_op jit(solution)/shard_map/ppermute | solution.py:550
  92.0 27.6 %collective-permute-start.17 = (bf16[8,64,1024]{2,1,0:T(8,128)(2,1)}, bf16[8,64,1024]{2,1,0:T(8,128)(2,1)S(1)}, u32[]{:S(2)}, u32[]{:S(2)}) collective-permute-start(bf16[8,64,1024]{2,1,0:T(8,128)(2,1)} %get-tuple-element.130), channel_id=1, source_target_pairs={{0,2},{2,0},{4,6},{6,4},{8,10},{10,8},{12,14},{14,12},{16,18},{18,... | collective-permute-start | bytes 3145736 | tf_op jit(solution)/shard_map/ppermute | solution.py:553
  92.6 27.0 %collective-permute-start.18 = (bf16[8,64,1024]{2,1,0:T(8,128)(2,1)}, bf16[8,64,1024]{2,1,0:T(8,128)(2,1)S(1)}, u32[]{:S(2)}, u32[]{:S(2)}) collective-permute-start(bf16[8,64,1024]{2,1,0:T(8,128)(2,1)} %get-tuple-element.131), channel_id=1, source_target_pairs={{0,4},{2,6},{4,0},{6,2},{8,12},{10,14},{12,8},{14,10},{16,20},{18,... | collective-permute-start | bytes 3145736 | tf_op jit(solution)/shard_map/ppermute | solution.py:553
  101.5 27.9 %collective-permute-start.21 = (bf16[4,64,1024]{2,1,0:T(8,128)(2,1)}, bf16[4,64,1024]{2,1,0:T(8,128)(2,1)S(1)}, u32[]{:S(2)}, u32[]{:S(2)}) collective-permute-start(bf16[4,64,1024]{2,1,0:T(8,128)(2,1)} %get-tuple-element.134), channel_id=1, source_target_pairs={{0,4},{2,6},{4,0},{6,2},{8,12},{10,14},{12,8},{14,10},{16,20},{18,... | collective-permute-start | bytes 1572872 | tf_op jit(solution)/shard_map/ppermute | solution.py:553
  103.6 25.8 %collective-permute-start.22 = (bf16[4,64,1024]{2,1,0:T(8,128)(2,1)}, bf16[4,64,1024]{2,1,0:T(8,128)(2,1)}, u32[]{:S(2)}, u32[]{:S(2)}) collective-permute-start(bf16[4,64,1024]{2,1,0:T(8,128)(2,1)} %get-tuple-element.135), channel_id=1, source_target_pairs={{0,2},{2,0},{4,6},{6,4},{8,10},{10,8},{12,14},{14,12},{16,18},{18,... | collective-permute-start | bytes 1572872 | tf_op jit(solution)/shard_map/ppermute | solution.py:553
  129.4 8.7 %collective-permute-start.26 = (bf16[256,1024]{1,0:T(8,128)(2,1)}, bf16[256,1024]{1,0:T(8,128)(2,1)}, u32[]{:S(2)}, u32[]{:S(2)}) collective-permute-start(bf16[256,1024]{1,0:T(8,128)(2,1)} %get-tuple-element.163.refs_5_), channel_id=1, source_target_pairs={{0,1},{1,0},{2,3},{3,2},{4,5},{5,4},{6,7},{7,6},{8,9},{9,8},{10,11... | collective-permute-start | bytes 1572872 | tf_op jit(solution)/shard_map/ppermute | solution.py:550
  129.4 6.5 %collective-permute-start.24 = (bf16[256,768]{1,0:T(8,128)(2,1)}, bf16[256,768]{1,0:T(8,128)(2,1)S(1)}, u32[]{:S(2)}, u32[]{:S(2)}) collective-permute-start(bf16[256,768]{1,0:T(8,128)(2,1)} %get-tuple-element.156.refs_1_), channel_id=1, source_target_pairs={{0,1},{1,0},{2,3},{3,2},{4,5},{5,4},{6,7},{7,6},{8,9},{9,8},{10,11... | collective-permute-start | bytes 1179656 | tf_op jit(solution)/shard_map/ppermute | solution.py:550
  129.9 8.2 %collective-permute-start.25 = (bf16[256,768]{1,0:T(8,128)(2,1)}, bf16[256,768]{1,0:T(8,128)(2,1)S(1)}, u32[]{:S(2)}, u32[]{:S(2)}) collective-permute-start(bf16[256,768]{1,0:T(8,128)(2,1)} %get-tuple-element.157.refs_2_), channel_id=1, source_target_pairs={{0,1},{1,0},{2,3},{3,2},{4,5},{5,4},{6,7},{7,6},{8,9},{9,8},{10,11... | collective-permute-start | bytes 1179656 | tf_op jit(solution)/shard_map/ppermute | solution.py:550
  132.9 15.2 %collective-permute-start.23 = (bf16[2,64,2048]{2,1,0:T(8,128)(2,1)}, bf16[2,64,2048]{2,1,0:T(8,128)(2,1)}, u32[]{:S(2)}, u32[]{:S(2)}) collective-permute-start(bf16[2,64,2048]{2,1,0:T(8,128)(2,1)} %get-tuple-element.153), channel_id=1, source_target_pairs={{0,8},{2,10},{4,12},{6,14},{8,0},{10,2},{12,4},{14,6},{16,24},{18,... | collective-permute-start | bytes 1572872 | tf_op jit(solution)/shard_map/ppermute | solution.py:553
  134.4 16.0 %collective-permute-start.19 = (bf16[4,64,1024]{2,1,0:T(8,128)(2,1)}, bf16[4,64,1024]{2,1,0:T(8,128)(2,1)}, u32[]{:S(2)}, u32[]{:S(2)}) collective-permute-start(bf16[4,64,1024]{2,1,0:T(8,128)(2,1)} %get-tuple-element.149), channel_id=1, source_target_pairs={{0,4},{2,6},{4,0},{6,2},{8,12},{10,14},{12,8},{14,10},{16,20},{18,... | collective-permute-start | bytes 1572872 | tf_op jit(solution)/shard_map/ppermute | solution.py:553
  135.8 16.9 %collective-permute-start.20 = (bf16[4,64,1024]{2,1,0:T(8,128)(2,1)}, bf16[4,64,1024]{2,1,0:T(8,128)(2,1)}, u32[]{:S(2)}, u32[]{:S(2)}) collective-permute-start(bf16[4,64,1024]{2,1,0:T(8,128)(2,1)} %get-tuple-element.150), channel_id=1, source_target_pairs={{0,2},{2,0},{4,6},{6,4},{8,10},{10,8},{12,14},{14,12},{16,18},{18,... | collective-permute-start | bytes 1572872 | tf_op jit(solution)/shard_map/ppermute | solution.py:553
  145.8 31.5 %collective-permute-start.27 = (bf16[8,64,1024]{2,1,0:T(8,128)(2,1)}, bf16[8,64,1024]{2,1,0:T(8,128)(2,1)S(1)}, u32[]{:S(2)}, u32[]{:S(2)}) collective-permute-start(bf16[8,64,1024]{2,1,0:T(8,128)(2,1)} %get-tuple-element.165), channel_id=1, source_target_pairs={{0,2},{2,0},{4,6},{6,4},{8,10},{10,8},{12,14},{14,12},{16,18},{18,... | collective-permute-start | bytes 3145736 | tf_op jit(solution)/shard_map/ppermute | solution.py:553
  147.3 29.9 %collective-permute-start.28 = (bf16[8,64,1024]{2,1,0:T(8,128)(2,1)}, bf16[8,64,1024]{2,1,0:T(8,128)(2,1)}, u32[]{:S(2)}, u32[]{:S(2)}) collective-permute-start(bf16[8,64,1024]{2,1,0:T(8,128)(2,1)} %get-tuple-element.166), channel_id=1, source_target_pairs={{0,4},{2,6},{4,0},{6,2},{8,12},{10,14},{12,8},{14,10},{16,20},{18,... | collective-permute-start | bytes 3145736 | tf_op jit(solution)/shard_map/ppermute | solution.py:553
  148.1 37.6 %collective-permute-start.30 = (f32[8]{0:T(128)S(1)}, f32[8]{0:T(128)S(1)}, u32[]{:S(2)}, u32[]{:S(2)}) collective-permute-start(f32[8]{0:T(128)S(1)} %slice_bitcast_fusion.3), channel_id=1, source_target_pairs={{0,1},{1,0},{2,3},{3,2},{4,5},{5,4},{6,7},{7,6},{8,9},{9,8},{10,11... | collective-permute-start | bytes 104 | tf_op jit(solution)/shard_map/ppermute | solution.py:550
  150.3 17.3 %collective-permute-start.29 = (bf16[1,64,2048]{2,1,0:T(8,128)(2,1)}, bf16[1,64,2048]{2,1,0:T(8,128)(2,1)}, u32[]{:S(2)}, u32[]{:S(2)}) collective-permute-start(bf16[1,64,2048]{2,1,0:T(8,128)(2,1)} %get-tuple-element.168), channel_id=1, source_target_pairs={{0,16},{2,18},{4,20},{6,22},{8,24},{10,26},{12,28},{14,30},{16,0},... | collective-permute-start | bytes 786440 | tf_op jit(solution)/shard_map/ppermute | solution.py:553
  163.6 39.2 %all-to-all-start.2 = ((bf16[32,32,512]{2,1,0:T(8,128)(2,1)}), bf16[32,32,512]{2,1,0:T(8,128)(2,1)S(1)}, u32[]{:S(2)}, u32[]{:S(2)}) async-start(bf16[32,32,512]{2,1,0:T(8,128)(2,1)} %pad_maximum_fusion), calls=%async_computation.2 | async-start | bytes 2097152 | tf_op jit(solution)/shard_map/all_to_all | solution.py:578
  185.8 8.2 %collective-permute-start.31 = (bf16[10248]{0:T(1024)(128)(2,1)S(1)}, bf16[10248]{0:T(1024)(128)(2,1)S(1)}, u32[]{:S(2)}, u32[]{:S(2)}) collective-permute-start(bf16[10248]{0:T(1024)(128)(2,1)S(1)} %get-tuple-element.294), channel_id=1, source_target_pairs={{0,8},{2,10},{4,12},{6,14},{8,0},{10,2},{12,4},{14,6},{16,24},{18,... | collective-permute-start | bytes 61496 | tf_op jit(solution)/shard_map/ppermute | solution.py:553
  187.8 14.9 %collective-permute-start.34 = (bf16[4,64,1024]{2,1,0:T(8,128)(2,1)}, bf16[4,64,1024]{2,1,0:T(8,128)(2,1)S(1)}, u32[]{:S(2)}, u32[]{:S(2)}) collective-permute-start(bf16[4,64,1024]{2,1,0:T(8,128)(2,1)} %get-tuple-element.180), channel_id=1, source_target_pairs={{0,4},{2,6},{4,0},{6,2},{8,12},{10,14},{12,8},{14,10},{16,20},{18,... | collective-permute-start | bytes 1572872 | tf_op jit(solution)/shard_map/ppermute | solution.py:553
  187.9 14.8 %collective-permute-start.35 = (bf16[4,64,1024]{2,1,0:T(8,128)(2,1)}, bf16[4,64,1024]{2,1,0:T(8,128)(2,1)S(1)}, u32[]{:S(2)}, u32[]{:S(2)}) collective-permute-start(bf16[4,64,1024]{2,1,0:T(8,128)(2,1)} %get-tuple-element.181), channel_id=1, source_target_pairs={{0,2},{2,0},{4,6},{6,4},{8,10},{10,8},{12,14},{14,12},{16,18},{18,... | collective-permute-start | bytes 1572872 | tf_op jit(solution)/shard_map/ppermute | solution.py:553
  192.0 10.8 %collective-permute-start.33 = (bf16[2,64,2048]{2,1,0:T(8,128)(2,1)}, bf16[2,64,2048]{2,1,0:T(8,128)(2,1)}, u32[]{:S(2)}, u32[]{:S(2)}) collective-permute-start(bf16[2,64,2048]{2,1,0:T(8,128)(2,1)} %get-tuple-element.191), channel_id=1, source_target_pairs={{0,8},{2,10},{4,12},{6,14},{8,0},{10,2},{12,4},{14,6},{16,24},{18,... | collective-permute-start | bytes 1572872 | tf_op jit(solution)/shard_map/ppermute | solution.py:553
  194.2 4.5 %collective-permute-start.32 = (bf16[16392]{0:T(1024)(128)(2,1)S(1)}, bf16[16392]{0:T(1024)(128)(2,1)S(1)}, u32[]{:S(2)}, u32[]{:S(2)}) collective-permute-start(bf16[16392]{0:T(1024)(128)(2,1)S(1)} %pad_maximum_fusion.5), channel_id=1, source_target_pairs={{0,2},{2,0},{4,6},{6,4},{8,10},{10,8},{12,14},{14,12},{16,18},{18,... | collective-permute-start | bytes 98360 | tf_op jit(solution)/shard_map/ppermute | solution.py:553
  208.6 18.5 %collective-permute-start.39 = (bf16[1,64,2048]{2,1,0:T(8,128)(2,1)}, bf16[1,64,2048]{2,1,0:T(8,128)(2,1)}, u32[]{:S(2)}, u32[]{:S(2)}) collective-permute-start(bf16[1,64,2048]{2,1,0:T(8,128)(2,1)} %get-tuple-element.197), channel_id=1, source_target_pairs={{0,16},{2,18},{4,20},{6,22},{8,24},{10,26},{12,28},{14,30},{16,0},... | collective-permute-start | bytes 786440 | tf_op jit(solution)/shard_map/ppermute | solution.py:553
  209.7 17.3 %collective-permute-start.38 = (bf16[2,64,2048]{2,1,0:T(8,128)(2,1)}, bf16[2,64,2048]{2,1,0:T(8,128)(2,1)}, u32[]{:S(2)}, u32[]{:S(2)}) collective-permute-start(bf16[2,64,2048]{2,1,0:T(8,128)(2,1)} %get-tuple-element.195), channel_id=1, source_target_pairs={{0,8},{2,10},{4,12},{6,14},{8,0},{10,2},{12,4},{14,6},{16,24},{18,... | collective-permute-start | bytes 1572872 | tf_op jit(solution)/shard_map/ppermute | solution.py:553
  211.8 4.3 %collective-permute-start.36 = (bf16[28680]{0:T(1024)(128)(2,1)S(1)}, bf16[28680]{0:T(1024)(128)(2,1)S(1)}, u32[]{:S(2)}, u32[]{:S(2)}) collective-permute-start(bf16[28680]{0:T(1024)(128)(2,1)S(1)} %pad_maximum_fusion.4), channel_id=1, source_target_pairs={{0,4},{2,6},{4,0},{6,2},{8,12},{10,14},{12,8},{14,10},{16,20},{18,... | collective-permute-start | bytes 172088 | tf_op jit(solution)/shard_map/ppermute | solution.py:553
  214.6 14.6 %copy-start.23 = (f32[1,64,2048]{2,1,0:T(8,128)S(1)}, f32[1,64,2048]{2,1,0:T(8,128)}, u32[]{:S(2)}) copy-start(f32[1,64,2048]{2,1,0:T(8,128)} %get-tuple-element.204) | copy-start | bytes 1572868
  216.3 7.9 %collective-permute-start.37 = (bf16[53256]{0:T(1024)(128)(2,1)S(1)}, bf16[53256]{0:T(1024)(128)(2,1)S(1)}, u32[]{:S(2)}, u32[]{:S(2)}) collective-permute-start(bf16[53256]{0:T(1024)(128)(2,1)S(1)} %pad_maximum_fusion.3), channel_id=1, source_target_pairs={{0,16},{2,18},{4,20},{6,22},{8,24},{10,26},{12,28},{14,30},{16,0},... | collective-permute-start | bytes 319544 | tf_op jit(solution)/shard_map/ppermute | solution.py:553
  229.2 5.2 %collective-permute-start.40 = (bf16[16,6144]{1,0:T(8,128)(2,1)S(1)}, bf16[16,6144]{1,0:T(8,128)(2,1)S(1)}, u32[]{:S(2)}, u32[]{:S(2)}) collective-permute-start(bf16[16,6144]{1,0:T(8,128)(2,1)S(1)} %reshape.417), channel_id=1, source_target_pairs={{0,1},{1,0},{2,3},{3,2},{4,5},{5,4},{6,7},{7,6},{8,9},{9,8},{10,11... | collective-permute-start | bytes 589832 | tf_op jit(solution)/shard_map/ppermute | solution.py:550
  231.0 16.2 %collective-permute-start.41 = (bf16[1,64,2048]{2,1,0:T(8,128)(2,1)}, bf16[1,64,2048]{2,1,0:T(8,128)(2,1)S(1)}, u32[]{:S(2)}, u32[]{:S(2)}) collective-permute-start(bf16[1,64,2048]{2,1,0:T(8,128)(2,1)} %get-tuple-element.201), channel_id=1, source_target_pairs={{0,16},{2,18},{4,20},{6,22},{8,24},{10,26},{12,28},{14,30},{16,0},... | collective-permute-start | bytes 786440 | tf_op jit(solution)/shard_map/ppermute | solution.py:553
  (39 other events, 198.4 us)
